TPU v7x, 32 devices: a whole 2x2x4 slice. The times are simulated.
32 devices in a mesh: front: 4 (over y, core), panel: 8 (over z, x).
Axes of the slice: x: 2, y: 2, z: 4, core: 2. Of those that a mesh axis runs over, the one named last changes fastest.
Arguments:
- lower_panel: bfloat16 [4, 2, 4096, 4096], P('front', None, 'panel'), may hold values from -0.046875 to 0.046875
- inverse_cols: bfloat16 [4, 2, 4096, 512], P('front', None, 'panel'), may hold values from -0.1875 to 0.1875
- update_panel: bfloat16 [4, 2, 4096, 4096], P('front', None, 'panel'), may hold values from -0.046875 to 0.046875
- pivot_rhs: bfloat16 [4, 2, 128, 4096], P('front', None, None, 'panel'), may hold values from -6 to 6
- update_rhs: bfloat16 [4, 2, 128, 4096], P('front', None, None, 'panel'), may hold values from -6 to 6
- row_maps: int32 [4, 4096], replicated, may hold values from 0 to 8191, as said below
- parent_rhs: float32 [4, 2, 128, 4096], P('front', None, None, 'panel'), may hold values from -6 to 6
Outputs:
- solved: bfloat16 [4, 2, 128, 4096], P('front', None, None, 'panel')
- parent_out: float32 [4, 2, 128, 4096], P('front', None, None, 'panel')
Inputs may be any that keep to these rules, and one draw needn't show every extreme that they name: `row_maps`: each row lists 4096 distinct parent rows in increasing order; it always contains 0 and 8191.
All inputs are finite; a program needn't handle non-finite values.
Results may differ from a plain program's by a relative error of at most 0.019.
Values may be sent and summed in bfloat16 or wider, within the bound.
No kernel may reach another device: no remote copies, remote signals or barrier semaphores. Data moves between devices by JAX's collectives and lax.ppermute only.
A program may use at most 64 MiB of HBM per device.

v0:
```python
import jax
import jax.numpy as jnp
from jax import lax
from jax.sharding import PartitionSpec as P

CB = 512


def swapped(value, axis, stride):
    mask = 2**stride
    pairs = [(source, source ^ mask) for source in range(lax.axis_size(axis))]
    return lax.ppermute(value, axis, pairs)


def complex_product(matrix, vector, pattern):
    real_part = jnp.einsum(
        pattern, matrix[0], vector[0], preferred_element_type=jnp.float32
    ) - jnp.einsum(pattern, matrix[1], vector[1], preferred_element_type=jnp.float32)
    imag_part = jnp.einsum(
        pattern, matrix[0], vector[1], preferred_element_type=jnp.float32
    ) + jnp.einsum(pattern, matrix[1], vector[0], preferred_element_type=jnp.float32)
    return jnp.stack([real_part, imag_part])


def select_rows(block_rows, index_map, base, owned):
    targets = base + jnp.arange(owned, dtype=jnp.int32)
    placement = (index_map[:, None] == targets[None, :]).astype(jnp.bfloat16)
    return jnp.einsum("csu,ur->csr", block_rows, placement, preferred_element_type=jnp.float32)


def body(lower_panel, inverse_cols, update_panel, pivot_rhs, update_rhs, row_maps, parent_rhs):
    lower_f = lower_panel[0]
    inverse_f = inverse_cols[0]
    update_f = update_panel[0]
    pivot_f = pivot_rhs[0]
    upd_rhs_f = update_rhs[0]
    parent_f = parent_rhs[0]
    own_rows = lower_f.shape[1]
    panel_width = lower_f.shape[2]
    block_count = panel_width // CB
    panel_count = lax.axis_size("panel")
    panel_number = lax.axis_index("panel")
    front_number = lax.axis_index("front")
    owner_block = panel_number * own_rows // CB
    shots = pivot_f.shape[1]
    upd_rows = update_f.shape[1]
    partial_sum = jnp.zeros((2, shots, own_rows), jnp.float32)
    blocks = []
    for block in range(block_count):
        first = block * CB
        residual = (pivot_f.astype(jnp.float32) - partial_sum).astype(jnp.bfloat16)
        block_term = complex_product(inverse_f, residual, "ri,sr->si")
        block_term = jnp.where(owner_block == block, block_term, 0.0)
        block_value = lax.psum(block_term.astype(jnp.bfloat16), "panel")
        blocks.append(block_value)
        partial_sum = partial_sum + complex_product(
            lower_f[:, :, first : first + CB], block_value, "rc,sc->sr"
        )
    solution = jnp.concatenate(blocks, axis=2)
    own_solution = lax.dynamic_slice_in_dim(solution, panel_number * own_rows, own_rows, 2)
    applied = complex_product(update_f, solution, "rc,sc->sr")
    child_update = (upd_rhs_f.astype(jnp.float32) - applied).astype(jnp.bfloat16)
    parity = front_number % 2
    sibling_front = front_number + 1 - 2 * parity
    own_map = lax.dynamic_index_in_dim(row_maps, front_number, 0, keepdims=False)
    my_base = (parity * panel_count + panel_number) * upd_rows
    gathered = lax.all_gather(child_update, "panel", axis=2, tiled=True)
    sibling = swapped(gathered, "front", 0)
    sibling_map = lax.dynamic_index_in_dim(row_maps, sibling_front, 0, keepdims=False)
    assembled = select_rows(gathered, own_map, my_base, upd_rows) + select_rows(
        sibling, sibling_map, my_base, upd_rows
    )
    parent_out = parent_f + assembled
    return (own_solution[None], parent_out[None])


def solution(mesh):
    in_specs = (
        P("front", None, "panel", None),
        P("front", None, "panel", None),
        P("front", None, "panel", None),
        P("front", None, None, "panel"),
        P("front", None, None, "panel"),
        P(),
        P("front", None, None, "panel"),
    )
    out_specs = (P("front", None, None, "panel"), P("front", None, None, "panel"))
    return jax.shard_map(body, mesh=mesh, in_specs=in_specs, out_specs=out_specs, check_vma=False)
```

profile of v0, /device:TPU:0, one launch (start us, length us, event | category | flops | bytes accessed | tf_op | source)
XLA Modules:
  0.0 713.5 jit_solution(12262862138530588806)
XLA Ops:
  7.2 1.4 fusion.133
  8.7 1.3 fusion.135
  10.0 1.3 fusion.59
  11.4 1.4 fusion.60
  13.6 73.4 %all-reduce.9.cloned.1.call-done = bf16[2,128,512]{2,1,0:T(8,128)(2,1)} async-done(((bf16[2,128,512]{2,1,0:T(8,128)(2,1)}), bf16[2,128,512]{2,1,0:T(8,128)(2,1)}) %all-reduce.9.cloned.1.call-update) | async-done | bytes 262160 | tf_op jit(solution)/shard_map/psum | solution.py:54
  87.0 1.4 fusion.137
  88.4 1.4 fusion.138
  89.8 1.4 fusion.57
  91.2 1.4 fusion.58
  94.5 69.9 %all-reduce.11.cloned.1.call-done = bf16[2,128,512]{2,1,0:T(8,128)(2,1)} async-done(((bf16[2,128,512]{2,1,0:T(8,128)(2,1)}), bf16[2,128,512]{2,1,0:T(8,128)(2,1)}) %all-reduce.11.cloned.1.call-update) | async-done | bytes 262160 | tf_op jit(solution)/shard_map/psum | solution.py:54
  164.5 1.4 fusion.139
  165.9 1.4 fusion.140
  167.3 1.4 fusion.53
  168.7 1.4 fusion.54
  172.1 70.0 %all-reduce.13.cloned.1.call-done = bf16[2,128,512]{2,1,0:T(8,128)(2,1)} async-done(((bf16[2,128,512]{2,1,0:T(8,128)(2,1)}), bf16[2,128,512]{2,1,0:T(8,128)(2,1)}) %all-reduce.13.cloned.1.call-update) | async-done | bytes 262160 | tf_op jit(solution)/shard_map/psum | solution.py:54
  242.1 1.4 fusion.141
  243.5 1.4 fusion.142
  244.9 1.4 fusion.49
  246.3 1.4 fusion.50
  249.7 69.9 %all-reduce.15.cloned.1.call-done = bf16[2,128,512]{2,1,0:T(8,128)(2,1)} async-done(((bf16[2,128,512]{2,1,0:T(8,128)(2,1)}), bf16[2,128,512]{2,1,0:T(8,128)(2,1)}) %all-reduce.15.cloned.1.call-update) | async-done | bytes 262160 | tf_op jit(solution)/shard_map/psum | solution.py:54
  319.7 1.4 fusion.143
  321.1 1.4 fusion.144
  322.5 1.4 fusion.45
  323.9 1.4 fusion.46
  327.3 69.9 %all-reduce.17.cloned.1.call-done = bf16[2,128,512]{2,1,0:T(8,128)(2,1)} async-done(((bf16[2,128,512]{2,1,0:T(8,128)(2,1)}), bf16[2,128,512]{2,1,0:T(8,128)(2,1)}) %all-reduce.17.cloned.1.call-update) | async-done | bytes 262160 | tf_op jit(solution)/shard_map/psum | solution.py:54
  397.2 1.4 fusion.145
  398.7 1.4 fusion.146
  400.1 1.4 fusion.41
  401.5 1.4 fusion.42
  405.7 69.2 %all-reduce.19.cloned.1.call-done = bf16[2,128,512]{2,1,0:T(8,128)(2,1)} async-done(((bf16[2,128,512]{2,1,0:T(8,128)(2,1)}), bf16[2,128,512]{2,1,0:T(8,128)(2,1)}) %all-reduce.19.cloned.1.call-update) | async-done | bytes 262160 | tf_op jit(solution)/shard_map/psum | solution.py:54
  474.9 1.4 fusion.147
  476.3 1.4 fusion.148
  477.7 1.4 fusion.37
  479.1 1.4 fusion.38
  485.3 67.7 %all-reduce.21.cloned.1.call-done = bf16[2,128,512]{2,1,0:T(8,128)(2,1)} async-done(((bf16[2,128,512]{2,1,0:T(8,128)(2,1)}), bf16[2,128,512]{2,1,0:T(8,128)(2,1)}) %all-reduce.21.cloned.1.call-update) | async-done | bytes 262160 | tf_op jit(solution)/shard_map/psum | solution.py:54
  553.1 1.4 fusion.149
  554.5 1.4 fusion.150
  555.9 1.4 fusion.33
  557.4 1.4 fusion.34
  564.2 67.5 %all-reduce.23.cloned.1.call-done = bf16[2,128,512]{2,1,0:T(8,128)(2,1)} async-done(((bf16[2,128,512]{2,1,0:T(8,128)(2,1)}), bf16[2,128,512]{2,1,0:T(8,128)(2,1)}) %all-reduce.23.cloned.1.call-update) | async-done | bytes 262160 | tf_op jit(solution)/shard_map/psum | solution.py:54
  631.7 1.7 constant_dynamic-update-slice_fusion
  633.4 4.2 fusion.6
  637.6 4.2 fusion.8
  641.8 3.8 fusion.70
  645.6 1.5 fusion.64
  648.0 50.5 %all-gather.2.cloned.1.call-done = bf16[2,128,4096]{2,1,0:T(8,128)(2,1)} async-done(((bf16[2,128,512]{2,1,0:T(8,128)(2,1)}), bf16[2,128,4096]{2,1,0:T(8,128)(2,1)}) %all-gather.2.cloned.1.call-update) | async-done | bytes 2097168 | tf_op jit(solution)/shard_map/all_gather | solution.py:67
  699.3 3.3 fusion.2
  703.0 4.0 fusion.28
  (105 shorter events, 23.2 us)
Async XLA Ops:
  7.2 85.5 %copy-start.1 = (bf16[1,2,128,512]{3,2,1,0:T(8,128)(2,1)S(1)}, bf16[1,2,128,512]{3,2,1,0:T(8,128)(2,1)}, u32[]{:S(2)}) copy-start(bf16[1,2,128,512]{3,2,1,0:T(8,128)(2,1)} %param.10) | copy-start | bytes 786436
  7.2 85.6 %copy-start = (bf16[1,2,512,512]{3,2,1,0:T(8,128)(2,1)S(1)}, bf16[1,2,512,512]{3,2,1,0:T(8,128)(2,1)}, u32[]{:S(2)}) copy-start(bf16[1,2,512,512]{3,2,1,0:T(8,128)(2,1)} %param.8) | copy-start | bytes 3145732
  7.2 79.8 %all-reduce.9.cloned.1.call-start = ((), (), s32[]{:S(2)}) async-start(), calls=%async_computation | async-start | bytes 524288 | tf_op jit(solution)/shard_map/psum | solution.py:54
  13.5 150.9 %all-reduce.11.cloned.1.call-start = ((), (), s32[]{:S(2)}) async-start(), calls=%async_computation.1 | async-start | bytes 524288 | tf_op jit(solution)/shard_map/psum | solution.py:54
  94.5 147.6 %all-reduce.13.cloned.1.call-start = ((), (), s32[]{:S(2)}) async-start(), calls=%async_computation.2 | async-start | bytes 524288 | tf_op jit(solution)/shard_map/psum | solution.py:54
  172.0 147.6 %all-reduce.15.cloned.1.call-start = ((), (), s32[]{:S(2)}) async-start(), calls=%async_computation.3 | async-start | bytes 524288 | tf_op jit(solution)/shard_map/psum | solution.py:54
  249.7 147.6 %all-reduce.17.cloned.1.call-start = ((), (), s32[]{:S(2)}) async-start(), calls=%async_computation.4 | async-start | bytes 524288 | tf_op jit(solution)/shard_map/psum | solution.py:54
  325.5 79.4 %copy-start.3 = (bf16[2,128,512]{2,1,0:T(8,128)(2,1)S(1)}, bf16[2,128,512]{2,1,0:T(8,128)(2,1)}, u32[]{:S(2)}) copy-start(bf16[2,128,512]{2,1,0:T(8,128)(2,1)} %all-reduce.9.cloned.1.call-done) | copy-start | bytes 786436
  327.2 147.6 %all-reduce.19.cloned.1.call-start = ((), (), s32[]{:S(2)}) async-start(), calls=%async_computation.5 | async-start | bytes 524288 | tf_op jit(solution)/shard_map/psum | solution.py:54
  403.1 79.9 %copy-start.2 = (bf16[2,128,512]{2,1,0:T(8,128)(2,1)S(1)}, bf16[2,128,512]{2,1,0:T(8,128)(2,1)}, u32[]{:S(2)}) copy-start(bf16[2,128,512]{2,1,0:T(8,128)(2,1)} %all-reduce.11.cloned.1.call-done) | copy-start | bytes 786436
  403.2 80.7 %copy-start.4 = (bf16[2,128,512]{2,1,0:T(8,128)(2,1)S(1)}, bf16[2,128,512]{2,1,0:T(8,128)(2,1)}, u32[]{:S(2)}) copy-start(bf16[2,128,512]{2,1,0:T(8,128)(2,1)} %all-reduce.13.cloned.1.call-done) | copy-start | bytes 786436
  403.2 81.4 %copy-start.6 = (bf16[2,128,512]{2,1,0:T(8,128)(2,1)S(1)}, bf16[2,128,512]{2,1,0:T(8,128)(2,1)}, u32[]{:S(2)}) copy-start(bf16[2,128,512]{2,1,0:T(8,128)(2,1)} %all-reduce.15.cloned.1.call-done) | copy-start | bytes 786436
  404.9 148.2 %all-reduce.21.cloned.1.call-start = ((), (), s32[]{:S(2)}) async-start(), calls=%async_computation.6 | async-start | bytes 524288 | tf_op jit(solution)/shard_map/psum | solution.py:54
  480.6 0.7 copy-start.9
  481.5 80.4 %copy-start.5 = (bf16[2,128,512]{2,1,0:T(8,128)(2,1)S(1)}, bf16[2,128,512]{2,1,0:T(8,128)(2,1)}, u32[]{:S(2)}) copy-start(bf16[2,128,512]{2,1,0:T(8,128)(2,1)} %all-reduce.17.cloned.1.call-done) | copy-start | bytes 786436
  481.5 81.1 %copy-start.7 = (bf16[2,128,512]{2,1,0:T(8,128)(2,1)S(1)}, bf16[2,128,512]{2,1,0:T(8,128)(2,1)}, u32[]{:S(2)}) copy-start(bf16[2,128,512]{2,1,0:T(8,128)(2,1)} %all-reduce.19.cloned.1.call-done) | copy-start | bytes 786436
  483.0 148.7 %all-reduce.23.cloned.1.call-start = ((), (), s32[]{:S(2)}) async-start(), calls=%async_computation.7 | async-start | bytes 524288 | tf_op jit(solution)/shard_map/psum | solution.py:54
  553.1 10.4 %copy-start.8 = (bf16[2,128,512]{2,1,0:T(8,128)(2,1)S(1)}, bf16[2,128,512]{2,1,0:T(8,128)(2,1)}, u32[]{:S(2)}) copy-start(bf16[2,128,512]{2,1,0:T(8,128)(2,1)} %all-reduce.21.cloned.1.call-done) | copy-start | bytes 786436
  561.7 136.8 %all-gather.2.cloned.1.call-start = ((), (), s32[]{:S(2)}) async-start(), calls=%async_computation.8 | async-start | bytes 2359296 | tf_op jit(solution)/shard_map/all_gather | solution.py:67
  633.4 8.4 %copy-start.11 = (bf16[2,128,4096]{2,1,0:T(8,128)(2,1)S(1)}, bf16[2,128,4096]{2,1,0:T(8,128)(2,1)}, u32[]{:S(2)}) copy-start(bf16[2,128,4096]{2,1,0:T(8,128)(2,1)} %constant_dynamic-update-slice_fusion) | copy-start | bytes 6291460
  633.4 12.2 %slice-start = ((s8[8388608]{0:T(1024)(128)(4,1)}), s8[4194304]{0:T(1024)(128)(4,1)S(1)}, s32[]{:S(2)}) async-start(s8[8388608]{0:T(1024)(128)(4,1)} %bitcast.399), calls=%async_computation.9 | async-start | bytes 8388608
  637.6 8.0 %slice-start.1 = ((s8[8388608]{0:T(1024)(128)(4,1)}), s8[4194304]{0:T(1024)(128)(4,1)S(1)}, s32[]{:S(2)}) async-start(s8[8388608]{0:T(1024)(128)(4,1)} %bitcast.399), calls=%async_computation.10 | async-start | bytes 8388608
  641.8 5.4 copy-start.10
  641.8 56.7 %copy-start.12 = (s32[4,4096]{1,0:T(4,128)S(1)}, s32[4,4096]{1,0:T(4,128)}, u32[]{:S(2)}) copy-start(s32[4,4096]{1,0:T(4,128)} %param.12) | copy-start | bytes 196612
  698.5 4.5 collective-permute-start
Sparse Core Ops, SparseCore 0:
  13.6 73.2 all-reduce.8
  94.6 69.8 all-reduce.10
  172.2 69.8 all-reduce.12
  249.8 69.8 all-reduce.14
  327.4 69.8 all-reduce.16
  405.0 69.8 all-reduce.18
  483.1 69.8 all-reduce.20
  561.8 69.8 all-reduce.22
  648.1 50.3 all-gather.1
where the time goes:
time: 715 us; the launch traced here: 714 us
  waiting for transfers between devices  609 us (85%)
  matrix products  72.7 us (10%)
  between operations  14.5 us (2%)
  other arithmetic  8.8 us (1%)
  local copies, waits for them, and re-layouts  8.38 us (1%)
    psum x8, waiting for transfers between devices, body(): block_value = lax.psum(block_term.astype(jnp.bfloat16), 'panel')  558 us
    all_gather x1, waiting for transfers between devices, body(): gathered = lax.all_gather(child_update, 'panel', axis=2, tiled=True)  50.5 us
    dot_general x16, matrix products, complex_product(): jnp.einsum(pattern, matrix[1], vector[1], preferred_element_type=jnp.floa...  17.2 us
    dot_general x16, matrix products, complex_product(): jnp.einsum(pattern, matrix[1], vector[0], preferred_element_type=jnp.floa...  17.1 us
    dot_general x16, matrix products, complex_product(): jnp.einsum(pattern, matrix[0], vector[1], preferred_element_type=jnp.floa...  16.7 us
    dot_general x16, matrix products, complex_product(): jnp.einsum(pattern, matrix[0], vector[0], preferred_element_type=jnp.floa...  14.4 us
  transfers between devices with their start and end apart: 10, of which 10 were waited for; matrix products, arithmetic and copies ran while one was open for 1% of the time, Pallas kernels for 0%

commit v1 on v0

v1 whole, which is shorter than its diff:
```python
import functools

import jax
import jax.numpy as jnp
import numpy as np
from jax import lax
from jax.experimental import pallas as pl
from jax.experimental.pallas import tpu as pltpu
from jax.sharding import PartitionSpec as P

CB = 512
CHUNKS = 2
F32 = jnp.float32
BF16 = jnp.bfloat16

CHAIN = (
    (1, 0, 3, 2, 5, 4, 7, 6),
    (1, 2, 0, 5, 3, 4, 7, 6),
    (1, 0, 3, 2, 5, 4, 7, 6),
    (1, 0, 3, 4, 5, 2, 7, 6),
    (1, 0, 3, 2, 5, 4, 7, 6),
    (1, 0, 3, 2, 5, 6, 7, 4),
    (1, 0, 3, 2, 5, 4, 7, 6),
)
SPREAD = (
    (2, 0, 3, 1, 5, 4, 7, 6),
    (4, 3, 0, 1, 2, 6, 7, 5),
    (6, 5, 4, 0, 2, 1, 7, 3),
    (1, 7, 6, 5, 0, 2, 4, 3),
    (1, 2, 0, 7, 6, 3, 4, 5),
    (3, 0, 4, 1, 2, 7, 5, 6),
    (1, 2, 6, 7, 0, 3, 4, 5),
    (3, 0, 4, 7, 6, 1, 2, 5),
    (1, 2, 4, 5, 6, 7, 0, 3),
    (2, 0, 3, 5, 6, 4, 7, 1),
)
PAIRS = ((0,), (1, 0), (2, 1, 0), (3, 2, 1), (4, 3, 2), (5, 4, 3), (6, 5, 4), (7, 6, 5), (7, 6), (7,))
SWAP = (1, 0, 3, 2, 5, 4, 7, 6)


def pairs_of(dests):
    return [(source, dest) for source, dest in enumerate(dests)]


def spread_plan(count):
    have = [{p, p - 1} for p in range(count)]
    arrivals = []
    for hop, sources in enumerate(PAIRS):
        first = [-1] * count
        second = [-1] * count
        for source in sources:
            dest = SPREAD[hop][source]
            second[dest] = source
            if source != count - 1:
                first[dest] = source - 1
        for p in range(count):
            for block in (first[p], second[p]):
                if block >= 0:
                    assert block not in have[p]
                    have[p].add(block)
        arrivals.append((first, second))
    last = [-1] * count
    for p in range(count):
        block = count - 1 if p % 2 == 0 else count - 2
        if block not in have[p]:
            last[p] = block
            have[p].add(block)
    assert all(held >= set(range(count)) for held in have)
    return arrivals, last


def stacked(value):
    return jnp.concatenate([value[0], value[1]], axis=0)


def turned_of(value):
    half = value.shape[0] // 2
    return jnp.concatenate([-value[half:], value[:half]], axis=0)


def apply_rows(value, matrix_real, matrix_imag):
    dims = (((1,), (1,)), ((), ()))
    return lax.dot_general(value, matrix_real, dims, preferred_element_type=F32) + lax.dot_general(
        turned_of(value), matrix_imag, dims, preferred_element_type=F32
    )


def apply_columns(value, matrix_real, matrix_imag):
    return jnp.dot(value, matrix_real, preferred_element_type=F32) + jnp.dot(
        turned_of(value), matrix_imag, preferred_element_type=F32
    )


def weights_kernel(place_ref, lower_ref, inverse_ref, near_ref, inv_ref, sems):
    width = near_ref.shape[-1]
    block = jnp.maximum(place_ref[0] - 1, 0)
    columns = pl.ds(pl.multiple_of(block * width, width), width)
    copies = (
        pltpu.make_async_copy(lower_ref.at[0, :, :, columns], near_ref, sems.at[0]),
        pltpu.make_async_copy(inverse_ref.at[0], inv_ref, sems.at[1]),
    )
    for copy in copies:
        copy.start()
    for copy in copies:
        copy.wait()


def resident_weights(place, lower, inverse):
    rows = lower.shape[2]
    hbm = pl.BlockSpec(memory_space=pl.ANY)
    vmem = pl.BlockSpec(memory_space=pltpu.VMEM)
    return pl.pallas_call(
        weights_kernel,
        out_shape=(pltpu.VMEM((2, rows, CB), BF16), pltpu.VMEM((2, rows, CB), BF16)),
        in_specs=[pl.BlockSpec(memory_space=pltpu.SMEM), hbm, hbm],
        out_specs=(vmem, vmem),
        scratch_shapes=[pltpu.SemaphoreType.DMA((2,))],
        name="weights",
    )(place, lower, inverse)


def solve_kernel(hop, chunk, place_ref, rhs_ref, acc_ref, urgent_ref, near_ref, inv_ref, out_ref):
    shots = out_ref.shape[1]
    piece = slice(chunk * shots, (chunk + 1) * shots)

    @pl.when(place_ref[0] != hop)
    def _():
        out_ref[...] = jnp.zeros_like(out_ref)

    @pl.when(place_ref[0] == hop)
    def _():
        residual = stacked(rhs_ref[:, piece]).astype(F32)
        if hop > 0:
            residual = residual - stacked(acc_ref[:, piece])
            residual = residual - apply_rows(stacked(urgent_ref[...]), near_ref[0], near_ref[1])
        term = apply_columns(residual.astype(BF16), inv_ref[0], inv_ref[1]).astype(BF16)
        out_ref[0] = term[:shots]
        out_ref[1] = term[shots:]


def solve(hop, chunk, place, rhs, acc, urgent, near, inv):
    vmem = pl.BlockSpec(memory_space=pltpu.VMEM)
    return pl.pallas_call(
        functools.partial(solve_kernel, hop, chunk),
        out_shape=jax.ShapeDtypeStruct(urgent.shape, BF16),
        in_specs=[pl.BlockSpec(memory_space=pltpu.SMEM)] + [vmem] * 5,
        out_specs=vmem,
        compiler_params=pltpu.CompilerParams(vmem_limit_bytes=16 * 2**20),
        name=f"solve_{hop}_{chunk}",
    )(place, rhs, acc, urgent, near, inv)


def gather_kernel(left, table_ref, *refs):
    count = len(left)
    parts = refs[:count]
    lower_ref, update_ref, acc_l_in, acc_u_in, acc_l_ref, acc_u_ref, buf_l, buf_u, sems = refs[count:]
    width = buf_l.shape[-1]
    shots = acc_l_ref.shape[1]
    place = table_ref[0]

    def copy_of(i, panel_ref, buf, which):
        block = jnp.maximum(table_ref[1 + i], 0)
        columns = pl.ds(pl.multiple_of(block * width, width), width)
        return pltpu.make_async_copy(panel_ref.at[0, :, :, columns], buf.at[i], sems.at[i, which])

    def when_update(i):
        return table_ref[1 + i] >= 0

    def when_lower(i):
        return jnp.logical_and(table_ref[1 + i] >= 0, table_ref[1 + i] < place)

    for i in range(count):
        if left[i]:

            @pl.when(when_lower(i))
            def _(i=i):
                copy_of(i, lower_ref, buf_l, 0).start()

        @pl.when(when_update(i))
        def _(i=i):
            copy_of(i, update_ref, buf_u, 1).start()

    acc_l_ref[...] = acc_l_in[...]
    acc_u_ref[...] = acc_u_in[...]

    def add(i, copy, buf, acc_ref):
        copy.wait()
        product = apply_rows(stacked(parts[i][...]), buf[i, 0], buf[i, 1])
        acc_ref[0] += product[:shots]
        acc_ref[1] += product[shots:]

    for i in range(count):
        if left[i]:

            @pl.when(when_lower(i))
            def _(i=i):
                add(i, copy_of(i, lower_ref, buf_l, 0), buf_l, acc_l_ref)

        @pl.when(when_update(i))
        def _(i=i):
            add(i, copy_of(i, update_ref, buf_u, 1), buf_u, acc_u_ref)


def accumulate(name, table, parts, left, lower, update, acc_l, acc_u):
    count = len(parts)
    vmem = pl.BlockSpec(memory_space=pltpu.VMEM)
    hbm = pl.BlockSpec(memory_space=pl.ANY)
    rows = lower.shape[2]
    shape = jax.ShapeDtypeStruct(acc_l.shape, F32)
    return pl.pallas_call(
        functools.partial(gather_kernel, left),
        out_shape=(shape, shape),
        in_specs=[pl.BlockSpec(memory_space=pltpu.SMEM)] + [vmem] * count + [hbm, hbm, vmem, vmem],
        out_specs=(vmem, vmem),
        scratch_shapes=[
            pltpu.VMEM((count, 2, rows, CB), BF16),
            pltpu.VMEM((count, 2, rows, CB), BF16),
            pltpu.SemaphoreType.DMA((count, 2)),
        ],
        input_output_aliases={count + 3: 0, count + 4: 1},
        compiler_params=pltpu.CompilerParams(vmem_limit_bytes=24 * 2**20),
        name=name,
    )(table, *parts, lower, update, acc_l, acc_u)


def place_kernel(own_ref, other_ref, own_hot_ref, other_hot_ref, *out_refs):
    own = stacked(own_ref[...])
    other = stacked(other_ref[...])
    shots = own_ref.shape[1]
    for i, out_ref in enumerate(out_refs):
        rows = jnp.dot(own, own_hot_ref[i], preferred_element_type=F32) + jnp.dot(
            other, other_hot_ref[i], preferred_element_type=F32
        )
        rows = rows.astype(BF16)
        out_ref[0] = rows[:shots]
        out_ref[1] = rows[shots:]


def place_rows(own, other, own_hot, other_hot):
    vmem = pl.BlockSpec(memory_space=pltpu.VMEM)
    shape = jax.ShapeDtypeStruct(own.shape, BF16)
    count = own_hot.shape[0]
    return pl.pallas_call(
        place_kernel,
        out_shape=(shape,) * count,
        in_specs=[vmem] * 4,
        out_specs=(vmem,) * count,
        compiler_params=pltpu.CompilerParams(vmem_limit_bytes=24 * 2**20),
        name="place_rows",
    )(own, other, own_hot, other_hot)


def placements(row_maps, place, count, rows):
    own_map = lax.dynamic_index_in_dim(row_maps, lax.axis_index("front"), 0, keepdims=False)
    level = place // 2
    firsts = [place * rows, (count + place) * rows]
    for step in range(1, count // 2):
        far = level ^ step
        target = 2 * far + place % 2
        firsts.append(jnp.where(far < level, count + target, target) * rows)
    firsts = jnp.stack(firsts)
    targets = firsts[:, None] + jnp.arange(rows, dtype=jnp.int32)[None, :]

    def hot(device):
        mapped = lax.dynamic_slice_in_dim(own_map, device * rows, rows, 0)
        return (mapped[None, :, None] == targets[:, None, :]).astype(BF16)

    return hot(place), hot(place ^ 1)


def relay_body(lower_panel, inverse_cols, update_panel, pivot_rhs, update_rhs, row_maps, parent_rhs):
    pivot_f = pivot_rhs[0]
    shots, own_rows = pivot_f.shape[1:]
    upd_rows = update_panel.shape[2]
    count = lax.axis_size("panel")
    place = lax.axis_index("panel").astype(jnp.int32)
    level = place // 2
    arrivals, last = spread_plan(count)
    piece = shots // CHUNKS

    def send(value, dests):
        return lax.ppermute(value, "panel", pairs_of(dests))

    def table(*rows):
        columns = np.array([list(range(count)), *rows], np.int32)
        return lax.dynamic_index_in_dim(jnp.asarray(columns), place, 1, keepdims=False)

    def only(hop, block):
        return [block if p == hop else -1 for p in range(count)]

    place_ref = jnp.reshape(place, (1,))
    own_hot, other_hot = placements(row_maps, place, count, upd_rows)
    near, inv = resident_weights(place_ref, lower_panel, inverse_cols)
    acc_l = jnp.zeros((2, shots, own_rows), F32)
    acc_u = jnp.zeros((2, shots, upd_rows), F32)
    mine = jnp.zeros((2, shots, CB), BF16)
    before = mine
    urgent = [jnp.zeros((2, piece, CB), BF16)] * CHUNKS
    got = None
    for hop in range(count):
        fresh = [solve(hop, i, place_ref, pivot_f, acc_l, urgent[i], near, inv) for i in range(CHUNKS)]
        arrived = urgent
        if hop + 1 < count:
            urgent = [send(value, CHAIN[hop]) for value in fresh]
        here = place == hop
        before = jnp.where(here, jnp.concatenate(arrived, axis=1), before)
        mine = jnp.where(here, jnp.concatenate(fresh, axis=1), mine)
        if got is None:
            parts = [mine]
            blocks = [only(hop, hop)]
            left = (False,)
        else:
            parts = [before, mine, *got]
            blocks = [only(hop, hop - 1), only(hop, hop), *arrivals[hop - 1]]
            left = (False, False, True, True)
        spread = [send(before, SPREAD[hop]), send(mine, SPREAD[hop])]
        acc_l, acc_u = accumulate(
            f"accumulate_{hop}", table(*blocks), parts, left, lower_panel, update_panel, acc_l, acc_u
        )
        previous, got = got, spread
    late = [send(before, SPREAD[count]), send(mine, SPREAD[count])]
    latest = send(mine, SPREAD[count + 1])
    crossing = mine
    for p, value in ((0, late[1]), (1, latest), (2, got[1]), (3, late[1]), (4, previous[1]), (5, got[1])):
        crossing = jnp.where(place == p, value, crossing)
    crossed = send(crossing, SWAP)
    blocks = [*arrivals[count - 1], *arrivals[count], arrivals[count + 1][1]]
    acc_l, acc_u = accumulate(
        "accumulate_late", table(*blocks), [*got, *late, latest], (False,) * 5, lower_panel, update_panel, acc_l, acc_u
    )
    acc_l, acc_u = accumulate(
        "accumulate_last", table(last), [crossed], (False,), lower_panel, update_panel, acc_l, acc_u
    )
    child = (update_rhs[0].astype(F32) - acc_u).astype(BF16)
    other = send(child, SWAP)
    placed = place_rows(child, other, own_hot, other_hot)
    sums = [placed[0].astype(F32), placed[1].astype(F32)]
    for step in range(1, count // 2):
        came = send(placed[1 + step], [p ^ (2 * step) for p in range(count)]).astype(F32)
        below = (level ^ step) < level
        sums[0] = sums[0] + jnp.where(below, came, 0.0)
        sums[1] = sums[1] + jnp.where(below, 0.0, came)
    second = lax.axis_index("front") % 2 == 1
    kept = jnp.where(second, sums[1], sums[0])
    given = jnp.where(second, sums[0], sums[1]).astype(BF16)
    sibling = lax.ppermute(given, "front", [(f, f ^ 1) for f in range(lax.axis_size("front"))])
    parent_out = parent_rhs[0] + kept + sibling.astype(F32)
    return (mine[None], parent_out[None])


def select_rows(block_rows, index_map, base, owned):
    targets = base + jnp.arange(owned, dtype=jnp.int32)
    placement = (index_map[:, None] == targets[None, :]).astype(BF16)
    return jnp.einsum("csu,ur->csr", block_rows, placement, preferred_element_type=F32)


def extend_add(child_update, row_maps, parent_f):
    upd_rows = child_update.shape[2]
    panel_count = lax.axis_size("panel")
    panel_number = lax.axis_index("panel")
    front_number = lax.axis_index("front")
    parity = front_number % 2
    sibling_front = front_number + 1 - 2 * parity
    my_base = (parity * panel_count + panel_number) * upd_rows
    own_map = lax.dynamic_index_in_dim(row_maps, front_number, 0, keepdims=False)
    sibling_map = lax.dynamic_index_in_dim(row_maps, sibling_front, 0, keepdims=False)
    gathered = lax.all_gather(child_update, "panel", axis=2, tiled=True)
    pairs = [(source, source ^ 1) for source in range(lax.axis_size("front"))]
    sibling = lax.ppermute(gathered, "front", pairs)
    assembled = select_rows(gathered, own_map, my_base, upd_rows) + select_rows(
        sibling, sibling_map, my_base, upd_rows
    )
    return parent_f + assembled


def complex_product(matrix, vector, pattern):
    real_part = jnp.einsum(pattern, matrix[0], vector[0], preferred_element_type=F32) - jnp.einsum(
        pattern, matrix[1], vector[1], preferred_element_type=F32
    )
    imag_part = jnp.einsum(pattern, matrix[0], vector[1], preferred_element_type=F32) + jnp.einsum(
        pattern, matrix[1], vector[0], preferred_element_type=F32
    )
    return jnp.stack([real_part, imag_part])


def summed_body(lower_panel, inverse_cols, update_panel, pivot_rhs, update_rhs, row_maps, parent_rhs):
    lower_f = lower_panel[0]
    pivot_f = pivot_rhs[0]
    own_rows = lower_f.shape[1]
    block_count = lower_f.shape[2] // CB
    panel_number = lax.axis_index("panel")
    owner_block = panel_number * own_rows // CB
    partial_sum = jnp.zeros((2, pivot_f.shape[1], own_rows), F32)
    blocks = []
    for block in range(block_count):
        first = block * CB
        residual = (pivot_f.astype(F32) - partial_sum).astype(BF16)
        block_term = complex_product(inverse_cols[0], residual, "ri,sr->si")
        block_term = jnp.where(owner_block == block, block_term, 0.0)
        block_value = lax.psum(block_term.astype(BF16), "panel")
        blocks.append(block_value)
        partial_sum = partial_sum + complex_product(lower_f[:, :, first : first + CB], block_value, "rc,sc->sr")
    solution_f = jnp.concatenate(blocks, axis=2)
    own_solution = lax.dynamic_slice_in_dim(solution_f, panel_number * own_rows, own_rows, 2)
    applied = complex_product(update_panel[0], solution_f, "rc,sc->sr")
    child_update = (update_rhs[0].astype(F32) - applied).astype(BF16)
    parent_out = extend_add(child_update, row_maps, parent_rhs[0])
    return (own_solution[None], parent_out[None])


def solution(mesh):
    in_specs = (
        P("front", None, "panel", None),
        P("front", None, "panel", None),
        P("front", None, "panel", None),
        P("front", None, None, "panel"),
        P("front", None, None, "panel"),
        P(),
        P("front", None, None, "panel"),
    )
    out_specs = (P("front", None, None, "panel"), P("front", None, None, "panel"))

    def run(lower_panel, *others):
        blocks = lower_panel.shape[3] // CB
        one_block = mesh.shape["panel"] == blocks == len(SWAP)
        body = relay_body if one_block else summed_body
        call = jax.shard_map(body, mesh=mesh, in_specs=in_specs, out_specs=out_specs, check_vma=False)
        return call(lower_panel, *others)

    return run
```

time: 715 us -> 238 us (0.33)
  waiting for transfers between devices: 609 us -> 55 us
  starting transfers between devices: 0.56 us -> 88.3 us
  matrix products: 72.7 us -> 0 us
  local copies, waits for them, and re-layouts: 8.38 us -> 41.1 us
  Pallas kernels: 0 us -> 24.5 us
  other arithmetic: 8.8 us -> 25.6 us
  between operations: 14.5 us -> 1.55 us
    psum x8 -> x0, waiting for transfers between devices: 558 us -> none  [body(): block_value = lax.psum(block_term.astype(jnp.bfloat16), 'panel')]
    ppermute x1 -> x39, starting transfers between devices: 0.01 us -> 88.3 us  [the longest x38 88.2 us: send(): return lax.ppermute(value, 'panel', pairs_of(dests))]
    dot_general x66 -> x0, matrix products: 72.7 us -> none  [the longest x16 17.2 us: complex_product(): jnp.einsum(pattern, matrix[1], vector[1], preferred_element_type=jnp.floa...]
    ppermute x1 -> x39, waiting for transfers between devices: 0.46 us -> 55 us  [the longest x38 55 us: send(): return lax.ppermute(value, 'panel', pairs_of(dests))]
    all_gather x1 -> x0, waiting for transfers between devices: 50.5 us -> none  [body(): gathered = lax.all_gather(child_update, 'panel', axis=2, tiled=True)]
    unnamed x37 -> x104, local copies, waits for them, and re-layouts: 5.9 us -> 31.4 us
    pallas_call x0 -> x28, Pallas kernels: none -> 24.5 us  [the longest x10 17.8 us: accumulate(): pl.pallas_call(functools.partial(gather_kernel, left), out_shape=(shape,...]
    select_n x0 -> x14, other arithmetic: none -> 20.4 us  [the longest x9 13.3 us: relay_body(): mine = jnp.where(here, jnp.concatenate(fresh, axis=1), mine)]
  transfers between devices with their start and end apart: 10 -> 39, of which waited for: 10 -> 8; matrix products, arithmetic and copies ran while one was open for 1% -> 13% of each run, Pallas kernels for 0% -> 8%
where the time goes in v1:
time: 238 us; the launch traced here: 236 us
  starting transfers between devices  88.3 us (37%)
  waiting for transfers between devices  55 us (23%)
  local copies, waits for them, and re-layouts  41.1 us (17%)
  other arithmetic  25.6 us (11%)
  Pallas kernels  24.5 us (10%)
    ppermute x38, starting transfers between devices, send(): return lax.ppermute(value, 'panel', pairs_of(dests))  88.2 us
    ppermute x38, waiting for transfers between devices, send(): return lax.ppermute(value, 'panel', pairs_of(dests))  55 us
    unnamed x104, local copies, waits for them, and re-layouts  31.4 us
    pallas_call x10, Pallas kernels, accumulate(): pl.pallas_call(functools.partial(gather_kernel, left), out_shape=(shape,...  17.8 us
    select_n x9, other arithmetic, relay_body(): mine = jnp.where(here, jnp.concatenate(fresh, axis=1), mine)  13.3 us
    squeeze x10, local copies, waits for them, and re-layouts, table(): lax.dynamic_index_in_dim(jnp.asarray(columns), place, 1, keepdims=False)  6.92 us
    select_n x4, other arithmetic, relay_body(): before = jnp.where(here, jnp.concatenate(arrived, axis=1), before)  6.38 us
  transfers between devices with their start and end apart: 39, of which 8 were waited for; matrix products, arithmetic and copies ran while one was open for 13% of the time, Pallas kernels for 8%

profile of v1, /device:TPU:0, one launch (start us, length us, event | category | flops | bytes accessed | tf_op | source)
XLA Modules:
  0.0 236.1 jit_solution(14525212366146593558)
XLA Ops:
  2.7 2.7 %collective-permute-start.2 = (bf16[2,64,512]{2,1,0:T(8,128)(2,1)S(1)}, bf16[2,64,512]{2,1,0:T(8,128)(2,1)}, u32[]{:S(2)}, u32[]{:S(2)}) collective-permute-start(bf16[2,64,512]{2,1,0:T(8,128)(2,1)S(1)} %solve_0_1.1), channel_id=1, source_target_pairs={{0,1},{1,0},{2,3},{3,2},{4,5},{5,4},{6,7},{7,6},{8,9},{9,8},{10,11... | collective-permute-start | bytes 393224 | tf_op jit(solution)/shard_map/ppermute | solution.py:282
  7.1 1.8 collective-permute-start.4
  8.9 1.7 maximum_select_fusion.refs_0_
  14.9 3.4 %copy-done = bf16[1,2,512,4096]{3,2,1,0:T(8,128)(2,1)S(1)} copy-done((bf16[1,2,512,4096]{3,2,1,0:T(8,128)(2,1)S(1)}, bf16[1,2,512,4096]{3,2,1,0:T(8,128)(2,1)}, u32[]{:S(2)}) %copy-start) | copy-done | bytes 8388632
  18.2 3.4 %copy-done.4 = bf16[1,2,512,4096]{3,2,1,0:T(8,128)(2,1)S(1)} copy-done((bf16[1,2,512,4096]{3,2,1,0:T(8,128)(2,1)S(1)}, bf16[1,2,512,4096]{3,2,1,0:T(8,128)(2,1)}, u32[]{:S(2)}) %copy-start.4) | copy-done | bytes 8388632
  21.6 1.7 accumulate_0.1
  26.6 1.7 collective-permute-start.1
  28.3 1.7 maximum_select_fusion.2.refs_0_
  31.6 1.7 maximum_select_fusion.3.refs_1_
  33.6 3.4 %copy-done.5 = bf16[1,2,512,4096]{3,2,1,0:T(8,128)(2,1)S(1)} copy-done((bf16[1,2,512,4096]{3,2,1,0:T(8,128)(2,1)S(1)}, bf16[1,2,512,4096]{3,2,1,0:T(8,128)(2,1)}, u32[]{:S(2)}) %copy-start.5) | copy-done | bytes 8388632
  38.5 2.7 %collective-permute-start.10 = (bf16[2,64,512]{2,1,0:T(8,128)(2,1)S(1)}, bf16[2,64,512]{2,1,0:T(8,128)(2,1)S(1)}, u32[]{:S(2)}, u32[]{:S(2)}) collective-permute-start(bf16[2,64,512]{2,1,0:T(8,128)(2,1)S(1)} %solve_2_1.1), channel_id=1, source_target_pairs={{0,1},{1,0},{2,3},{3,2},{4,5},{5,4},{6,7},{7,6},{8,9},{9,8},{10,11... | collective-permute-start | bytes 393224 | tf_op jit(solution)/shard_map/ppermute | solution.py:282
  41.3 1.7 maximum_select_fusion.4.refs_1_
  43.1 5.7 %collective-permute-start.13 = (bf16[2,128,512]{2,1,0:T(8,128)(2,1)}, bf16[2,128,512]{2,1,0:T(8,128)(2,1)}, u32[]{:S(2)}, u32[]{:S(2)}) collective-permute-start(bf16[2,128,512]{2,1,0:T(8,128)(2,1)} %maximum_select_fusion.4.refs_1_), channel_id=1, source_target_pairs={{0,6},{1,5},{2,4},{3,0},{4,2},{5,1},{6,7},{7,3},{8,14},{9,13},{10,... | collective-permute-start | bytes 786440 | tf_op jit(solution)/shard_map/ppermute | solution.py:282
  48.8 1.9 maximum_select_fusion.6
  50.7 3.2 %collective-permute-start.12 = (bf16[2,128,512]{2,1,0:T(8,128)(2,1)}, bf16[2,128,512]{2,1,0:T(8,128)(2,1)}, u32[]{:S(2)}, u32[]{:S(2)}) collective-permute-start(bf16[2,128,512]{2,1,0:T(8,128)(2,1)} %get-tuple-element.59.refs_0_), channel_id=1, source_target_pairs={{0,6},{1,5},{2,4},{3,0},{4,2},{5,1},{6,7},{7,3},{8,14},{9,13},{10,... | collective-permute-start | bytes 786440 | tf_op jit(solution)/shard_map/ppermute | solution.py:282
  54.6 3.4 %copy-done.1 = bf16[1,2,512,4096]{3,2,1,0:T(8,128)(2,1)S(1)} copy-done((bf16[1,2,512,4096]{3,2,1,0:T(8,128)(2,1)S(1)}, bf16[1,2,512,4096]{3,2,1,0:T(8,128)(2,1)}, u32[]{:S(2)}) %copy-start.1) | copy-done | bytes 8388632
  58.0 3.4 %copy-done.6 = bf16[1,2,512,4096]{3,2,1,0:T(8,128)(2,1)S(1)} copy-done((bf16[1,2,512,4096]{3,2,1,0:T(8,128)(2,1)S(1)}, bf16[1,2,512,4096]{3,2,1,0:T(8,128)(2,1)}, u32[]{:S(2)}) %copy-start.6) | copy-done | bytes 8388632
  65.9 1.7 maximum_select_fusion.7.refs_1_
  67.6 1.9 collective-permute-start.15
  69.5 1.7 accumulate_3.1
  71.3 11.9 %collective-permute-start.18 = (bf16[2,64,512]{2,1,0:T(8,128)(2,1)S(1)}, bf16[2,64,512]{2,1,0:T(8,128)(2,1)S(1)}, u32[]{:S(2)}, u32[]{:S(2)}) collective-permute-start(bf16[2,64,512]{2,1,0:T(8,128)(2,1)S(1)} %solve_4_1.1), channel_id=1, source_target_pairs={{0,1},{1,0},{2,3},{3,2},{4,5},{5,4},{6,7},{7,6},{8,9},{9,8},{10,11... | collective-permute-start | bytes 393224 | tf_op jit(solution)/shard_map/ppermute | solution.py:282
  83.3 1.7 maximum_select_fusion.8.refs_1_
  85.1 2.0 collective-permute-start.21
  88.3 1.9 maximum_select_fusion.10
  90.2 2.1 collective-permute-start.20
  93.0 3.4 %copy-done.2 = bf16[1,2,512,4096]{3,2,1,0:T(8,128)(2,1)S(1)} copy-done((bf16[1,2,512,4096]{3,2,1,0:T(8,128)(2,1)S(1)}, bf16[1,2,512,4096]{3,2,1,0:T(8,128)(2,1)}, u32[]{:S(2)}) %copy-start.2) | copy-done | bytes 8388632
  96.4 3.4 %copy-done.7 = bf16[1,2,512,4096]{3,2,1,0:T(8,128)(2,1)S(1)} copy-done((bf16[1,2,512,4096]{3,2,1,0:T(8,128)(2,1)S(1)}, bf16[1,2,512,4096]{3,2,1,0:T(8,128)(2,1)}, u32[]{:S(2)}) %copy-start.7) | copy-done | bytes 8388632
  101.4 18.8 %collective-permute-start.19 = (bf16[2,64,512]{2,1,0:T(8,128)(2,1)S(1)}, bf16[2,64,512]{2,1,0:T(8,128)(2,1)S(1)}, u32[]{:S(2)}, u32[]{:S(2)}) collective-permute-start(bf16[2,64,512]{2,1,0:T(8,128)(2,1)S(1)} %solve_5_1.1), channel_id=1, source_target_pairs={{0,1},{1,0},{2,3},{3,2},{4,5},{5,6},{6,7},{7,4},{8,9},{9,8},{10,11... | collective-permute-start | bytes 393224 | tf_op jit(solution)/shard_map/ppermute | solution.py:282
  122.1 2.7 %collective-permute-start.23 = (bf16[2,128,512]{2,1,0:T(8,128)(2,1)S(1)}, bf16[2,128,512]{2,1,0:T(8,128)(2,1)S(1)}, u32[]{:S(2)}, u32[]{:S(2)}) collective-permute-start(bf16[2,128,512]{2,1,0:T(8,128)(2,1)S(1)} %maximum_select_fusion.11.refs_1_), channel_id=1, source_target_pairs={{0,3},{1,0},{2,4},{3,1},{4,2},{5,7},{6,5},{7,6},{8,11},{9,8},{10,1... | collective-permute-start | bytes 786440 | tf_op jit(solution)/shard_map/ppermute | solution.py:282
  124.8 2.6 %accumulate_5.1 = (f32[2,128,512]{2,1,0:T(8,128)S(1)}, f32[2,128,512]{2,1,0:T(8,128)S(1)}) custom-call(s32[5]{0:T(128)S(1)} %fusion.15.table_ref, bf16[2,128,512]{2,1,0:T(8,128)(2,1)S(1)} %copy-done.10, bf16[2,128,512]{2,1,0:T(8,128)(2,1)S(1)} %maximum_select_fusion.11.refs_1_, ...), custom_call_target="tpu_custom_call", output_to_operand_aliasing={{0}: (7, {}), {1}: (8, {})} | custom-call | tf_op jit(solution)/shard_map/accumulate_5/pallas_call | solution.py:210
  127.6 2.1 collective-permute-start.24
  130.5 10.9 %collective-permute-done.25.urgent_ref = bf16[2,64,512]{2,1,0:T(8,128)(2,1)S(1)} collective-permute-done((bf16[2,64,512]{2,1,0:T(8,128)(2,1)S(1)}, bf16[2,64,512]{2,1,0:T(8,128)(2,1)S(1)}, u32[]{:S(2)}, u32[]{:S(2)}) %collective-permute-start.25) | collective-permute-done | bytes 131104 | tf_op jit(solution)/shard_map/ppermute | solution.py:282
  141.3 1.9 collective-permute-done.24.urgent_ref
  147.3 1.6 collective-permute-start.28
  148.9 4.1 %collective-permute-start.29 = (bf16[2,128,512]{2,1,0:T(8,128)(2,1)S(1)}, bf16[2,128,512]{2,1,0:T(8,128)(2,1)S(1)}, u32[]{:S(2)}, u32[]{:S(2)}) collective-permute-start(bf16[2,128,512]{2,1,0:T(8,128)(2,1)S(1)} %maximum_select_fusion.21.refs_1_), channel_id=1, source_target_pairs={{0,2},{1,0},{2,3},{3,5},{4,6},{5,4},{6,7},{7,1},{8,10},{9,8},{10,1... | collective-permute-start | bytes 786440 | tf_op jit(solution)/shard_map/ppermute | solution.py:282
  158.0 6.7 %collective-permute-done.28.refs_3_ = bf16[2,128,512]{2,1,0:T(8,128)(2,1)S(1)} collective-permute-done((bf16[2,128,512]{2,1,0:T(8,128)(2,1)S(1)}, bf16[2,128,512]{2,1,0:T(8,128)(2,1)S(1)}, u32[]{:S(2)}, u32[]{:S(2)}) %collective-permute-start.28) | collective-permute-done | bytes 262176 | tf_op jit(solution)/shard_map/ppermute | solution.py:282
  165.4 7.4 %collective-permute-start.30 = (bf16[2,128,512]{2,1,0:T(8,128)(2,1)}, bf16[2,128,512]{2,1,0:T(8,128)(2,1)S(1)}, u32[]{:S(2)}, u32[]{:S(2)}) collective-permute-start(bf16[2,128,512]{2,1,0:T(8,128)(2,1)} %select_select_fusion), channel_id=1, source_target_pairs={{0,1},{1,0},{2,3},{3,2},{4,5},{5,4},{6,7},{7,6},{8,9},{9,8},{10,11... | collective-permute-start | bytes 786440 | tf_op jit(solution)/shard_map/ppermute | solution.py:282
  174.7 6.2 %collective-permute-done.33.refs_2_ = bf16[2,128,512]{2,1,0:T(8,128)(2,1)S(1)} collective-permute-done((bf16[2,128,512]{2,1,0:T(8,128)(2,1)}, bf16[2,128,512]{2,1,0:T(8,128)(2,1)S(1)}, u32[]{:S(2)}, u32[]{:S(2)}) %collective-permute-start.33) | collective-permute-done | bytes 262176 | tf_op jit(solution)/shard_map/ppermute | solution.py:282
  180.9 3.4 %copy-done.3 = bf16[1,2,512,4096]{3,2,1,0:T(8,128)(2,1)S(1)} copy-done((bf16[1,2,512,4096]{3,2,1,0:T(8,128)(2,1)S(1)}, bf16[1,2,512,4096]{3,2,1,0:T(8,128)(2,1)}, u32[]{:S(2)}) %copy-start.3) | copy-done | bytes 8388632
  184.3 3.4 %copy-done.8 = bf16[1,2,512,4096]{3,2,1,0:T(8,128)(2,1)S(1)} copy-done((bf16[1,2,512,4096]{3,2,1,0:T(8,128)(2,1)S(1)}, bf16[1,2,512,4096]{3,2,1,0:T(8,128)(2,1)}, u32[]{:S(2)}) %copy-start.8) | copy-done | bytes 8388632
  187.7 2.5 %accumulate_7.1 = (f32[2,128,512]{2,1,0:T(8,128)S(1)}, f32[2,128,512]{2,1,0:T(8,128)S(1)}) custom-call(s32[5]{0:T(128)S(1)} %fusion.18.table_ref, bf16[2,128,512]{2,1,0:T(8,128)(2,1)S(1)} %copy-done.39, bf16[2,128,512]{2,1,0:T(8,128)(2,1)S(1)} %maximum_select_fusion.21.refs_1_, ...), custom_call_target="tpu_custom_call", output_to_operand_aliasing={{0}: (7, {}), {1}: (8, {})} | custom-call | tf_op jit(solution)/shard_map/accumulate_7/pallas_call | solution.py:210
  190.2 2.1 accumulate_late.1
  194.8 7.3 %collective-permute-done.34.other_ref = bf16[2,128,512]{2,1,0:T(8,128)(2,1)S(1)} collective-permute-done((bf16[2,128,512]{2,1,0:T(8,128)(2,1)S(1)}, bf16[2,128,512]{2,1,0:T(8,128)(2,1)S(1)}, u32[]{:S(2)}, u32[]{:S(2)}) %collective-permute-start.34) | collective-permute-done | bytes 262176 | tf_op jit(solution)/shard_map/ppermute | solution.py:282
  203.7 5.2 %collective-permute-start.37 = (bf16[2,128,512]{2,1,0:T(8,128)(2,1)S(1)}, bf16[2,128,512]{2,1,0:T(8,128)(2,1)S(1)}, u32[]{:S(2)}, u32[]{:S(2)}) collective-permute-start(bf16[2,128,512]{2,1,0:T(8,128)(2,1)S(1)} %get-tuple-element.52), channel_id=1, source_target_pairs={{0,6},{1,7},{2,4},{3,5},{4,2},{5,3},{6,0},{7,1},{8,14},{9,15},{10,... | collective-permute-start | bytes 786440 | tf_op jit(solution)/shard_map/ppermute | solution.py:282
  209.6 6.7 %collective-permute-done.37 = bf16[2,128,512]{2,1,0:T(8,128)(2,1)S(1)} collective-permute-done((bf16[2,128,512]{2,1,0:T(8,128)(2,1)S(1)}, bf16[2,128,512]{2,1,0:T(8,128)(2,1)S(1)}, u32[]{:S(2)}, u32[]{:S(2)}) %collective-permute-start.37) | collective-permute-done | bytes 262176 | tf_op jit(solution)/shard_map/ppermute | solution.py:282
  216.3 14.1 %collective-permute-done.36 = bf16[2,128,512]{2,1,0:T(8,128)(2,1)} collective-permute-done((bf16[2,128,512]{2,1,0:T(8,128)(2,1)S(1)}, bf16[2,128,512]{2,1,0:T(8,128)(2,1)}, u32[]{:S(2)}, u32[]{:S(2)}) %collective-permute-start.36) | collective-permute-done | bytes 262176 | tf_op jit(solution)/shard_map/ppermute | solution.py:282
  232.0 1.9 maximum_select_fusion.13
  233.9 2.2 fusion.8
  (197 shorter events, 44.1 us)
Async XLA Ops:
  2.7 21.4 %collective-permute-start.2 = (bf16[2,64,512]{2,1,0:T(8,128)(2,1)S(1)}, bf16[2,64,512]{2,1,0:T(8,128)(2,1)}, u32[]{:S(2)}, u32[]{:S(2)}) collective-permute-start(bf16[2,64,512]{2,1,0:T(8,128)(2,1)S(1)} %solve_0_1.1), channel_id=1, source_target_pairs={{0,1},{1,0},{2,3},{3,2},{4,5},{5,4},{6,7},{7,6},{8,9},{9,8},{10,11... | collective-permute-start | bytes 393224 | tf_op jit(solution)/shard_map/ppermute | solution.py:282
  6.4 19.3 %collective-permute-start = (bf16[2,64,512]{2,1,0:T(8,128)(2,1)}, bf16[2,64,512]{2,1,0:T(8,128)(2,1)}, u32[]{:S(2)}, u32[]{:S(2)}) collective-permute-start(bf16[2,64,512]{2,1,0:T(8,128)(2,1)} %solve_0_0.1), channel_id=1, source_target_pairs={{0,1},{1,0},{2,3},{3,2},{4,5},{5,4},{6,7},{7,6},{8,9},{9,8},{10,11... | collective-permute-start | bytes 393224 | tf_op jit(solution)/shard_map/ppermute | solution.py:282
  7.1 26.3 %collective-permute-start.4 = (bf16[2,128,512]{2,1,0:T(8,128)(2,1)}, bf16[2,128,512]{2,1,0:T(8,128)(2,1)}, u32[]{:S(2)}, u32[]{:S(2)}) collective-permute-start(bf16[2,128,512]{2,1,0:T(8,128)(2,1)} %broadcast.85), channel_id=1, source_target_pairs={{0,2},{1,0},{2,3},{3,1},{4,5},{5,4},{6,7},{7,6},{8,10},{9,8},{10,1... | collective-permute-start | bytes 786440 | tf_op jit(solution)/shard_map/ppermute | solution.py:282
  10.5 23.0 %collective-permute-start.5 = (bf16[2,128,512]{2,1,0:T(8,128)(2,1)}, bf16[2,128,512]{2,1,0:T(8,128)(2,1)}, u32[]{:S(2)}, u32[]{:S(2)}) collective-permute-start(bf16[2,128,512]{2,1,0:T(8,128)(2,1)} %maximum_select_fusion.refs_0_), channel_id=1, source_target_pairs={{0,2},{1,0},{2,3},{3,1},{4,5},{5,4},{6,7},{7,6},{8,10},{9,8},{10,1... | collective-permute-start | bytes 786440 | tf_op jit(solution)/shard_map/ppermute | solution.py:282
  25.0 13.5 %collective-permute-start.3 = (bf16[2,64,512]{2,1,0:T(8,128)(2,1)S(1)}, bf16[2,64,512]{2,1,0:T(8,128)(2,1)S(1)}, u32[]{:S(2)}, u32[]{:S(2)}) collective-permute-start(bf16[2,64,512]{2,1,0:T(8,128)(2,1)S(1)} %solve_1_1.1), channel_id=1, source_target_pairs={{0,1},{1,2},{2,0},{3,5},{4,3},{5,4},{6,7},{7,6},{8,9},{9,10},{10,8... | collective-permute-start | bytes 393224 | tf_op jit(solution)/shard_map/ppermute | solution.py:282
  26.6 14.6 %collective-permute-start.1 = (bf16[2,64,512]{2,1,0:T(8,128)(2,1)S(1)}, bf16[2,64,512]{2,1,0:T(8,128)(2,1)S(1)}, u32[]{:S(2)}, u32[]{:S(2)}) collective-permute-start(bf16[2,64,512]{2,1,0:T(8,128)(2,1)S(1)} %solve_1_0.1), channel_id=1, source_target_pairs={{0,1},{1,2},{2,0},{3,5},{4,3},{5,4},{6,7},{7,6},{8,9},{9,10},{10,8... | collective-permute-start | bytes 393224 | tf_op jit(solution)/shard_map/ppermute | solution.py:282
  30.1 24.5 %collective-permute-start.6 = (bf16[2,128,512]{2,1,0:T(8,128)(2,1)}, bf16[2,128,512]{2,1,0:T(8,128)(2,1)}, u32[]{:S(2)}, u32[]{:S(2)}) collective-permute-start(bf16[2,128,512]{2,1,0:T(8,128)(2,1)} %maximum_select_fusion.2.refs_0_), channel_id=1, source_target_pairs={{0,4},{1,3},{2,0},{3,1},{4,2},{5,6},{6,7},{7,5},{8,12},{9,11},{10,... | collective-permute-start | bytes 786440 | tf_op jit(solution)/shard_map/ppermute | solution.py:282
  33.3 21.2 %collective-permute-start.7 = (bf16[2,128,512]{2,1,0:T(8,128)(2,1)}, bf16[2,128,512]{2,1,0:T(8,128)(2,1)}, u32[]{:S(2)}, u32[]{:S(2)}) collective-permute-start(bf16[2,128,512]{2,1,0:T(8,128)(2,1)} %maximum_select_fusion.3.refs_1_), channel_id=1, source_target_pairs={{0,4},{1,3},{2,0},{3,1},{4,2},{5,6},{6,7},{7,5},{8,12},{9,11},{10,... | collective-permute-start | bytes 786440 | tf_op jit(solution)/shard_map/ppermute | solution.py:282
  38.5 10.2 %collective-permute-start.10 = (bf16[2,64,512]{2,1,0:T(8,128)(2,1)S(1)}, bf16[2,64,512]{2,1,0:T(8,128)(2,1)S(1)}, u32[]{:S(2)}, u32[]{:S(2)}) collective-permute-start(bf16[2,64,512]{2,1,0:T(8,128)(2,1)S(1)} %solve_2_1.1), channel_id=1, source_target_pairs={{0,1},{1,0},{2,3},{3,2},{4,5},{5,4},{6,7},{7,6},{8,9},{9,8},{10,11... | collective-permute-start | bytes 393224 | tf_op jit(solution)/shard_map/ppermute | solution.py:282
  41.3 7.5 %collective-permute-start.8 = (bf16[2,64,512]{2,1,0:T(8,128)(2,1)S(1)}, bf16[2,64,512]{2,1,0:T(8,128)(2,1)S(1)}, u32[]{:S(2)}, u32[]{:S(2)}) collective-permute-start(bf16[2,64,512]{2,1,0:T(8,128)(2,1)S(1)} %solve_2_0.1), channel_id=1, source_target_pairs={{0,1},{1,0},{2,3},{3,2},{4,5},{5,4},{6,7},{7,6},{8,9},{9,8},{10,11... | collective-permute-start | bytes 393224 | tf_op jit(solution)/shard_map/ppermute | solution.py:282
  43.1 24.5 %collective-permute-start.13 = (bf16[2,128,512]{2,1,0:T(8,128)(2,1)}, bf16[2,128,512]{2,1,0:T(8,128)(2,1)}, u32[]{:S(2)}, u32[]{:S(2)}) collective-permute-start(bf16[2,128,512]{2,1,0:T(8,128)(2,1)} %maximum_select_fusion.4.refs_1_), channel_id=1, source_target_pairs={{0,6},{1,5},{2,4},{3,0},{4,2},{5,1},{6,7},{7,3},{8,14},{9,13},{10,... | collective-permute-start | bytes 786440 | tf_op jit(solution)/shard_map/ppermute | solution.py:282
  50.7 18.8 %collective-permute-start.12 = (bf16[2,128,512]{2,1,0:T(8,128)(2,1)}, bf16[2,128,512]{2,1,0:T(8,128)(2,1)}, u32[]{:S(2)}, u32[]{:S(2)}) collective-permute-start(bf16[2,128,512]{2,1,0:T(8,128)(2,1)} %get-tuple-element.59.refs_0_), channel_id=1, source_target_pairs={{0,6},{1,5},{2,4},{3,0},{4,2},{5,1},{6,7},{7,3},{8,14},{9,13},{10,... | collective-permute-start | bytes 786440 | tf_op jit(solution)/shard_map/ppermute | solution.py:282
  62.9 8.3 %collective-permute-start.11 = (bf16[2,64,512]{2,1,0:T(8,128)(2,1)S(1)}, bf16[2,64,512]{2,1,0:T(8,128)(2,1)S(1)}, u32[]{:S(2)}, u32[]{:S(2)}) collective-permute-start(bf16[2,64,512]{2,1,0:T(8,128)(2,1)S(1)} %solve_3_1.1), channel_id=1, source_target_pairs={{0,1},{1,0},{2,3},{3,4},{4,5},{5,2},{6,7},{7,6},{8,9},{9,8},{10,11... | collective-permute-start | bytes 393224 | tf_op jit(solution)/shard_map/ppermute | solution.py:282
  63.8 19.4 %collective-permute-start.9 = (bf16[2,64,512]{2,1,0:T(8,128)(2,1)S(1)}, bf16[2,64,512]{2,1,0:T(8,128)(2,1)S(1)}, u32[]{:S(2)}, u32[]{:S(2)}) collective-permute-start(bf16[2,64,512]{2,1,0:T(8,128)(2,1)S(1)} %solve_3_0.1), channel_id=1, source_target_pairs={{0,1},{1,0},{2,3},{3,4},{4,5},{5,2},{6,7},{7,6},{8,9},{9,8},{10,11... | collective-permute-start | bytes 393224 | tf_op jit(solution)/shard_map/ppermute | solution.py:282
  65.1 27.9 %collective-permute-start.14 = (bf16[2,128,512]{2,1,0:T(8,128)(2,1)}, bf16[2,128,512]{2,1,0:T(8,128)(2,1)}, u32[]{:S(2)}, u32[]{:S(2)}) collective-permute-start(bf16[2,128,512]{2,1,0:T(8,128)(2,1)} %get-tuple-element.58.refs_0_), channel_id=1, source_target_pairs={{0,1},{1,7},{2,6},{3,5},{4,0},{5,2},{6,4},{7,3},{8,9},{9,15},{10,1... | collective-permute-start | bytes 786440 | tf_op jit(solution)/shard_map/ppermute | solution.py:282
  67.6 25.4 %collective-permute-start.15 = (bf16[2,128,512]{2,1,0:T(8,128)(2,1)}, bf16[2,128,512]{2,1,0:T(8,128)(2,1)}, u32[]{:S(2)}, u32[]{:S(2)}) collective-permute-start(bf16[2,128,512]{2,1,0:T(8,128)(2,1)} %maximum_select_fusion.7.refs_1_), channel_id=1, source_target_pairs={{0,1},{1,7},{2,6},{3,5},{4,0},{5,2},{6,4},{7,3},{8,9},{9,15},{10,1... | collective-permute-start | bytes 786440 | tf_op jit(solution)/shard_map/ppermute | solution.py:282
  71.3 15.8 %collective-permute-start.18 = (bf16[2,64,512]{2,1,0:T(8,128)(2,1)S(1)}, bf16[2,64,512]{2,1,0:T(8,128)(2,1)S(1)}, u32[]{:S(2)}, u32[]{:S(2)}) collective-permute-start(bf16[2,64,512]{2,1,0:T(8,128)(2,1)S(1)} %solve_4_1.1), channel_id=1, source_target_pairs={{0,1},{1,0},{2,3},{3,2},{4,5},{5,4},{6,7},{7,6},{8,9},{9,8},{10,11... | collective-permute-start | bytes 393224 | tf_op jit(solution)/shard_map/ppermute | solution.py:282
  83.2 5.0 %collective-permute-start.16 = (bf16[2,64,512]{2,1,0:T(8,128)(2,1)S(1)}, bf16[2,64,512]{2,1,0:T(8,128)(2,1)S(1)}, u32[]{:S(2)}, u32[]{:S(2)}) collective-permute-start(bf16[2,64,512]{2,1,0:T(8,128)(2,1)S(1)} %solve_4_0.1), channel_id=1, source_target_pairs={{0,1},{1,0},{2,3},{3,2},{4,5},{5,4},{6,7},{7,6},{8,9},{9,8},{10,11... | collective-permute-start | bytes 393224 | tf_op jit(solution)/shard_map/ppermute | solution.py:282
  85.1 37.0 %collective-permute-start.21 = (bf16[2,128,512]{2,1,0:T(8,128)(2,1)}, bf16[2,128,512]{2,1,0:T(8,128)(2,1)}, u32[]{:S(2)}, u32[]{:S(2)}) collective-permute-start(bf16[2,128,512]{2,1,0:T(8,128)(2,1)} %maximum_select_fusion.8.refs_1_), channel_id=1, source_target_pairs={{0,1},{1,2},{2,0},{3,7},{4,6},{5,3},{6,4},{7,5},{8,9},{9,10},{10,8... | collective-permute-start | bytes 786440 | tf_op jit(solution)/shard_map/ppermute | solution.py:282
  90.2 34.6 %collective-permute-start.20 = (bf16[2,128,512]{2,1,0:T(8,128)(2,1)}, bf16[2,128,512]{2,1,0:T(8,128)(2,1)}, u32[]{:S(2)}, u32[]{:S(2)}) collective-permute-start(bf16[2,128,512]{2,1,0:T(8,128)(2,1)} %get-tuple-element.57.refs_0_), channel_id=1, source_target_pairs={{0,1},{1,2},{2,0},{3,7},{4,6},{5,3},{6,4},{7,5},{8,9},{9,10},{10,8... | collective-permute-start | bytes 786440 | tf_op jit(solution)/shard_map/ppermute | solution.py:282
  101.4 26.1 %collective-permute-start.19 = (bf16[2,64,512]{2,1,0:T(8,128)(2,1)S(1)}, bf16[2,64,512]{2,1,0:T(8,128)(2,1)S(1)}, u32[]{:S(2)}, u32[]{:S(2)}) collective-permute-start(bf16[2,64,512]{2,1,0:T(8,128)(2,1)S(1)} %solve_5_1.1), channel_id=1, source_target_pairs={{0,1},{1,0},{2,3},{3,2},{4,5},{5,6},{6,7},{7,4},{8,9},{9,8},{10,11... | collective-permute-start | bytes 393224 | tf_op jit(solution)/shard_map/ppermute | solution.py:282
  120.2 7.4 %collective-permute-start.17 = (bf16[2,64,512]{2,1,0:T(8,128)(2,1)S(1)}, bf16[2,64,512]{2,1,0:T(8,128)(2,1)S(1)}, u32[]{:S(2)}, u32[]{:S(2)}) collective-permute-start(bf16[2,64,512]{2,1,0:T(8,128)(2,1)S(1)} %solve_5_0.1), channel_id=1, source_target_pairs={{0,1},{1,0},{2,3},{3,2},{4,5},{5,6},{6,7},{7,4},{8,9},{9,8},{10,11... | collective-permute-start | bytes 393224 | tf_op jit(solution)/shard_map/ppermute | solution.py:282
  121.0 23.0 %collective-permute-start.22 = (bf16[2,128,512]{2,1,0:T(8,128)(2,1)S(1)}, bf16[2,128,512]{2,1,0:T(8,128)(2,1)S(1)}, u32[]{:S(2)}, u32[]{:S(2)}) collective-permute-start(bf16[2,128,512]{2,1,0:T(8,128)(2,1)S(1)} %copy-done.10), channel_id=1, source_target_pairs={{0,3},{1,0},{2,4},{3,1},{4,2},{5,7},{6,5},{7,6},{8,11},{9,8},{10,1... | collective-permute-start | bytes 786440 | tf_op jit(solution)/shard_map/ppermute | solution.py:282
  122.1 22.0 %collective-permute-start.23 = (bf16[2,128,512]{2,1,0:T(8,128)(2,1)S(1)}, bf16[2,128,512]{2,1,0:T(8,128)(2,1)S(1)}, u32[]{:S(2)}, u32[]{:S(2)}) collective-permute-start(bf16[2,128,512]{2,1,0:T(8,128)(2,1)S(1)} %maximum_select_fusion.11.refs_1_), channel_id=1, source_target_pairs={{0,3},{1,0},{2,4},{3,1},{4,2},{5,7},{6,5},{7,6},{8,11},{9,8},{10,1... | collective-permute-start | bytes 786440 | tf_op jit(solution)/shard_map/ppermute | solution.py:282
  127.5 13.9 %collective-permute-start.25 = (bf16[2,64,512]{2,1,0:T(8,128)(2,1)S(1)}, bf16[2,64,512]{2,1,0:T(8,128)(2,1)S(1)}, u32[]{:S(2)}, u32[]{:S(2)}) collective-permute-start(bf16[2,64,512]{2,1,0:T(8,128)(2,1)S(1)} %solve_6_1.1), channel_id=1, source_target_pairs={{0,1},{1,0},{2,3},{3,2},{4,5},{5,4},{6,7},{7,6},{8,9},{9,8},{10,11... | collective-permute-start | bytes 393224 | tf_op jit(solution)/shard_map/ppermute | solution.py:282
  127.6 15.6 %collective-permute-start.24 = (bf16[2,64,512]{2,1,0:T(8,128)(2,1)S(1)}, bf16[2,64,512]{2,1,0:T(8,128)(2,1)S(1)}, u32[]{:S(2)}, u32[]{:S(2)}) collective-permute-start(bf16[2,64,512]{2,1,0:T(8,128)(2,1)S(1)} %solve_6_0.1), channel_id=1, source_target_pairs={{0,1},{1,0},{2,3},{3,2},{4,5},{5,4},{6,7},{7,6},{8,9},{9,8},{10,11... | collective-permute-start | bytes 393224 | tf_op jit(solution)/shard_map/ppermute | solution.py:282
  130.4 26.5 %collective-permute-start.27 = (bf16[2,128,512]{2,1,0:T(8,128)(2,1)}, bf16[2,128,512]{2,1,0:T(8,128)(2,1)}, u32[]{:S(2)}, u32[]{:S(2)}) collective-permute-start(bf16[2,128,512]{2,1,0:T(8,128)(2,1)} %maximum_select_fusion.12.refs_1_), channel_id=1, source_target_pairs={{0,1},{1,2},{2,6},{3,7},{4,0},{5,3},{6,4},{7,5},{8,9},{9,10},{10,1... | collective-permute-start | bytes 786440 | tf_op jit(solution)/shard_map/ppermute | solution.py:282
  145.7 35.2 %copy-start.39 = (bf16[2,128,512]{2,1,0:T(8,128)(2,1)S(1)}, bf16[2,128,512]{2,1,0:T(8,128)(2,1)}, u32[]{:S(2)}) copy-start(bf16[2,128,512]{2,1,0:T(8,128)(2,1)} %get-tuple-element.54.refs_0_) | copy-start | bytes 786436
  146.8 11.0 %collective-permute-start.26 = (bf16[2,128,512]{2,1,0:T(8,128)(2,1)S(1)}, bf16[2,128,512]{2,1,0:T(8,128)(2,1)S(1)}, u32[]{:S(2)}, u32[]{:S(2)}) collective-permute-start(bf16[2,128,512]{2,1,0:T(8,128)(2,1)S(1)} %maximum_select_fusion.21.refs_1_), channel_id=1, source_target_pairs={{0,3},{1,0},{2,4},{3,7},{4,6},{5,1},{6,2},{7,5},{8,11},{9,8},{10,1... | collective-permute-start | bytes 786440 | tf_op jit(solution)/shard_map/ppermute | solution.py:282
  147.3 17.4 %collective-permute-start.28 = (bf16[2,128,512]{2,1,0:T(8,128)(2,1)S(1)}, bf16[2,128,512]{2,1,0:T(8,128)(2,1)S(1)}, u32[]{:S(2)}, u32[]{:S(2)}) collective-permute-start(bf16[2,128,512]{2,1,0:T(8,128)(2,1)S(1)} %maximum_select_fusion.21.refs_1_), channel_id=1, source_target_pairs={{0,1},{1,2},{2,4},{3,5},{4,6},{5,7},{6,0},{7,3},{8,9},{9,10},{10,1... | collective-permute-start | bytes 786440 | tf_op jit(solution)/shard_map/ppermute | solution.py:282
  148.9 15.7 %collective-permute-start.29 = (bf16[2,128,512]{2,1,0:T(8,128)(2,1)S(1)}, bf16[2,128,512]{2,1,0:T(8,128)(2,1)S(1)}, u32[]{:S(2)}, u32[]{:S(2)}) collective-permute-start(bf16[2,128,512]{2,1,0:T(8,128)(2,1)S(1)} %maximum_select_fusion.21.refs_1_), channel_id=1, source_target_pairs={{0,2},{1,0},{2,3},{3,5},{4,6},{5,4},{6,7},{7,1},{8,10},{9,8},{10,1... | collective-permute-start | bytes 786440 | tf_op jit(solution)/shard_map/ppermute | solution.py:282
  155.8 34.4 %collective-permute-start.31 = (bf16[2,128,512]{2,1,0:T(8,128)(2,1)}, bf16[2,128,512]{2,1,0:T(8,128)(2,1)S(1)}, u32[]{:S(2)}, u32[]{:S(2)}) collective-permute-start(bf16[2,128,512]{2,1,0:T(8,128)(2,1)} %get-tuple-element.54.refs_0_), channel_id=1, source_target_pairs={{0,3},{1,0},{2,4},{3,7},{4,6},{5,1},{6,2},{7,5},{8,11},{9,8},{10,1... | collective-permute-start | bytes 786440 | tf_op jit(solution)/shard_map/ppermute | solution.py:282
  157.0 33.2 %collective-permute-start.32 = (bf16[2,128,512]{2,1,0:T(8,128)(2,1)}, bf16[2,128,512]{2,1,0:T(8,128)(2,1)S(1)}, u32[]{:S(2)}, u32[]{:S(2)}) collective-permute-start(bf16[2,128,512]{2,1,0:T(8,128)(2,1)} %get-tuple-element.54.refs_0_), channel_id=1, source_target_pairs={{0,1},{1,2},{2,4},{3,5},{4,6},{5,7},{6,0},{7,3},{8,9},{9,10},{10,1... | collective-permute-start | bytes 786440 | tf_op jit(solution)/shard_map/ppermute | solution.py:282
  157.8 23.1 %collective-permute-start.33 = (bf16[2,128,512]{2,1,0:T(8,128)(2,1)}, bf16[2,128,512]{2,1,0:T(8,128)(2,1)S(1)}, u32[]{:S(2)}, u32[]{:S(2)}) collective-permute-start(bf16[2,128,512]{2,1,0:T(8,128)(2,1)} %copy-done.40), channel_id=1, source_target_pairs={{0,1},{1,2},{2,6},{3,7},{4,0},{5,3},{6,4},{7,5},{8,9},{9,10},{10,1... | collective-permute-start | bytes 786440 | tf_op jit(solution)/shard_map/ppermute | solution.py:282
  165.4 26.9 %collective-permute-start.30 = (bf16[2,128,512]{2,1,0:T(8,128)(2,1)}, bf16[2,128,512]{2,1,0:T(8,128)(2,1)S(1)}, u32[]{:S(2)}, u32[]{:S(2)}) collective-permute-start(bf16[2,128,512]{2,1,0:T(8,128)(2,1)} %select_select_fusion), channel_id=1, source_target_pairs={{0,1},{1,0},{2,3},{3,2},{4,5},{5,4},{6,7},{7,6},{8,9},{9,8},{10,11... | collective-permute-start | bytes 786440 | tf_op jit(solution)/shard_map/ppermute | solution.py:282
  193.8 8.3 %collective-permute-start.34 = (bf16[2,128,512]{2,1,0:T(8,128)(2,1)S(1)}, bf16[2,128,512]{2,1,0:T(8,128)(2,1)S(1)}, u32[]{:S(2)}, u32[]{:S(2)}) collective-permute-start(bf16[2,128,512]{2,1,0:T(8,128)(2,1)S(1)} %fusion.6.own_ref), channel_id=1, source_target_pairs={{0,1},{1,0},{2,3},{3,2},{4,5},{5,4},{6,7},{7,6},{8,9},{9,8},{10,11... | collective-permute-start | bytes 786440 | tf_op jit(solution)/shard_map/ppermute | solution.py:282
  202.1 29.8 %copy-start.20 = (bf16[2,64,512]{2,1,0:T(8,128)(2,1)S(1)}, bf16[2,64,512]{2,1,0:T(8,128)(2,1)}, u32[]{:S(2)}) copy-start(bf16[2,64,512]{2,1,0:T(8,128)(2,1)} %copy-done.19) | copy-start | bytes 393220
  202.1 29.8 %copy-start.22 = (bf16[2,64,512]{2,1,0:T(8,128)(2,1)S(1)}, bf16[2,64,512]{2,1,0:T(8,128)(2,1)}, u32[]{:S(2)}) copy-start(bf16[2,64,512]{2,1,0:T(8,128)(2,1)} %copy-done.21) | copy-start | bytes 393220
  202.1 29.8 %copy-start.24 = (bf16[2,64,512]{2,1,0:T(8,128)(2,1)S(1)}, bf16[2,64,512]{2,1,0:T(8,128)(2,1)}, u32[]{:S(2)}) copy-start(bf16[2,64,512]{2,1,0:T(8,128)(2,1)} %copy-done.23) | copy-start | bytes 393220
  202.1 29.8 %copy-start.26 = (bf16[2,64,512]{2,1,0:T(8,128)(2,1)S(1)}, bf16[2,64,512]{2,1,0:T(8,128)(2,1)}, u32[]{:S(2)}) copy-start(bf16[2,64,512]{2,1,0:T(8,128)(2,1)} %copy-done.25) | copy-start | bytes 393220
  202.1 29.8 %copy-start.28 = (bf16[2,64,512]{2,1,0:T(8,128)(2,1)S(1)}, bf16[2,64,512]{2,1,0:T(8,128)(2,1)}, u32[]{:S(2)}) copy-start(bf16[2,64,512]{2,1,0:T(8,128)(2,1)} %copy-done.27) | copy-start | bytes 393220
  202.1 29.8 %copy-start.30 = (bf16[2,64,512]{2,1,0:T(8,128)(2,1)S(1)}, bf16[2,64,512]{2,1,0:T(8,128)(2,1)}, u32[]{:S(2)}) copy-start(bf16[2,64,512]{2,1,0:T(8,128)(2,1)} %copy-done.29) | copy-start | bytes 393220
  202.1 29.8 %copy-start.32 = (bf16[2,64,512]{2,1,0:T(8,128)(2,1)S(1)}, bf16[2,64,512]{2,1,0:T(8,128)(2,1)}, u32[]{:S(2)}) copy-start(bf16[2,64,512]{2,1,0:T(8,128)(2,1)} %copy-done.31) | copy-start | bytes 393220
  202.1 29.8 %copy-start.34 = (bf16[2,64,512]{2,1,0:T(8,128)(2,1)S(1)}, bf16[2,64,512]{2,1,0:T(8,128)(2,1)}, u32[]{:S(2)}) copy-start(bf16[2,64,512]{2,1,0:T(8,128)(2,1)} %copy-done.33) | copy-start | bytes 393220
  203.7 12.6 %collective-permute-start.37 = (bf16[2,128,512]{2,1,0:T(8,128)(2,1)S(1)}, bf16[2,128,512]{2,1,0:T(8,128)(2,1)S(1)}, u32[]{:S(2)}, u32[]{:S(2)}) collective-permute-start(bf16[2,128,512]{2,1,0:T(8,128)(2,1)S(1)} %get-tuple-element.52), channel_id=1, source_target_pairs={{0,6},{1,7},{2,4},{3,5},{4,2},{5,3},{6,0},{7,1},{8,14},{9,15},{10,... | collective-permute-start | bytes 786440 | tf_op jit(solution)/shard_map/ppermute | solution.py:282
  208.9 21.5 %collective-permute-start.36 = (bf16[2,128,512]{2,1,0:T(8,128)(2,1)S(1)}, bf16[2,128,512]{2,1,0:T(8,128)(2,1)}, u32[]{:S(2)}, u32[]{:S(2)}) collective-permute-start(bf16[2,128,512]{2,1,0:T(8,128)(2,1)S(1)} %get-tuple-element.51), channel_id=1, source_target_pairs={{0,4},{1,5},{2,6},{3,7},{4,0},{5,1},{6,2},{7,3},{8,12},{9,13},{10,... | collective-permute-start | bytes 786440 | tf_op jit(solution)/shard_map/ppermute | solution.py:282
  208.9 21.5 %collective-permute-start.35 = (bf16[2,128,512]{2,1,0:T(8,128)(2,1)S(1)}, bf16[2,128,512]{2,1,0:T(8,128)(2,1)}, u32[]{:S(2)}, u32[]{:S(2)}) collective-permute-start(bf16[2,128,512]{2,1,0:T(8,128)(2,1)S(1)} %get-tuple-element.50), channel_id=1, source_target_pairs={{0,2},{1,3},{2,0},{3,1},{4,6},{5,7},{6,4},{7,5},{8,10},{9,11},{10,... | collective-permute-start | bytes 786440 | tf_op jit(solution)/shard_map/ppermute | solution.py:282
  231.8 2.1 collective-permute-start.38
  (43 other events, 461.5 us)

commit v2 on v1

v2 whole, which is shorter than its diff:
```python
import functools

import jax
import jax.numpy as jnp
import numpy as np
from jax import lax
from jax.experimental import pallas as pl
from jax.experimental.pallas import tpu as pltpu
from jax.sharding import PartitionSpec as P

CB = 512
F32 = jnp.float32
BF16 = jnp.bfloat16

SWAP = ((0, 1), (1, 0), (2, 3), (3, 2), (4, 5), (5, 4), (6, 7), (7, 6))
CHAIN = (SWAP, ((1, 2),), SWAP, ((3, 4),), SWAP, ((5, 6),), SWAP)
RELAY = {2: {4: (0, 1), 6: (0, 2)}, 4: {6: (2, 2), 7: (2, 3)}, 6: {0: (4, 3), 1: (4, 2)}}
SPREAD = (
    ((True, ((0, 2),), 1), (True, ((0, 4),), 3), (True, ((0, 6),), 5)),
    ((False, ((1, 3),), 2), (True, ((1, 3),), 2), (True, ((1, 5),), 4)),
    ((False, ((2, 4),), 3), (True, ((2, 4),), 3), (True, ((2, 6),), 5), (True, ((1, 7),), 6)),
    ((False, ((3, 5),), 4), (True, ((3, 5),), 4)),
    ((False, ((4, 6),), 5), (True, ((4, 6), (3, 7)), 5), (True, ((3, 1),), 7), (True, ((2, 0),), 7)),
    ((False, ((5, 7),), 6), (True, ((5, 7), (4, 2)), 6)),
    (
        (True, ((6, 4), (5, 3), (4, 0)), 7),
        (True, ((6, 2), (5, 1)), 7),
        (True, ((6, 0),), 7),
        (False, ((5, 3),), 7),
        (False, ((5, 1),), 7),
    ),
    ((True, ((7, 5),), 8), (True, ((7, 3),), 8), (True, ((7, 1),), 8)),
)


def spread_plan(count):
    have = [{p} for p in range(count)]

    def taken(edges, block_of):
        row = [-1] * count
        for source, dest in edges:
            block = block_of(source)
            if block is not None and block not in have[dest]:
                row[dest] = block
        return row

    def keep(row):
        for p, block in enumerate(row):
            if block >= 0:
                assert block not in have[p]
                have[p].add(block)

    chain = []
    spread = []
    for hop in range(count):
        if hop < len(CHAIN):

            def passed(p, hop=hop):
                if p in RELAY.get(hop, {}):
                    earlier, i = RELAY[hop][p]
                    return spread[earlier][i][p]
                return p if p <= hop else None

            row = taken(CHAIN[hop], passed)
            assert row[hop + 1] == hop
            keep(row)
            chain.append(row)
        rows = []
        for own, edges, _ in SPREAD[hop]:
            row = taken(edges, lambda source, own=own: source if own else source - 1)
            assert sum(block >= 0 for block in row) == len(edges)
            keep(row)
            rows.append(row)
        spread.append(rows)
    swaps = []
    for even, odd in ((count - 3, count - 2), (count - 1, None)):
        row = taken(SWAP, lambda source, even=even, odd=odd: even if source % 2 else odd)
        keep(row)
        swaps.append(row)
    assert all(held == set(range(count)) for held in have)
    for p in range(count):
        for hop, rows in enumerate(spread):
            for (_, _, use), row in zip(SPREAD[hop], rows):
                assert use > hop and (row[p] < 0 or row[p] > p or use < p)
        for hop, row in enumerate(chain):
            assert row[p] < 0 or row[p] > p or hop + 1 < p or (hop + 1 == p and row[p] == hop)
    return spread, chain, swaps


def stacked(value):
    return jnp.concatenate([value[0], value[1]], axis=0)


def turned_of(value):
    half = value.shape[0] // 2
    return jnp.concatenate([-value[half:], value[:half]], axis=0)


def apply_rows(value, matrix_real, matrix_imag):
    dims = (((1,), (1,)), ((), ()))
    return lax.dot_general(value, matrix_real, dims, preferred_element_type=F32) + lax.dot_general(
        turned_of(value), matrix_imag, dims, preferred_element_type=F32
    )


def apply_columns(value, matrix_real, matrix_imag):
    return jnp.dot(value, matrix_real, preferred_element_type=F32) + jnp.dot(
        turned_of(value), matrix_imag, preferred_element_type=F32
    )


def setup_kernel(place_ref, lower_ref, inverse_ref, pivot_ref, near_ref, inv_ref, rhs_ref, acc_l_ref, acc_u_ref, mine_ref, before_ref, sems):
    width = near_ref.shape[-1]
    block = jnp.maximum(place_ref[0] - 1, 0)
    columns = pl.ds(pl.multiple_of(block * width, width), width)
    copies = (
        pltpu.make_async_copy(pivot_ref.at[0], rhs_ref, sems.at[0]),
        pltpu.make_async_copy(inverse_ref.at[0], inv_ref, sems.at[1]),
        pltpu.make_async_copy(lower_ref.at[0, :, :, columns], near_ref, sems.at[2]),
    )
    for copy in copies:
        copy.start()
    for ref in (acc_l_ref, acc_u_ref, mine_ref, before_ref):
        ref[...] = jnp.zeros_like(ref)
    for copy in copies:
        copy.wait()


def setup(place, lower, inverse, pivot):
    rows = lower.shape[2]
    shots = pivot.shape[2]
    hbm = pl.BlockSpec(memory_space=pltpu.HBM)
    vmem = pl.BlockSpec(memory_space=pltpu.VMEM)
    weight = pltpu.VMEM((2, rows, CB), BF16)
    block = pltpu.VMEM((2, shots, CB), BF16)
    acc = pltpu.VMEM((2, shots, rows), F32)
    return pl.pallas_call(
        setup_kernel,
        out_shape=(weight, weight, block, acc, acc, block, block),
        in_specs=[pl.BlockSpec(memory_space=pltpu.SMEM), hbm, hbm, hbm],
        out_specs=(vmem,) * 7,
        scratch_shapes=[pltpu.SemaphoreType.DMA((3,))],
        compiler_params=pltpu.CompilerParams(vmem_limit_bytes=46 * 2**20),
        name="setup",
    )(place, lower, inverse, pivot)


def solve_kernel(hop, relays, place_ref, rhs_ref, acc_ref, near_ref, inv_ref, urgent_ref, mine_in, before_in, *refs):
    relay_refs, (out_ref, mine_ref, before_ref) = refs[: len(relays)], refs[len(relays) :]
    place = place_ref[0]
    shots = out_ref.shape[1]

    @pl.when(place != hop)
    def _():
        out_ref[...] = mine_in[...]
        mine_ref[...] = mine_in[...]
        before_ref[...] = before_in[...]

    for p, relay_ref in zip(relays, relay_refs):

        @pl.when(place == p)
        def _(relay_ref=relay_ref):
            out_ref[...] = relay_ref[...]

    @pl.when(place == hop)
    def _():
        residual = stacked(rhs_ref[...]).astype(F32)
        if hop > 0:
            residual = residual - stacked(acc_ref[...])
            residual = residual - apply_rows(stacked(urgent_ref[...]), near_ref[0], near_ref[1])
        term = apply_columns(residual.astype(BF16), inv_ref[0], inv_ref[1]).astype(BF16)
        for ref in (out_ref, mine_ref):
            ref[0] = term[:shots]
            ref[1] = term[shots:]
        before_ref[...] = urgent_ref[...]


def solve(hop, place, rhs, acc, near, inv, urgent, mine, before, relays):
    vmem = pl.BlockSpec(memory_space=pltpu.VMEM)
    smem = pl.BlockSpec(memory_space=pltpu.SMEM)
    block = pltpu.VMEM(mine.shape, BF16)
    args = [rhs, acc, near, inv, urgent, mine, before, *relays.values()]
    return pl.pallas_call(
        functools.partial(solve_kernel, hop, tuple(relays)),
        out_shape=(block,) * 3,
        in_specs=[smem] + [vmem] * len(args),
        out_specs=(vmem,) * 3,
        compiler_params=pltpu.CompilerParams(vmem_limit_bytes=16 * 2**20),
        name=f"solve_{hop}",
    )(place, *args)


def gather_kernel(arrivals, left, place_ref, *refs):
    count = len(left)
    parts = refs[:count]
    lower_ref, update_ref, acc_l_in, acc_u_in, acc_l_ref, acc_u_ref, buf_l, buf_u, sems = refs[count:]
    width = buf_l.shape[-1]
    shots = acc_l_ref.shape[1]
    place = place_ref[0]
    blocks = []
    for row in arrivals:
        block = jnp.int32(-1)
        for p, value in enumerate(row):
            if value >= 0:
                block = jnp.where(place == p, value, block)
        blocks.append(block)

    def copy_of(i, panel_ref, buf, which):
        block = jnp.maximum(blocks[i], 0)
        columns = pl.ds(pl.multiple_of(block * width, width), width)
        return pltpu.make_async_copy(panel_ref.at[0, :, :, columns], buf.at[i], sems.at[i, which])

    def when_update(i):
        return blocks[i] >= 0

    def when_lower(i):
        return jnp.logical_and(blocks[i] >= 0, blocks[i] < place)

    for i in range(count):
        if left[i]:

            @pl.when(when_lower(i))
            def _(i=i):
                copy_of(i, lower_ref, buf_l, 0).start()

        @pl.when(when_update(i))
        def _(i=i):
            copy_of(i, update_ref, buf_u, 1).start()

    acc_l_ref[...] = acc_l_in[...]
    acc_u_ref[...] = acc_u_in[...]

    def add(i, copy, buf, acc_ref):
        copy.wait()
        product = apply_rows(stacked(parts[i][...]), buf[i, 0], buf[i, 1])
        acc_ref[0] += product[:shots]
        acc_ref[1] += product[shots:]

    for i in range(count):
        if left[i]:

            @pl.when(when_lower(i))
            def _(i=i):
                add(i, copy_of(i, lower_ref, buf_l, 0), buf_l, acc_l_ref)

        @pl.when(when_update(i))
        def _(i=i):
            add(i, copy_of(i, update_ref, buf_u, 1), buf_u, acc_u_ref)


def accumulate(name, place, items, lower, update, acc_l, acc_u):
    parts = [item[0] for item in items]
    arrivals = [item[1] for item in items]
    left = [item[2] for item in items]
    count = len(parts)
    vmem = pl.BlockSpec(memory_space=pltpu.VMEM)
    hbm = pl.BlockSpec(memory_space=pltpu.HBM)
    rows = lower.shape[2]
    shape = pltpu.VMEM(acc_l.shape, F32)
    return pl.pallas_call(
        functools.partial(gather_kernel, arrivals, left),
        out_shape=(shape, shape),
        in_specs=[pl.BlockSpec(memory_space=pltpu.SMEM)] + [vmem] * count + [hbm, hbm, vmem, vmem],
        out_specs=(vmem, vmem),
        scratch_shapes=[
            pltpu.VMEM((count, 2, rows, CB), BF16),
            pltpu.VMEM((count, 2, rows, CB), BF16),
            pltpu.SemaphoreType.DMA((count, 2)),
        ],
        input_output_aliases={count + 3: 0, count + 4: 1},
        compiler_params=pltpu.CompilerParams(vmem_limit_bytes=46 * 2**20),
        name=name,
    )(place, *parts, lower, update, acc_l, acc_u)


def place_kernel(own_ref, other_ref, own_hot_ref, other_hot_ref, *out_refs):
    own = stacked(own_ref[...])
    other = stacked(other_ref[...])
    shots = own_ref.shape[1]
    for i, out_ref in enumerate(out_refs):
        rows = jnp.dot(own, own_hot_ref[i], preferred_element_type=F32) + jnp.dot(
            other, other_hot_ref[i], preferred_element_type=F32
        )
        rows = rows.astype(BF16)
        out_ref[0] = rows[:shots]
        out_ref[1] = rows[shots:]


def place_rows(own, other, own_hot, other_hot):
    vmem = pl.BlockSpec(memory_space=pltpu.VMEM)
    shape = jax.ShapeDtypeStruct(own.shape, BF16)
    count = own_hot.shape[0]
    return pl.pallas_call(
        place_kernel,
        out_shape=(shape,) * count,
        in_specs=[vmem] * 4,
        out_specs=(vmem,) * count,
        compiler_params=pltpu.CompilerParams(vmem_limit_bytes=24 * 2**20),
        name="place_rows",
    )(own, other, own_hot, other_hot)


def placements(row_maps, place, count, rows):
    own_map = lax.dynamic_index_in_dim(row_maps, lax.axis_index("front"), 0, keepdims=False)
    level = place // 2
    firsts = [place * rows, (count + place) * rows]
    for step in range(1, count // 2):
        far = level ^ step
        target = 2 * far + place % 2
        firsts.append(jnp.where(far < level, count + target, target) * rows)
    firsts = jnp.stack(firsts)
    targets = firsts[:, None] + jnp.arange(rows, dtype=jnp.int32)[None, :]

    def hot(device):
        mapped = lax.dynamic_slice_in_dim(own_map, device * rows, rows, 0)
        return (mapped[None, :, None] == targets[:, None, :]).astype(BF16)

    return hot(place), hot(place ^ 1)


def relay_body(lower_panel, inverse_cols, update_panel, pivot_rhs, update_rhs, row_maps, parent_rhs):
    shots = pivot_rhs.shape[2]
    upd_rows = update_panel.shape[2]
    count = lax.axis_size("panel")
    place = lax.axis_index("panel").astype(jnp.int32)
    level = place // 2
    spread_rows, chain_rows, swap_rows = spread_plan(count)

    def send(value, edges):
        return lax.ppermute(value, "panel", edges)

    place_ref = jnp.reshape(place, (1,))
    own_hot, other_hot = placements(row_maps, place, count, upd_rows)
    near, inv, rhs, acc_l, acc_u, mine, before = setup(place_ref, lower_panel, inverse_cols, pivot_rhs)
    urgent = mine
    came = []
    for hop in range(count):
        relays = {p: came[earlier][i] for p, (earlier, i) in RELAY.get(hop, {}).items()}
        passed, mine, before = solve(hop, place_ref, rhs, acc_l, near, inv, urgent, mine, before, relays)
        parts = [(mine, [hop if p == hop else -1 for p in range(count)], False)]
        if hop:
            parts.append((urgent, chain_rows[hop - 1], True))
        if hop < len(CHAIN):
            urgent = send(passed, CHAIN[hop])
        came.append([send(mine if own else before, edges) for own, edges, _ in SPREAD[hop]])
        for earlier in range(hop):
            for i, (_, _, use) in enumerate(SPREAD[earlier]):
                if use == hop:
                    parts.append((came[earlier][i], spread_rows[earlier][i], True))
        acc_l, acc_u = accumulate(f"accumulate_{hop}", place_ref, parts, lower_panel, update_panel, acc_l, acc_u)

    def cross(blocks):
        value = mine
        for earlier, rows in enumerate(spread_rows):
            for i, row in enumerate(rows):
                for p in range(count):
                    if row[p] == blocks[p % 2]:
                        value = jnp.where(place == p, came[earlier][i], value)
        return send(value, SWAP)

    first = cross((count - 2, count - 3))
    second = cross((None, count - 1))
    parts = [(came[-1][i], row, False) for i, row in enumerate(spread_rows[-1])]
    parts.append((first, swap_rows[0], False))
    acc_l, acc_u = accumulate("accumulate_late", place_ref, parts, lower_panel, update_panel, acc_l, acc_u)
    parts = [(second, swap_rows[1], False)]
    acc_l, acc_u = accumulate("accumulate_last", place_ref, parts, lower_panel, update_panel, acc_l, acc_u)
    child = (update_rhs[0].astype(F32) - acc_u).astype(BF16)
    other = send(child, SWAP)
    placed = place_rows(child, other, own_hot, other_hot)
    sums = [placed[0].astype(F32), placed[1].astype(F32)]
    for step in range(1, count // 2):
        moved = send(placed[1 + step], [(p, p ^ (2 * step)) for p in range(count)]).astype(F32)
        below = (level ^ step) < level
        sums[0] = sums[0] + jnp.where(below, moved, 0.0)
        sums[1] = sums[1] + jnp.where(below, 0.0, moved)
    odd_front = lax.axis_index("front") % 2 == 1
    kept = jnp.where(odd_front, sums[1], sums[0])
    given = jnp.where(odd_front, sums[0], sums[1]).astype(BF16)
    sibling = lax.ppermute(given, "front", [(f, f ^ 1) for f in range(lax.axis_size("front"))])
    parent_out = parent_rhs[0] + kept + sibling.astype(F32)
    return (mine[None], parent_out[None])


def select_rows(block_rows, index_map, base, owned):
    targets = base + jnp.arange(owned, dtype=jnp.int32)
    placement = (index_map[:, None] == targets[None, :]).astype(BF16)
    return jnp.einsum("csu,ur->csr", block_rows, placement, preferred_element_type=F32)


def extend_add(child_update, row_maps, parent_f):
    upd_rows = child_update.shape[2]
    panel_count = lax.axis_size("panel")
    panel_number = lax.axis_index("panel")
    front_number = lax.axis_index("front")
    parity = front_number % 2
    sibling_front = front_number + 1 - 2 * parity
    my_base = (parity * panel_count + panel_number) * upd_rows
    own_map = lax.dynamic_index_in_dim(row_maps, front_number, 0, keepdims=False)
    sibling_map = lax.dynamic_index_in_dim(row_maps, sibling_front, 0, keepdims=False)
    gathered = lax.all_gather(child_update, "panel", axis=2, tiled=True)
    pairs = [(source, source ^ 1) for source in range(lax.axis_size("front"))]
    sibling = lax.ppermute(gathered, "front", pairs)
    assembled = select_rows(gathered, own_map, my_base, upd_rows) + select_rows(
        sibling, sibling_map, my_base, upd_rows
    )
    return parent_f + assembled


def complex_product(matrix, vector, pattern):
    real_part = jnp.einsum(pattern, matrix[0], vector[0], preferred_element_type=F32) - jnp.einsum(
        pattern, matrix[1], vector[1], preferred_element_type=F32
    )
    imag_part = jnp.einsum(pattern, matrix[0], vector[1], preferred_element_type=F32) + jnp.einsum(
        pattern, matrix[1], vector[0], preferred_element_type=F32
    )
    return jnp.stack([real_part, imag_part])


def summed_body(lower_panel, inverse_cols, update_panel, pivot_rhs, update_rhs, row_maps, parent_rhs):
    lower_f = lower_panel[0]
    pivot_f = pivot_rhs[0]
    own_rows = lower_f.shape[1]
    block_count = lower_f.shape[2] // CB
    panel_number = lax.axis_index("panel")
    owner_block = panel_number * own_rows // CB
    partial_sum = jnp.zeros((2, pivot_f.shape[1], own_rows), F32)
    blocks = []
    for block in range(block_count):
        first = block * CB
        residual = (pivot_f.astype(F32) - partial_sum).astype(BF16)
        block_term = complex_product(inverse_cols[0], residual, "ri,sr->si")
        block_term = jnp.where(owner_block == block, block_term, 0.0)
        block_value = lax.psum(block_term.astype(BF16), "panel")
        blocks.append(block_value)
        partial_sum = partial_sum + complex_product(lower_f[:, :, first : first + CB], block_value, "rc,sc->sr")
    solution_f = jnp.concatenate(blocks, axis=2)
    own_solution = lax.dynamic_slice_in_dim(solution_f, panel_number * own_rows, own_rows, 2)
    applied = complex_product(update_panel[0], solution_f, "rc,sc->sr")
    child_update = (update_rhs[0].astype(F32) - applied).astype(BF16)
    parent_out = extend_add(child_update, row_maps, parent_rhs[0])
    return (own_solution[None], parent_out[None])


def solution(mesh):
    in_specs = (
        P("front", None, "panel", None),
        P("front", None, "panel", None),
        P("front", None, "panel", None),
        P("front", None, None, "panel"),
        P("front", None, None, "panel"),
        P(),
        P("front", None, None, "panel"),
    )
    out_specs = (P("front", None, None, "panel"), P("front", None, None, "panel"))

    def run(lower_panel, *others):
        blocks = lower_panel.shape[3] // CB
        one_block = mesh.shape["panel"] == blocks == len(SWAP)
        body = relay_body if one_block else summed_body
        call = jax.shard_map(body, mesh=mesh, in_specs=in_specs, out_specs=out_specs, check_vma=False)
        return call(lower_panel, *others)

    return run
```

time: 238 us -> 170 us (0.71)
  local copies, waits for them, and re-layouts: 41.1 us -> 4.78 us
  starting transfers between devices: 88.3 us -> 66.1 us
  other arithmetic: 25.6 us -> 3.43 us
  waiting for transfers between devices: 55 us -> 71 us
    unnamed x104 -> x17, local copies, waits for them, and re-layouts: 31.4 us -> 3.84 us
    ppermute x38 -> x39, starting transfers between devices: 88.2 us -> 66.1 us  [send(): return lax.ppermute(value, 'panel', edges)]
    select_n x14 -> x1, other arithmetic: 20.4 us -> 0.9 us  [cross(): value = jnp.where(place == p, came[earlier][i], value)]
    ppermute x38 -> x39, waiting for transfers between devices: 55 us -> 70.2 us  [send(): return lax.ppermute(value, 'panel', edges)]
    squeeze x10 -> x0, local copies, waits for them, and re-layouts: 6.92 us -> none  [table(): lax.dynamic_index_in_dim(jnp.asarray(columns), place, 1, keepdims=False)]
    pallas_call x27 -> x19, Pallas kernels: 23 us -> 20.6 us  [the longest x10 15.8 us: accumulate(): pl.pallas_call(functools.partial(gather_kernel, arrivals, left), out_shap...]
  transfers between devices with their start and end apart: 39 -> 40, of which waited for: 8 -> 14; matrix products, arithmetic and copies ran while one was open for 13% -> 2% of each run, Pallas kernels for 8% -> 10%
where the time goes in v2:
time: 170 us; the launch traced here: 169 us
  waiting for transfers between devices  71 us (42%)
  starting transfers between devices  66.1 us (39%)
  Pallas kernels  22.2 us (13%)
  local copies, waits for them, and re-layouts  4.78 us (3%)
  other arithmetic  3.43 us (2%)
    ppermute x39, waiting for transfers between devices, send(): return lax.ppermute(value, 'panel', edges)  70.2 us
    ppermute x39, starting transfers between devices, send(): return lax.ppermute(value, 'panel', edges)  66.1 us
    pallas_call x10, Pallas kernels, accumulate(): pl.pallas_call(functools.partial(gather_kernel, arrivals, left), out_shap...  15.8 us
    unnamed x17, local copies, waits for them, and re-layouts  3.84 us
    pallas_call x8, Pallas kernels, solve(): pl.pallas_call(functools.partial(solve_kernel, hop, tuple(relays)), out_s...  3.42 us
  transfers between devices with their start and end apart: 40, of which 14 were waited for; matrix products, arithmetic and copies ran while one was open for 2% of the time, Pallas kernels for 10%

profile of v2, /device:TPU:0, one launch (start us, length us, event | category | flops | bytes accessed | tf_op | source)
XLA Modules:
  0.0 168.8 jit_solution(17972970888810629160)
XLA Ops:
  0.6 1.2 copy-done.3
  1.9 0.9 copy-done.4
  2.8 1.4 setup.1
  4.7 2.6 %collective-permute-start = (bf16[2,128,512]{2,1,0:T(8,128)(2,1)S(1)}, bf16[2,128,512]{2,1,0:T(8,128)(2,1)S(1)}, u32[]{:S(2)}, u32[]{:S(2)}) collective-permute-start(bf16[2,128,512]{2,1,0:T(8,128)(2,1)S(1)} %get-tuple-element.64), channel_id=1, source_target_pairs={{0,1},{1,0},{2,3},{3,2},{4,5},{5,4},{6,7},{7,6},{8,9},{9,8},{10,11... | collective-permute-start | bytes 786440 | tf_op jit(solution)/shard_map/ppermute | solution.py:330
  7.3 3.5 %collective-permute-start.1 = (bf16[2,128,512]{2,1,0:T(8,128)(2,1)S(1)}, bf16[2,128,512]{2,1,0:T(8,128)(2,1)S(1)}, u32[]{:S(2)}, u32[]{:S(2)}) collective-permute-start(bf16[2,128,512]{2,1,0:T(8,128)(2,1)S(1)} %get-tuple-element.61.refs_0_.mine_in), channel_id=1, source_target_pairs={{0,2},{8,10},{16,18},{24,26}} | collective-permute-start | bytes 786440 | tf_op jit(solution)/shard_map/ppermute | solution.py:330
  10.8 1.7 %collective-permute-start.3 = (bf16[2,128,512]{2,1,0:T(8,128)(2,1)S(1)}, bf16[2,128,512]{2,1,0:T(8,128)(2,1)S(1)}, u32[]{:S(2)}, u32[]{:S(2)}) collective-permute-start(bf16[2,128,512]{2,1,0:T(8,128)(2,1)S(1)} %get-tuple-element.61.refs_0_.mine_in), channel_id=1, source_target_pairs={{0,4},{8,12},{16,20},{24,28}} | collective-permute-start | bytes 786440 | tf_op jit(solution)/shard_map/ppermute | solution.py:330
  12.5 1.7 %collective-permute-start.4 = (bf16[2,128,512]{2,1,0:T(8,128)(2,1)S(1)}, bf16[2,128,512]{2,1,0:T(8,128)(2,1)S(1)}, u32[]{:S(2)}, u32[]{:S(2)}) collective-permute-start(bf16[2,128,512]{2,1,0:T(8,128)(2,1)S(1)} %get-tuple-element.61.refs_0_.mine_in), channel_id=1, source_target_pairs={{0,6},{8,14},{16,22},{24,30}} | collective-permute-start | bytes 786440 | tf_op jit(solution)/shard_map/ppermute | solution.py:330
  14.2 1.7 %accumulate_0.1 = (f32[2,128,512]{2,1,0:T(8,128)S(1)}, f32[2,128,512]{2,1,0:T(8,128)S(1)}) custom-call(s32[1]{0:T(128)} %bitcast.place_ref, bf16[2,128,512]{2,1,0:T(8,128)(2,1)S(1)} %get-tuple-element.61.refs_0_.mine_in, bf16[1,2,512,4096]{3,2,1,0:T(8,128)(2,1)} %refs_1_.3, ...), custom_call_target="tpu_custom_call", output_to_operand_aliasing={{0}: (4, {}), {1}: (5, {})} | custom-call | tf_op jit(solution)/shard_map/accumulate_0/pallas_call | solution.py:260
  16.7 0.7 collective-permute-start.5
  18.4 4.7 %collective-permute-done.3.refs_0_.refs_2_ = bf16[2,128,512]{2,1,0:T(8,128)(2,1)S(1)} collective-permute-done((bf16[2,128,512]{2,1,0:T(8,128)(2,1)S(1)}, bf16[2,128,512]{2,1,0:T(8,128)(2,1)S(1)}, u32[]{:S(2)}, u32[]{:S(2)}) %collective-permute-start.3) | collective-permute-done | bytes 262176 | tf_op jit(solution)/shard_map/ppermute | solution.py:330
  23.2 4.2 %collective-permute-done.4.refs_1_.refs_2_ = bf16[2,128,512]{2,1,0:T(8,128)(2,1)S(1)} collective-permute-done((bf16[2,128,512]{2,1,0:T(8,128)(2,1)S(1)}, bf16[2,128,512]{2,1,0:T(8,128)(2,1)S(1)}, u32[]{:S(2)}, u32[]{:S(2)}) %collective-permute-start.4) | collective-permute-done | bytes 262176 | tf_op jit(solution)/shard_map/ppermute | solution.py:330
  30.5 3.8 %collective-permute-done.7.urgent_ref.refs_1_ = bf16[2,128,512]{2,1,0:T(8,128)(2,1)S(1)} collective-permute-done((bf16[2,128,512]{2,1,0:T(8,128)(2,1)S(1)}, bf16[2,128,512]{2,1,0:T(8,128)(2,1)S(1)}, u32[]{:S(2)}, u32[]{:S(2)}) %collective-permute-start.7) | collective-permute-done | bytes 262176 | tf_op jit(solution)/shard_map/ppermute | solution.py:330
  35.1 0.7 collective-permute-start.13
  36.4 1.8 %accumulate_3.1 = (f32[2,128,512]{2,1,0:T(8,128)S(1)}, f32[2,128,512]{2,1,0:T(8,128)S(1)}) custom-call(s32[1]{0:T(128)} %bitcast.place_ref, bf16[2,128,512]{2,1,0:T(8,128)(2,1)S(1)} %get-tuple-element.76.refs_0_.mine_in, bf16[2,128,512]{2,1,0:T(8,128)(2,1)S(1)} %collective-permute-done.7.urgent_ref.refs_1_, ...), custom_call_target="tpu_custom_call", output_to_operand_aliasing={{0}: (8, {}), {1}: (9, {})} | custom-call | tf_op jit(solution)/shard_map/accumulate_3/pallas_call | solution.py:260
  39.1 5.7 %collective-permute-start.16 = (bf16[2,128,512]{2,1,0:T(8,128)(2,1)S(1)}, bf16[2,128,512]{2,1,0:T(8,128)(2,1)S(1)}, u32[]{:S(2)}, u32[]{:S(2)}) collective-permute-start(bf16[2,128,512]{2,1,0:T(8,128)(2,1)S(1)} %get-tuple-element.84), channel_id=1, source_target_pairs={{0,1},{1,0},{2,3},{3,2},{4,5},{5,4},{6,7},{7,6},{8,9},{9,8},{10,11... | collective-permute-start | bytes 786440 | tf_op jit(solution)/shard_map/ppermute | solution.py:330
  46.2 1.3 collective-permute-start.20
  49.2 0.7 collective-permute-start.19
  50.6 0.7 collective-permute-start.23
  51.6 11.9 %collective-permute-done.20.refs_0_.refs_3_ = bf16[2,128,512]{2,1,0:T(8,128)(2,1)S(1)} collective-permute-done((bf16[2,128,512]{2,1,0:T(8,128)(2,1)S(1)}, bf16[2,128,512]{2,1,0:T(8,128)(2,1)S(1)}, u32[]{:S(2)}, u32[]{:S(2)}) %collective-permute-start.20) | collective-permute-done | bytes 262176 | tf_op jit(solution)/shard_map/ppermute | solution.py:330
  63.5 0.8 solve_6.1
  64.3 10.7 %collective-permute-start.24 = (bf16[2,128,512]{2,1,0:T(8,128)(2,1)S(1)}, bf16[2,128,512]{2,1,0:T(8,128)(2,1)S(1)}, u32[]{:S(2)}, u32[]{:S(2)}) collective-permute-start(bf16[2,128,512]{2,1,0:T(8,128)(2,1)S(1)} %get-tuple-element.94), channel_id=1, source_target_pairs={{0,1},{1,0},{2,3},{3,2},{4,5},{5,4},{6,7},{7,6},{8,9},{9,8},{10,11... | collective-permute-start | bytes 786440 | tf_op jit(solution)/shard_map/ppermute | solution.py:330
  75.0 1.3 collective-permute-start.29
  77.0 1.3 collective-permute-start.31
  78.3 1.3 accumulate_6.1
  79.6 1.2 collective-permute-done.24.urgent_ref.refs_1_
  80.8 1.9 %solve_7.1 = (bf16[2,128,512]{2,1,0:T(8,128)(2,1)}, bf16[2,128,512]{2,1,0:T(8,128)(2,1)S(1)}, bf16[2,128,512]{2,1,0:T(8,128)(2,1)}) custom-call(s32[1]{0:T(128)} %bitcast.place_ref, bf16[2,128,512]{2,1,0:T(8,128)(2,1)S(1)} %get-tuple-element.55.rhs_ref, f32[2,128,512]{2,1,0:T(8,128)S(1)} %get-tuple-element.93.acc_ref.refs_11_, ...), custom_call_target="tpu_custom_call" | custom-call | tf_op jit(solution)/shard_map/solve_7/pallas_call | solution.py:183
  84.1 9.7 %collective-permute-done.29.refs_6_ = bf16[2,128,512]{2,1,0:T(8,128)(2,1)S(1)} collective-permute-done((bf16[2,128,512]{2,1,0:T(8,128)(2,1)}, bf16[2,128,512]{2,1,0:T(8,128)(2,1)S(1)}, u32[]{:S(2)}, u32[]{:S(2)}) %collective-permute-start.29) | collective-permute-done | bytes 262176 | tf_op jit(solution)/shard_map/ppermute | solution.py:330
  94.5 1.4 collective-permute-start.33
  95.9 6.7 %collective-permute-done.31.refs_4_ = bf16[2,128,512]{2,1,0:T(8,128)(2,1)S(1)} collective-permute-done((bf16[2,128,512]{2,1,0:T(8,128)(2,1)}, bf16[2,128,512]{2,1,0:T(8,128)(2,1)S(1)}, u32[]{:S(2)}, u32[]{:S(2)}) %collective-permute-start.31) | collective-permute-done | bytes 262176 | tf_op jit(solution)/shard_map/ppermute | solution.py:330
  102.6 1.4 collective-permute-start.34
  103.9 0.9 fusion.9
  104.8 7.1 %collective-permute-start.28 = (bf16[2,128,512]{2,1,0:T(8,128)(2,1)}, bf16[2,128,512]{2,1,0:T(8,128)(2,1)}, u32[]{:S(2)}, u32[]{:S(2)}) collective-permute-start(bf16[2,128,512]{2,1,0:T(8,128)(2,1)} %get-tuple-element.109), channel_id=1, source_target_pairs={{0,1},{1,0},{2,3},{3,2},{4,5},{5,4},{6,7},{7,6},{8,9},{9,8},{10,11... | collective-permute-start | bytes 786440 | tf_op jit(solution)/shard_map/ppermute | solution.py:330
  111.9 0.9 fusion.10
  112.9 0.9 copy-done.2
  113.9 4.3 %accumulate_7.1 = (f32[2,128,512]{2,1,0:T(8,128)S(1)}, f32[2,128,512]{2,1,0:T(8,128)S(1)}) custom-call(s32[1]{0:T(128)} %bitcast.place_ref, bf16[2,128,512]{2,1,0:T(8,128)(2,1)S(1)} %get-tuple-element.96.refs_0_, bf16[2,128,512]{2,1,0:T(8,128)(2,1)S(1)} %copy-done.2, ...), custom_call_target="tpu_custom_call", output_to_operand_aliasing={{0}: (12, {}), {1}: (13, {})} | custom-call | tf_op jit(solution)/shard_map/accumulate_7/pallas_call | solution.py:260
  118.2 3.5 %collective-permute-done.32.refs_3_ = bf16[2,128,512]{2,1,0:T(8,128)(2,1)} collective-permute-done((bf16[2,128,512]{2,1,0:T(8,128)(2,1)}, bf16[2,128,512]{2,1,0:T(8,128)(2,1)}, u32[]{:S(2)}, u32[]{:S(2)}) %collective-permute-start.32) | collective-permute-done | bytes 262176 | tf_op jit(solution)/shard_map/ppermute | solution.py:330
  121.7 2.7 %accumulate_late.1 = (f32[2,128,512]{2,1,0:T(8,128)S(1)}, f32[2,128,512]{2,1,0:T(8,128)S(1)}) custom-call(s32[1]{0:T(128)} %bitcast.place_ref, bf16[2,128,512]{2,1,0:T(8,128)(2,1)S(1)} %collective-permute-done.27.refs_0_, bf16[2,128,512]{2,1,0:T(8,128)(2,1)S(1)} %collective-permute-done.26.refs_1_, ...), custom_call_target="tpu_custom_call", output_to_operand_aliasing={{0}: (7, {}), {1}: (8, {})} | custom-call | tf_op jit(solution)/shard_map/accumulate_late/pallas_call | solution.py:260
  124.4 2.7 %accumulate_last.1 = (f32[2,128,512]{2,1,0:T(8,128)S(1)}, f32[2,128,512]{2,1,0:T(8,128)S(1)}) custom-call(s32[1]{0:T(128)} %bitcast.place_ref, bf16[2,128,512]{2,1,0:T(8,128)(2,1)} %collective-permute-done.28.refs_0_, bf16[1,2,512,4096]{3,2,1,0:T(8,128)(2,1)} %refs_1_.3, ...), custom_call_target="tpu_custom_call", output_to_operand_aliasing={{0}: (4, {}), {1}: (5, {})} | custom-call | tf_op jit(solution)/shard_map/accumulate_last/pallas_call | solution.py:260
  127.2 5.4 %collective-permute-start.35 = (bf16[2,128,512]{2,1,0:T(8,128)(2,1)S(1)}, bf16[2,128,512]{2,1,0:T(8,128)(2,1)S(1)}, u32[]{:S(2)}, u32[]{:S(2)}) collective-permute-start(bf16[2,128,512]{2,1,0:T(8,128)(2,1)S(1)} %fusion.6.own_ref), channel_id=1, source_target_pairs={{0,1},{1,0},{2,3},{3,2},{4,5},{5,4},{6,7},{7,6},{8,9},{9,8},{10,11... | collective-permute-start | bytes 786440 | tf_op jit(solution)/shard_map/ppermute | solution.py:330
  132.7 0.9 compare_convert_fusion
  133.6 4.3 %collective-permute-done.35.other_ref = bf16[2,128,512]{2,1,0:T(8,128)(2,1)S(1)} collective-permute-done((bf16[2,128,512]{2,1,0:T(8,128)(2,1)S(1)}, bf16[2,128,512]{2,1,0:T(8,128)(2,1)S(1)}, u32[]{:S(2)}, u32[]{:S(2)}) %collective-permute-start.35) | collective-permute-done | bytes 262176 | tf_op jit(solution)/shard_map/ppermute | solution.py:330
  137.9 1.5 place_rows.1
  139.4 6.0 %collective-permute-start.38 = (bf16[2,128,512]{2,1,0:T(8,128)(2,1)S(1)}, bf16[2,128,512]{2,1,0:T(8,128)(2,1)S(1)}, u32[]{:S(2)}, u32[]{:S(2)}) collective-permute-start(bf16[2,128,512]{2,1,0:T(8,128)(2,1)S(1)} %get-tuple-element.106), channel_id=1, source_target_pairs={{0,6},{1,7},{2,4},{3,5},{4,2},{5,3},{6,0},{7,1},{8,14},{9,15},{10,... | collective-permute-start | bytes 786440 | tf_op jit(solution)/shard_map/ppermute | solution.py:330
  146.2 6.4 %collective-permute-done.38 = bf16[2,128,512]{2,1,0:T(8,128)(2,1)S(1)} collective-permute-done((bf16[2,128,512]{2,1,0:T(8,128)(2,1)S(1)}, bf16[2,128,512]{2,1,0:T(8,128)(2,1)S(1)}, u32[]{:S(2)}, u32[]{:S(2)}) %collective-permute-start.38) | collective-permute-done | bytes 262176 | tf_op jit(solution)/shard_map/ppermute | solution.py:330
  152.6 13.1 %collective-permute-done.37 = bf16[2,128,512]{2,1,0:T(8,128)(2,1)S(1)} collective-permute-done((bf16[2,128,512]{2,1,0:T(8,128)(2,1)S(1)}, bf16[2,128,512]{2,1,0:T(8,128)(2,1)S(1)}, u32[]{:S(2)}, u32[]{:S(2)}) %collective-permute-start.37) | collective-permute-done | bytes 262176 | tf_op jit(solution)/shard_map/ppermute | solution.py:330
  166.1 0.7 copy.49
  166.8 0.8 collective-permute-done.39
  167.7 1.2 fusion.8
  (77 shorter events, 15.7 us)
Async XLA Ops:
  0.6 1.2 copy-start.3
  1.9 0.9 copy-start.4
  4.7 11.2 %collective-permute-start = (bf16[2,128,512]{2,1,0:T(8,128)(2,1)S(1)}, bf16[2,128,512]{2,1,0:T(8,128)(2,1)S(1)}, u32[]{:S(2)}, u32[]{:S(2)}) collective-permute-start(bf16[2,128,512]{2,1,0:T(8,128)(2,1)S(1)} %get-tuple-element.64), channel_id=1, source_target_pairs={{0,1},{1,0},{2,3},{3,2},{4,5},{5,4},{6,7},{7,6},{8,9},{9,8},{10,11... | collective-permute-start | bytes 786440 | tf_op jit(solution)/shard_map/ppermute | solution.py:330
  7.3 10.2 %collective-permute-start.1 = (bf16[2,128,512]{2,1,0:T(8,128)(2,1)S(1)}, bf16[2,128,512]{2,1,0:T(8,128)(2,1)S(1)}, u32[]{:S(2)}, u32[]{:S(2)}) collective-permute-start(bf16[2,128,512]{2,1,0:T(8,128)(2,1)S(1)} %get-tuple-element.61.refs_0_.mine_in), channel_id=1, source_target_pairs={{0,2},{8,10},{16,18},{24,26}} | collective-permute-start | bytes 786440 | tf_op jit(solution)/shard_map/ppermute | solution.py:330
  10.8 12.3 %collective-permute-start.3 = (bf16[2,128,512]{2,1,0:T(8,128)(2,1)S(1)}, bf16[2,128,512]{2,1,0:T(8,128)(2,1)S(1)}, u32[]{:S(2)}, u32[]{:S(2)}) collective-permute-start(bf16[2,128,512]{2,1,0:T(8,128)(2,1)S(1)} %get-tuple-element.61.refs_0_.mine_in), channel_id=1, source_target_pairs={{0,4},{8,12},{16,20},{24,28}} | collective-permute-start | bytes 786440 | tf_op jit(solution)/shard_map/ppermute | solution.py:330
  12.5 14.8 %collective-permute-start.4 = (bf16[2,128,512]{2,1,0:T(8,128)(2,1)S(1)}, bf16[2,128,512]{2,1,0:T(8,128)(2,1)S(1)}, u32[]{:S(2)}, u32[]{:S(2)}) collective-permute-start(bf16[2,128,512]{2,1,0:T(8,128)(2,1)S(1)} %get-tuple-element.61.refs_0_.mine_in), channel_id=1, source_target_pairs={{0,6},{8,14},{16,22},{24,30}} | collective-permute-start | bytes 786440 | tf_op jit(solution)/shard_map/ppermute | solution.py:330
  16.0 11.3 %collective-permute-start.2 = (bf16[2,128,512]{2,1,0:T(8,128)(2,1)S(1)}, bf16[2,128,512]{2,1,0:T(8,128)(2,1)S(1)}, u32[]{:S(2)}, u32[]{:S(2)}) collective-permute-start(bf16[2,128,512]{2,1,0:T(8,128)(2,1)S(1)} %get-tuple-element.69), channel_id=1, source_target_pairs={{1,2},{9,10},{17,18},{25,26}} | collective-permute-start | bytes 786440 | tf_op jit(solution)/shard_map/ppermute | solution.py:330
  16.7 12.2 %collective-permute-start.5 = (bf16[2,128,512]{2,1,0:T(8,128)(2,1)S(1)}, bf16[2,128,512]{2,1,0:T(8,128)(2,1)S(1)}, u32[]{:S(2)}, u32[]{:S(2)}) collective-permute-start(bf16[2,128,512]{2,1,0:T(8,128)(2,1)S(1)} %get-tuple-element.70.before_in), channel_id=1, source_target_pairs={{1,3},{9,11},{17,19},{25,27}} | collective-permute-start | bytes 786440 | tf_op jit(solution)/shard_map/ppermute | solution.py:330
  17.5 12.0 %collective-permute-start.6 = (bf16[2,128,512]{2,1,0:T(8,128)(2,1)S(1)}, bf16[2,128,512]{2,1,0:T(8,128)(2,1)S(1)}, u32[]{:S(2)}, u32[]{:S(2)}) collective-permute-start(bf16[2,128,512]{2,1,0:T(8,128)(2,1)S(1)} %get-tuple-element.66.refs_0_.mine_in), channel_id=1, source_target_pairs={{1,3},{9,11},{17,19},{25,27}} | collective-permute-start | bytes 786440 | tf_op jit(solution)/shard_map/ppermute | solution.py:330
  27.4 6.9 %collective-permute-start.7 = (bf16[2,128,512]{2,1,0:T(8,128)(2,1)S(1)}, bf16[2,128,512]{2,1,0:T(8,128)(2,1)S(1)}, u32[]{:S(2)}, u32[]{:S(2)}) collective-permute-start(bf16[2,128,512]{2,1,0:T(8,128)(2,1)S(1)} %get-tuple-element.74), channel_id=1, source_target_pairs={{0,1},{1,0},{2,3},{3,2},{4,5},{5,4},{6,7},{7,6},{8,9},{9,8},{10,11... | collective-permute-start | bytes 786440 | tf_op jit(solution)/shard_map/ppermute | solution.py:330
  27.5 7.5 %collective-permute-start.8 = (bf16[2,128,512]{2,1,0:T(8,128)(2,1)S(1)}, bf16[2,128,512]{2,1,0:T(8,128)(2,1)S(1)}, u32[]{:S(2)}, u32[]{:S(2)}) collective-permute-start(bf16[2,128,512]{2,1,0:T(8,128)(2,1)S(1)} %get-tuple-element.75.before_in), channel_id=1, source_target_pairs={{2,4},{10,12},{18,20},{26,28}} | collective-permute-start | bytes 786440 | tf_op jit(solution)/shard_map/ppermute | solution.py:330
  28.2 7.6 %collective-permute-start.9 = (bf16[2,128,512]{2,1,0:T(8,128)(2,1)S(1)}, bf16[2,128,512]{2,1,0:T(8,128)(2,1)S(1)}, u32[]{:S(2)}, u32[]{:S(2)}) collective-permute-start(bf16[2,128,512]{2,1,0:T(8,128)(2,1)S(1)} %get-tuple-element.71.refs_0_.mine_in), channel_id=1, source_target_pairs={{2,4},{10,12},{18,20},{26,28}} | collective-permute-start | bytes 786440 | tf_op jit(solution)/shard_map/ppermute | solution.py:330
  28.9 9.4 %collective-permute-start.11 = (bf16[2,128,512]{2,1,0:T(8,128)(2,1)S(1)}, bf16[2,128,512]{2,1,0:T(8,128)(2,1)S(1)}, u32[]{:S(2)}, u32[]{:S(2)}) collective-permute-start(bf16[2,128,512]{2,1,0:T(8,128)(2,1)S(1)} %get-tuple-element.71.refs_0_.mine_in), channel_id=1, source_target_pairs={{2,6},{10,14},{18,22},{26,30}} | collective-permute-start | bytes 786440 | tf_op jit(solution)/shard_map/ppermute | solution.py:330
  29.6 9.4 %collective-permute-start.12 = (bf16[2,128,512]{2,1,0:T(8,128)(2,1)S(1)}, bf16[2,128,512]{2,1,0:T(8,128)(2,1)S(1)}, u32[]{:S(2)}, u32[]{:S(2)}) collective-permute-start(bf16[2,128,512]{2,1,0:T(8,128)(2,1)S(1)} %get-tuple-element.71.refs_0_.mine_in), channel_id=1, source_target_pairs={{1,7},{9,15},{17,23},{25,31}} | collective-permute-start | bytes 786440 | tf_op jit(solution)/shard_map/ppermute | solution.py:330
  34.4 4.6 %collective-permute-start.10 = (bf16[2,128,512]{2,1,0:T(8,128)(2,1)S(1)}, bf16[2,128,512]{2,1,0:T(8,128)(2,1)S(1)}, u32[]{:S(2)}, u32[]{:S(2)}) collective-permute-start(bf16[2,128,512]{2,1,0:T(8,128)(2,1)S(1)} %get-tuple-element.79), channel_id=1, source_target_pairs={{3,4},{11,12},{19,20},{27,28}} | collective-permute-start | bytes 786440 | tf_op jit(solution)/shard_map/ppermute | solution.py:330
  35.1 10.4 %collective-permute-start.13 = (bf16[2,128,512]{2,1,0:T(8,128)(2,1)S(1)}, bf16[2,128,512]{2,1,0:T(8,128)(2,1)S(1)}, u32[]{:S(2)}, u32[]{:S(2)}) collective-permute-start(bf16[2,128,512]{2,1,0:T(8,128)(2,1)S(1)} %get-tuple-element.66.refs_0_.mine_in), channel_id=1, source_target_pairs={{1,5},{9,13},{17,21},{25,29}} | collective-permute-start | bytes 786440 | tf_op jit(solution)/shard_map/ppermute | solution.py:330
  35.8 11.7 %collective-permute-start.15 = (bf16[2,128,512]{2,1,0:T(8,128)(2,1)S(1)}, bf16[2,128,512]{2,1,0:T(8,128)(2,1)S(1)}, u32[]{:S(2)}, u32[]{:S(2)}) collective-permute-start(bf16[2,128,512]{2,1,0:T(8,128)(2,1)S(1)} %get-tuple-element.76.refs_0_.mine_in), channel_id=1, source_target_pairs={{3,5},{11,13},{19,21},{27,29}} | collective-permute-start | bytes 786440 | tf_op jit(solution)/shard_map/ppermute | solution.py:330
  38.3 7.9 %collective-permute-start.14 = (bf16[2,128,512]{2,1,0:T(8,128)(2,1)S(1)}, bf16[2,128,512]{2,1,0:T(8,128)(2,1)S(1)}, u32[]{:S(2)}, u32[]{:S(2)}) collective-permute-start(bf16[2,128,512]{2,1,0:T(8,128)(2,1)S(1)} %get-tuple-element.80.before_in), channel_id=1, source_target_pairs={{3,5},{11,13},{19,21},{27,29}} | collective-permute-start | bytes 786440 | tf_op jit(solution)/shard_map/ppermute | solution.py:330
  39.1 10.1 %collective-permute-start.16 = (bf16[2,128,512]{2,1,0:T(8,128)(2,1)S(1)}, bf16[2,128,512]{2,1,0:T(8,128)(2,1)S(1)}, u32[]{:S(2)}, u32[]{:S(2)}) collective-permute-start(bf16[2,128,512]{2,1,0:T(8,128)(2,1)S(1)} %get-tuple-element.84), channel_id=1, source_target_pairs={{0,1},{1,0},{2,3},{3,2},{4,5},{5,4},{6,7},{7,6},{8,9},{9,8},{10,11... | collective-permute-start | bytes 786440 | tf_op jit(solution)/shard_map/ppermute | solution.py:330
  44.8 5.1 %collective-permute-start.17 = (bf16[2,128,512]{2,1,0:T(8,128)(2,1)S(1)}, bf16[2,128,512]{2,1,0:T(8,128)(2,1)S(1)}, u32[]{:S(2)}, u32[]{:S(2)}) collective-permute-start(bf16[2,128,512]{2,1,0:T(8,128)(2,1)S(1)} %get-tuple-element.85.before_in), channel_id=1, source_target_pairs={{4,6},{12,14},{20,22},{28,30}} | collective-permute-start | bytes 786440 | tf_op jit(solution)/shard_map/ppermute | solution.py:330
  45.5 5.1 %collective-permute-start.18 = (bf16[2,128,512]{2,1,0:T(8,128)(2,1)S(1)}, bf16[2,128,512]{2,1,0:T(8,128)(2,1)S(1)}, u32[]{:S(2)}, u32[]{:S(2)}) collective-permute-start(bf16[2,128,512]{2,1,0:T(8,128)(2,1)S(1)} %get-tuple-element.81.refs_0_.mine_in), channel_id=1, source_target_pairs={{4,6},{3,7},{12,14},{11,15},{20,22},{19,23},{28,30},{27,31}} | collective-permute-start | bytes 786440 | tf_op jit(solution)/shard_map/ppermute | solution.py:330
  46.2 17.4 %collective-permute-start.20 = (bf16[2,128,512]{2,1,0:T(8,128)(2,1)S(1)}, bf16[2,128,512]{2,1,0:T(8,128)(2,1)S(1)}, u32[]{:S(2)}, u32[]{:S(2)}) collective-permute-start(bf16[2,128,512]{2,1,0:T(8,128)(2,1)S(1)} %get-tuple-element.81.refs_0_.mine_in), channel_id=1, source_target_pairs={{2,0},{10,8},{18,16},{26,24}} | collective-permute-start | bytes 786440 | tf_op jit(solution)/shard_map/ppermute | solution.py:330
  47.5 16.1 %collective-permute-start.21 = (bf16[2,128,512]{2,1,0:T(8,128)(2,1)S(1)}, bf16[2,128,512]{2,1,0:T(8,128)(2,1)S(1)}, u32[]{:S(2)}, u32[]{:S(2)}) collective-permute-start(bf16[2,128,512]{2,1,0:T(8,128)(2,1)S(1)} %get-tuple-element.81.refs_0_.mine_in), channel_id=1, source_target_pairs={{3,1},{11,9},{19,17},{27,25}} | collective-permute-start | bytes 786440 | tf_op jit(solution)/shard_map/ppermute | solution.py:330
  49.2 14.3 %collective-permute-start.19 = (bf16[2,128,512]{2,1,0:T(8,128)(2,1)S(1)}, bf16[2,128,512]{2,1,0:T(8,128)(2,1)S(1)}, u32[]{:S(2)}, u32[]{:S(2)}) collective-permute-start(bf16[2,128,512]{2,1,0:T(8,128)(2,1)S(1)} %get-tuple-element.89), channel_id=1, source_target_pairs={{5,6},{13,14},{21,22},{29,30}} | collective-permute-start | bytes 786440 | tf_op jit(solution)/shard_map/ppermute | solution.py:330
  49.9 27.1 %collective-permute-start.22 = (bf16[2,128,512]{2,1,0:T(8,128)(2,1)S(1)}, bf16[2,128,512]{2,1,0:T(8,128)(2,1)S(1)}, u32[]{:S(2)}, u32[]{:S(2)}) collective-permute-start(bf16[2,128,512]{2,1,0:T(8,128)(2,1)S(1)} %get-tuple-element.90.before_in), channel_id=1, source_target_pairs={{5,7},{13,15},{21,23},{29,31}} | collective-permute-start | bytes 786440 | tf_op jit(solution)/shard_map/ppermute | solution.py:330
  50.6 27.7 %collective-permute-start.23 = (bf16[2,128,512]{2,1,0:T(8,128)(2,1)S(1)}, bf16[2,128,512]{2,1,0:T(8,128)(2,1)S(1)}, u32[]{:S(2)}, u32[]{:S(2)}) collective-permute-start(bf16[2,128,512]{2,1,0:T(8,128)(2,1)S(1)} %get-tuple-element.86.refs_0_.mine_in), channel_id=1, source_target_pairs={{5,7},{4,2},{13,15},{12,10},{21,23},{20,18},{29,31},{28,26}} | collective-permute-start | bytes 786440 | tf_op jit(solution)/shard_map/ppermute | solution.py:330
  64.3 16.5 %copy-start.5 = (bf16[2,128,512]{2,1,0:T(8,128)(2,1)}, bf16[2,128,512]{2,1,0:T(8,128)(2,1)S(1)}, u32[]{:S(2)}) copy-start(bf16[2,128,512]{2,1,0:T(8,128)(2,1)S(1)} %get-tuple-element.95.before_in) | copy-start | bytes 786436
  64.3 16.5 %collective-permute-start.24 = (bf16[2,128,512]{2,1,0:T(8,128)(2,1)S(1)}, bf16[2,128,512]{2,1,0:T(8,128)(2,1)S(1)}, u32[]{:S(2)}, u32[]{:S(2)}) collective-permute-start(bf16[2,128,512]{2,1,0:T(8,128)(2,1)S(1)} %get-tuple-element.94), channel_id=1, source_target_pairs={{0,1},{1,0},{2,3},{3,2},{4,5},{5,4},{6,7},{7,6},{8,9},{9,8},{10,11... | collective-permute-start | bytes 786440 | tf_op jit(solution)/shard_map/ppermute | solution.py:330
  75.0 18.8 %collective-permute-start.29 = (bf16[2,128,512]{2,1,0:T(8,128)(2,1)}, bf16[2,128,512]{2,1,0:T(8,128)(2,1)S(1)}, u32[]{:S(2)}, u32[]{:S(2)}) collective-permute-start(bf16[2,128,512]{2,1,0:T(8,128)(2,1)} %get-tuple-element.91.refs_0_.mine_in), channel_id=1, source_target_pairs={{6,0},{14,8},{22,16},{30,24}} | collective-permute-start | bytes 786440 | tf_op jit(solution)/shard_map/ppermute | solution.py:330
  76.3 18.2 %collective-permute-start.30 = (bf16[2,128,512]{2,1,0:T(8,128)(2,1)}, bf16[2,128,512]{2,1,0:T(8,128)(2,1)S(1)}, u32[]{:S(2)}, u32[]{:S(2)}) collective-permute-start(bf16[2,128,512]{2,1,0:T(8,128)(2,1)} %get-tuple-element.91.refs_0_.mine_in), channel_id=1, source_target_pairs={{6,2},{5,1},{14,10},{13,9},{22,18},{21,17},{30,26},{29,25}} | collective-permute-start | bytes 786440 | tf_op jit(solution)/shard_map/ppermute | solution.py:330
  77.0 25.6 %collective-permute-start.31 = (bf16[2,128,512]{2,1,0:T(8,128)(2,1)}, bf16[2,128,512]{2,1,0:T(8,128)(2,1)S(1)}, u32[]{:S(2)}, u32[]{:S(2)}) collective-permute-start(bf16[2,128,512]{2,1,0:T(8,128)(2,1)} %get-tuple-element.91.refs_0_.mine_in), channel_id=1, source_target_pairs={{6,4},{5,3},{4,0},{14,12},{13,11},{12,8},{22,20},{21,19},{20,16},{... | collective-permute-start | bytes 786440 | tf_op jit(solution)/shard_map/ppermute | solution.py:330
  78.3 1.3 copy-start
  80.8 13.0 %copy-start.1 = (bf16[2,128,512]{2,1,0:T(8,128)(2,1)}, bf16[2,128,512]{2,1,0:T(8,128)(2,1)S(1)}, u32[]{:S(2)}) copy-start(bf16[2,128,512]{2,1,0:T(8,128)(2,1)S(1)} %collective-permute-done.24.urgent_ref.refs_1_) | copy-start | bytes 786436
  82.7 21.2 %collective-permute-start.25 = (bf16[2,128,512]{2,1,0:T(8,128)(2,1)S(1)}, bf16[2,128,512]{2,1,0:T(8,128)(2,1)S(1)}, u32[]{:S(2)}, u32[]{:S(2)}) collective-permute-start(bf16[2,128,512]{2,1,0:T(8,128)(2,1)S(1)} %get-tuple-element.96.refs_0_), channel_id=1, source_target_pairs={{7,1},{15,9},{23,17},{31,25}} | collective-permute-start | bytes 786440 | tf_op jit(solution)/shard_map/ppermute | solution.py:330
  83.4 20.5 %collective-permute-start.26 = (bf16[2,128,512]{2,1,0:T(8,128)(2,1)S(1)}, bf16[2,128,512]{2,1,0:T(8,128)(2,1)S(1)}, u32[]{:S(2)}, u32[]{:S(2)}) collective-permute-start(bf16[2,128,512]{2,1,0:T(8,128)(2,1)S(1)} %get-tuple-element.96.refs_0_), channel_id=1, source_target_pairs={{7,3},{15,11},{23,19},{31,27}} | collective-permute-start | bytes 786440 | tf_op jit(solution)/shard_map/ppermute | solution.py:330
  93.8 10.1 %collective-permute-start.27 = (bf16[2,128,512]{2,1,0:T(8,128)(2,1)S(1)}, bf16[2,128,512]{2,1,0:T(8,128)(2,1)S(1)}, u32[]{:S(2)}, u32[]{:S(2)}) collective-permute-start(bf16[2,128,512]{2,1,0:T(8,128)(2,1)S(1)} %get-tuple-element.96.refs_0_), channel_id=1, source_target_pairs={{7,5},{15,13},{23,21},{31,29}} | collective-permute-start | bytes 786440 | tf_op jit(solution)/shard_map/ppermute | solution.py:330
  94.5 18.4 %collective-permute-start.33 = (bf16[2,128,512]{2,1,0:T(8,128)(2,1)}, bf16[2,128,512]{2,1,0:T(8,128)(2,1)}, u32[]{:S(2)}, u32[]{:S(2)}) collective-permute-start(bf16[2,128,512]{2,1,0:T(8,128)(2,1)} %copy-done.5), channel_id=1, source_target_pairs={{5,3},{13,11},{21,19},{29,27}} | collective-permute-start | bytes 786440 | tf_op jit(solution)/shard_map/ppermute | solution.py:330
  102.6 10.4 %collective-permute-start.34 = (bf16[2,128,512]{2,1,0:T(8,128)(2,1)}, bf16[2,128,512]{2,1,0:T(8,128)(2,1)}, u32[]{:S(2)}, u32[]{:S(2)}) collective-permute-start(bf16[2,128,512]{2,1,0:T(8,128)(2,1)} %copy-done.5), channel_id=1, source_target_pairs={{5,1},{13,9},{21,17},{29,25}} | collective-permute-start | bytes 786440 | tf_op jit(solution)/shard_map/ppermute | solution.py:330
  104.8 19.6 %collective-permute-start.28 = (bf16[2,128,512]{2,1,0:T(8,128)(2,1)}, bf16[2,128,512]{2,1,0:T(8,128)(2,1)}, u32[]{:S(2)}, u32[]{:S(2)}) collective-permute-start(bf16[2,128,512]{2,1,0:T(8,128)(2,1)} %get-tuple-element.109), channel_id=1, source_target_pairs={{0,1},{1,0},{2,3},{3,2},{4,5},{5,4},{6,7},{7,6},{8,9},{9,8},{10,11... | collective-permute-start | bytes 786440 | tf_op jit(solution)/shard_map/ppermute | solution.py:330
  111.9 9.8 %collective-permute-start.32 = (bf16[2,128,512]{2,1,0:T(8,128)(2,1)}, bf16[2,128,512]{2,1,0:T(8,128)(2,1)}, u32[]{:S(2)}, u32[]{:S(2)}) collective-permute-start(bf16[2,128,512]{2,1,0:T(8,128)(2,1)} %get-tuple-element.108), channel_id=1, source_target_pairs={{0,1},{1,0},{2,3},{3,2},{4,5},{5,4},{6,7},{7,6},{8,9},{9,8},{10,11... | collective-permute-start | bytes 786440 | tf_op jit(solution)/shard_map/ppermute | solution.py:330
  112.9 1.0 copy-start.2
  124.4 2.7 %copy-start.7 = (bf16[1,2,128,512]{3,2,1,0:T(8,128)(2,1)S(1)}, bf16[1,2,128,512]{3,2,1,0:T(8,128)(2,1)}, u32[]{:S(2)}) copy-start(bf16[1,2,128,512]{3,2,1,0:T(8,128)(2,1)} %param.11) | copy-start | bytes 786436
  127.2 10.7 %collective-permute-start.35 = (bf16[2,128,512]{2,1,0:T(8,128)(2,1)S(1)}, bf16[2,128,512]{2,1,0:T(8,128)(2,1)S(1)}, u32[]{:S(2)}, u32[]{:S(2)}) collective-permute-start(bf16[2,128,512]{2,1,0:T(8,128)(2,1)S(1)} %fusion.6.own_ref), channel_id=1, source_target_pairs={{0,1},{1,0},{2,3},{3,2},{4,5},{5,4},{6,7},{7,6},{8,9},{9,8},{10,11... | collective-permute-start | bytes 786440 | tf_op jit(solution)/shard_map/ppermute | solution.py:330
  137.9 29.8 %copy-start.6 = (f32[1,2,128,512]{3,2,1,0:T(8,128)S(1)}, f32[1,2,128,512]{3,2,1,0:T(8,128)}, u32[]{:S(2)}) copy-start(f32[1,2,128,512]{3,2,1,0:T(8,128)} %param.13) | copy-start | bytes 1572868
  139.4 13.2 %collective-permute-start.38 = (bf16[2,128,512]{2,1,0:T(8,128)(2,1)S(1)}, bf16[2,128,512]{2,1,0:T(8,128)(2,1)S(1)}, u32[]{:S(2)}, u32[]{:S(2)}) collective-permute-start(bf16[2,128,512]{2,1,0:T(8,128)(2,1)S(1)} %get-tuple-element.106), channel_id=1, source_target_pairs={{0,6},{1,7},{2,4},{3,5},{4,2},{5,3},{6,0},{7,1},{8,14},{9,15},{10,... | collective-permute-start | bytes 786440 | tf_op jit(solution)/shard_map/ppermute | solution.py:330
  145.4 20.3 %collective-permute-start.37 = (bf16[2,128,512]{2,1,0:T(8,128)(2,1)S(1)}, bf16[2,128,512]{2,1,0:T(8,128)(2,1)S(1)}, u32[]{:S(2)}, u32[]{:S(2)}) collective-permute-start(bf16[2,128,512]{2,1,0:T(8,128)(2,1)S(1)} %get-tuple-element.105), channel_id=1, source_target_pairs={{0,4},{1,5},{2,6},{3,7},{4,0},{5,1},{6,2},{7,3},{8,12},{9,13},{10,... | collective-permute-start | bytes 786440 | tf_op jit(solution)/shard_map/ppermute | solution.py:330
  145.8 20.0 %collective-permute-start.36 = (bf16[2,128,512]{2,1,0:T(8,128)(2,1)S(1)}, bf16[2,128,512]{2,1,0:T(8,128)(2,1)S(1)}, u32[]{:S(2)}, u32[]{:S(2)}) collective-permute-start(bf16[2,128,512]{2,1,0:T(8,128)(2,1)S(1)} %get-tuple-element.104), channel_id=1, source_target_pairs={{0,2},{1,3},{2,0},{3,1},{4,6},{5,7},{6,4},{7,5},{8,10},{9,11},{10,... | collective-permute-start | bytes 786440 | tf_op jit(solution)/shard_map/ppermute | solution.py:330
  166.1 1.6 collective-permute-start.39

commit v3 on v2

--- a/solution.py
+++ b/solution.py
@@ -14,22 +14,28 @@
 
 SWAP = ((0, 1), (1, 0), (2, 3), (3, 2), (4, 5), (5, 4), (6, 7), (7, 6))
 CHAIN = (SWAP, ((1, 2),), SWAP, ((3, 4),), SWAP, ((5, 6),), SWAP)
-RELAY = {2: {4: (0, 1), 6: (0, 2)}, 4: {6: (2, 2), 7: (2, 3)}, 6: {0: (4, 3), 1: (4, 2)}}
+RELAY = {
+    2: {4: (0, 1), 6: (0, 2)},
+    4: {6: (2, 2), 7: (1, 3)},
+    6: {0: (4, 4), 2: (4, 3)},
+}
+OWN, PREV = "own", "prev"
 SPREAD = (
-    ((True, ((0, 2),), 1), (True, ((0, 4),), 3), (True, ((0, 6),), 5)),
-    ((False, ((1, 3),), 2), (True, ((1, 3),), 2), (True, ((1, 5),), 4)),
-    ((False, ((2, 4),), 3), (True, ((2, 4),), 3), (True, ((2, 6),), 5), (True, ((1, 7),), 6)),
-    ((False, ((3, 5),), 4), (True, ((3, 5),), 4)),
-    ((False, ((4, 6),), 5), (True, ((4, 6), (3, 7)), 5), (True, ((3, 1),), 7), (True, ((2, 0),), 7)),
-    ((False, ((5, 7),), 6), (True, ((5, 7), (4, 2)), 6)),
+    ((OWN, ((0, 2),)), (OWN, ((0, 4),)), (OWN, ((0, 6),))),
+    ((OWN, ((1, 3),)), ((0, 0), ((2, 3),)), (OWN, ((1, 5),)), (OWN, ((1, 7),))),
+    ((PREV, ((2, 4),)), (OWN, ((2, 4),)), (OWN, ((2, 6),))),
+    ((OWN, ((3, 5),)), ((2, 1), ((4, 5),))),
     (
-        (True, ((6, 4), (5, 3), (4, 0)), 7),
-        (True, ((6, 2), (5, 1)), 7),
-        (True, ((6, 0),), 7),
-        (False, ((5, 3),), 7),
-        (False, ((5, 1),), 7),
+        (PREV, ((4, 6),)),
+        (OWN, ((4, 6),)),
+        (OWN, ((2, 0), (3, 1))),
+        (OWN, ((4, 2),)),
+        (OWN, ((4, 0),)),
+        ((3, 0), ((5, 7),)),
     ),
-    ((True, ((7, 5),), 8), (True, ((7, 3),), 8), (True, ((7, 1),), 8)),
+    ((OWN, ((5, 7),)), ((4, 1), ((6, 7),)), ((4, 2), ((0, 1), (1, 0)))),
+    ((OWN, ((6, 4), (5, 3))), (OWN, ((6, 2), (5, 1))), (OWN, ((6, 0),))),
+    ((OWN, ((7, 5),)), (OWN, ((7, 3),)), (OWN, ((7, 1),))),
 )
 
 
@@ -66,8 +72,13 @@
             keep(row)
             chain.append(row)
         rows = []
-        for own, edges, _ in SPREAD[hop]:
-            row = taken(edges, lambda source, own=own: source if own else source - 1)
+        for value, edges in SPREAD[hop]:
+            if value == OWN:
+                row = taken(edges, lambda source: source)
+            elif value == PREV:
+                row = taken(edges, lambda source: source - 1)
+            else:
+                row = taken(edges, lambda source, value=value: spread[value[0]][value[1]][source])
             assert sum(block >= 0 for block in row) == len(edges)
             keep(row)
             rows.append(row)
@@ -80,8 +91,8 @@
     assert all(held == set(range(count)) for held in have)
     for p in range(count):
         for hop, rows in enumerate(spread):
-            for (_, _, use), row in zip(SPREAD[hop], rows):
-                assert use > hop and (row[p] < 0 or row[p] > p or use < p)
+            for row in rows:
+                assert row[p] < 0 or row[p] > p or hop + 1 < p
         for hop, row in enumerate(chain):
             assert row[p] < 0 or row[p] > p or hop + 1 < p or (hop + 1 == p and row[p] == hop)
     return spread, chain, swaps
@@ -145,7 +156,8 @@
     )(place, lower, inverse, pivot)
 
 
-def solve_kernel(hop, relays, place_ref, rhs_ref, acc_ref, near_ref, inv_ref, urgent_ref, mine_in, before_in, *refs):
+def solve_kernel(hop, relays, place_ref, settled_ref, rhs_ref, acc_ref, near_ref, inv_ref, urgent_ref, mine_in, before_in, *refs):
+    del settled_ref
     relay_refs, (out_ref, mine_ref, before_ref) = refs[: len(relays)], refs[len(relays) :]
     place = place_ref[0]
     shots = out_ref.shape[1]
@@ -175,7 +187,7 @@
         before_ref[...] = urgent_ref[...]
 
 
-def solve(hop, place, rhs, acc, near, inv, urgent, mine, before, relays):
+def solve(hop, place, settled, rhs, acc, near, inv, urgent, mine, before, relays):
     vmem = pl.BlockSpec(memory_space=pltpu.VMEM)
     smem = pl.BlockSpec(memory_space=pltpu.SMEM)
     block = pltpu.VMEM(mine.shape, BF16)
@@ -183,94 +195,91 @@
     return pl.pallas_call(
         functools.partial(solve_kernel, hop, tuple(relays)),
         out_shape=(block,) * 3,
-        in_specs=[smem] + [vmem] * len(args),
+        in_specs=[smem, pl.BlockSpec(memory_space=pl.ANY)] + [vmem] * len(args),
         out_specs=(vmem,) * 3,
         compiler_params=pltpu.CompilerParams(vmem_limit_bytes=16 * 2**20),
         name=f"solve_{hop}",
-    )(place, *args)
+    )(place, settled, *args)
 
 
 def gather_kernel(arrivals, left, place_ref, *refs):
-    count = len(left)
+    count = len(arrivals)
     parts = refs[:count]
-    lower_ref, update_ref, acc_l_in, acc_u_in, acc_l_ref, acc_u_ref, buf_l, buf_u, sems = refs[count:]
-    width = buf_l.shape[-1]
-    shots = acc_l_ref.shape[1]
+    panel_ref, acc_in, acc_ref, buf, sems = refs[count:]
+    width = buf.shape[-1]
+    shots = acc_ref.shape[1]
     place = place_ref[0]
     blocks = []
     for row in arrivals:
         block = jnp.int32(-1)
         for p, value in enumerate(row):
-            if value >= 0:
+            if value >= 0 and (value < p or not left):
                 block = jnp.where(place == p, value, block)
         blocks.append(block)
 
-    def copy_of(i, panel_ref, buf, which):
-        block = jnp.maximum(blocks[i], 0)
-        columns = pl.ds(pl.multiple_of(block * width, width), width)
-        return pltpu.make_async_copy(panel_ref.at[0, :, :, columns], buf.at[i], sems.at[i, which])
-
-    def when_update(i):
-        return blocks[i] >= 0
-
-    def when_lower(i):
-        return jnp.logical_and(blocks[i] >= 0, blocks[i] < place)
+    def copy_of(i):
+        columns = pl.ds(pl.multiple_of(jnp.maximum(blocks[i], 0) * width, width), width)
+        return pltpu.make_async_copy(panel_ref.at[0, :, :, columns], buf.at[i], sems.at[i])
 
     for i in range(count):
-        if left[i]:
-
-            @pl.when(when_lower(i))
-            def _(i=i):
-                copy_of(i, lower_ref, buf_l, 0).start()
-
-        @pl.when(when_update(i))
+
+        @pl.when(blocks[i] >= 0)
         def _(i=i):
-            copy_of(i, update_ref, buf_u, 1).start()
-
-    acc_l_ref[...] = acc_l_in[...]
-    acc_u_ref[...] = acc_u_in[...]
-
-    def add(i, copy, buf, acc_ref):
-        copy.wait()
-        product = apply_rows(stacked(parts[i][...]), buf[i, 0], buf[i, 1])
-        acc_ref[0] += product[:shots]
-        acc_ref[1] += product[shots:]
-
+            copy_of(i).start()
+
+    acc_ref[...] = acc_in[...]
     for i in range(count):
-        if left[i]:
-
-            @pl.when(when_lower(i))
-            def _(i=i):
-                add(i, copy_of(i, lower_ref, buf_l, 0), buf_l, acc_l_ref)
-
-        @pl.when(when_update(i))
+
+        @pl.when(blocks[i] >= 0)
         def _(i=i):
-            add(i, copy_of(i, update_ref, buf_u, 1), buf_u, acc_u_ref)
-
-
-def accumulate(name, place, items, lower, update, acc_l, acc_u):
+            copy_of(i).wait()
+            product = apply_rows(stacked(parts[i][...]), buf[i, 0], buf[i, 1])
+            acc_ref[0] += product[:shots]
+            acc_ref[1] += product[shots:]
+
+
+def pick_kernel(places, place_ref, *refs):
+    out_ref = refs[-1]
+
+    for p, ref in zip(places, refs):
+
+        @pl.when(place_ref[0] == p)
+        def _(ref=ref):
+            out_ref[...] = ref[...]
+
+
+def pick(name, place, values, default):
+    count = lax.axis_size("panel")
+    vmem = pl.BlockSpec(memory_space=pltpu.VMEM)
+    args = [values.get(p, default) for p in range(count)]
+    return pl.pallas_call(
+        functools.partial(pick_kernel, tuple(range(count))),
+        out_shape=pltpu.VMEM(default.shape, default.dtype),
+        in_specs=[pl.BlockSpec(memory_space=pltpu.SMEM)] + [vmem] * count,
+        out_specs=vmem,
+        compiler_params=pltpu.CompilerParams(vmem_limit_bytes=16 * 2**20),
+        name=name,
+    )(place, *args)
+
+
+def accumulate(name, left, place, items, panel, acc):
+    items = [item for item in items if not left or any(0 <= block < p for p, block in enumerate(item[1]))]
+    if not items:
+        return acc
     parts = [item[0] for item in items]
-    arrivals = [item[1] for item in items]
-    left = [item[2] for item in items]
     count = len(parts)
     vmem = pl.BlockSpec(memory_space=pltpu.VMEM)
     hbm = pl.BlockSpec(memory_space=pltpu.HBM)
-    rows = lower.shape[2]
-    shape = pltpu.VMEM(acc_l.shape, F32)
     return pl.pallas_call(
-        functools.partial(gather_kernel, arrivals, left),
-        out_shape=(shape, shape),
-        in_specs=[pl.BlockSpec(memory_space=pltpu.SMEM)] + [vmem] * count + [hbm, hbm, vmem, vmem],
-        out_specs=(vmem, vmem),
-        scratch_shapes=[
-            pltpu.VMEM((count, 2, rows, CB), BF16),
-            pltpu.VMEM((count, 2, rows, CB), BF16),
-            pltpu.SemaphoreType.DMA((count, 2)),
-        ],
-        input_output_aliases={count + 3: 0, count + 4: 1},
+        functools.partial(gather_kernel, [item[1] for item in items], left),
+        out_shape=pltpu.VMEM(acc.shape, F32),
+        in_specs=[pl.BlockSpec(memory_space=pltpu.SMEM)] + [vmem] * count + [hbm, vmem],
+        out_specs=vmem,
+        scratch_shapes=[pltpu.VMEM((count, 2, panel.shape[2], CB), BF16), pltpu.SemaphoreType.DMA((count,))],
+        input_output_aliases={count + 2: 0} if left else {},
         compiler_params=pltpu.CompilerParams(vmem_limit_bytes=46 * 2**20),
         name=name,
-    )(place, *parts, lower, update, acc_l, acc_u)
+    )(place, *parts, panel, acc)
 
 
 def place_kernel(own_ref, other_ref, own_hot_ref, other_hot_ref, *out_refs):
@@ -334,37 +343,44 @@
     near, inv, rhs, acc_l, acc_u, mine, before = setup(place_ref, lower_panel, inverse_cols, pivot_rhs)
     urgent = mine
     came = []
+    settled = [acc_u, acc_u]
     for hop in range(count):
         relays = {p: came[earlier][i] for p, (earlier, i) in RELAY.get(hop, {}).items()}
-        passed, mine, before = solve(hop, place_ref, rhs, acc_l, near, inv, urgent, mine, before, relays)
-        parts = [(mine, [hop if p == hop else -1 for p in range(count)], False)]
+        passed, mine, before = solve(hop, place_ref, settled[hop], rhs, acc_l, near, inv, urgent, mine, before, relays)
+        parts = [(mine, [hop if p == hop else -1 for p in range(count)])]
         if hop:
-            parts.append((urgent, chain_rows[hop - 1], True))
+            parts.append((urgent, chain_rows[hop - 1]))
+            parts += zip(came[hop - 1], spread_rows[hop - 1])
         if hop < len(CHAIN):
             urgent = send(passed, CHAIN[hop])
-        came.append([send(mine if own else before, edges) for own, edges, _ in SPREAD[hop]])
-        for earlier in range(hop):
-            for i, (_, _, use) in enumerate(SPREAD[earlier]):
-                if use == hop:
-                    parts.append((came[earlier][i], spread_rows[earlier][i], True))
-        acc_l, acc_u = accumulate(f"accumulate_{hop}", place_ref, parts, lower_panel, update_panel, acc_l, acc_u)
-
-    def cross(blocks):
-        value = mine
+        came.append([])
+        for value, edges in SPREAD[hop]:
+            if value not in (OWN, PREV):
+                value = came[value[0]][value[1]]
+            else:
+                value = mine if value == OWN else before
+            came[hop].append(send(value, edges))
+        if hop + 1 < count:
+            acc_l = accumulate(f"lower_{hop}", True, place_ref, parts, lower_panel, acc_l)
+        acc_u = accumulate(f"update_{hop}", False, place_ref, parts, update_panel, acc_u)
+        settled.append(acc_u)
+
+    def cross(name, blocks):
+        values = {}
         for earlier, rows in enumerate(spread_rows):
             for i, row in enumerate(rows):
                 for p in range(count):
                     if row[p] == blocks[p % 2]:
-                        value = jnp.where(place == p, came[earlier][i], value)
-        return send(value, SWAP)
-
-    first = cross((count - 2, count - 3))
-    second = cross((None, count - 1))
-    parts = [(came[-1][i], row, False) for i, row in enumerate(spread_rows[-1])]
-    parts.append((first, swap_rows[0], False))
-    acc_l, acc_u = accumulate("accumulate_late", place_ref, parts, lower_panel, update_panel, acc_l, acc_u)
-    parts = [(second, swap_rows[1], False)]
-    acc_l, acc_u = accumulate("accumulate_last", place_ref, parts, lower_panel, update_panel, acc_l, acc_u)
+                        values[p] = came[earlier][i]
+        return send(pick(name, place_ref, values, mine), SWAP)
+
+    first = cross("pick_first", (count - 2, count - 3))
+    second = cross("pick_second", (None, count - 1))
+    parts = [(came[-1][i], row) for i, row in enumerate(spread_rows[-1])]
+    parts.append((first, swap_rows[0]))
+    acc_u = accumulate("update_late", False, place_ref, parts, update_panel, acc_u)
+    parts = [(second, swap_rows[1])]
+    acc_u = accumulate("update_last", False, place_ref, parts, update_panel, acc_u)
     child = (update_rhs[0].astype(F32) - acc_u).astype(BF16)
     other = send(child, SWAP)
     placed = place_rows(child, other, own_hot, other_hot)

time: 170 us -> 143 us (0.84)
  waiting for transfers between devices: 71 us -> 53.6 us
  starting transfers between devices: 66.1 us -> 54.7 us
    ppermute x39 -> x40, waiting for transfers between devices: 70.2 us -> 52.8 us  [send(): return lax.ppermute(value, 'panel', edges)]
    ppermute x39 -> x40, starting transfers between devices: 66.1 us -> 54.7 us  [send(): return lax.ppermute(value, 'panel', edges)]
    pallas_call x10 -> x18, Pallas kernels: 15.8 us -> 18.4 us  [the longest x16 16.8 us: accumulate(): pl.pallas_call(functools.partial(gather_kernel, [item[1] for item in item...]
    pallas_call x8, Pallas kernels: 3.42 us -> 1.69 us  [solve(): pl.pallas_call(functools.partial(solve_kernel, hop, tuple(relays)), out_s...]
  transfers between devices with their start and end apart: 40 -> 41, of which waited for: 14 -> 12; matrix products, arithmetic and copies ran while one was open for 2% -> 2% of each run, Pallas kernels for 10% -> 12%
where the time goes in v3:
time: 143 us; the launch traced here: 141 us
  starting transfers between devices  54.7 us (38%)
  waiting for transfers between devices  53.6 us (37%)
  Pallas kernels  23 us (16%)
  local copies, waits for them, and re-layouts  5.47 us (4%)
  other arithmetic  2.53 us (2%)
    ppermute x40, starting transfers between devices, send(): return lax.ppermute(value, 'panel', edges)  54.7 us
    ppermute x40, waiting for transfers between devices, send(): return lax.ppermute(value, 'panel', edges)  52.8 us
    pallas_call x16, Pallas kernels, accumulate(): pl.pallas_call(functools.partial(gather_kernel, [item[1] for item in item...  16.8 us
    unnamed x17, local copies, waits for them, and re-layouts  4.54 us
  transfers between devices with their start and end apart: 41, of which 12 were waited for; matrix products, arithmetic and copies ran while one was open for 2% of the time, Pallas kernels for 12%

profile of v3, /device:TPU:0, one launch (start us, length us, event | category | flops | bytes accessed | tf_op | source)
XLA Modules:
  0.0 140.8 jit_solution(16224216580231209558)
XLA Ops:
  0.6 1.2 copy-done
  1.9 0.9 copy-done.4
  2.8 1.4 %setup.1 = (bf16[2,512,512]{2,1,0:T(8,128)(2,1)S(1)}, bf16[2,512,512]{2,1,0:T(8,128)(2,1)S(1)}, bf16[2,128,512]{2,1,0:T(8,128)(2,1)S(1)}, f32[2,128,512]{2,1,0:T...) custom-call(s32[1]{0:T(128)} %bitcast.place_ref, ...), custom_call_target="tpu_custom_call" | custom-call | tf_op jit(solution)/shard_map/setup/pallas_call | solution.py:148
  4.7 2.6 %collective-permute-start = (bf16[2,128,512]{2,1,0:T(8,128)(2,1)S(1)}, bf16[2,128,512]{2,1,0:T(8,128)(2,1)S(1)}, u32[]{:S(2)}, u32[]{:S(2)}) collective-permute-start(bf16[2,128,512]{2,1,0:T(8,128)(2,1)S(1)} %get-tuple-element.43), channel_id=1, source_target_pairs={{0,1},{1,0},{2,3},{3,2},{4,5},{5,4},{6,7},{7,6},{8,9},{9,8},{10,11... | collective-permute-start | bytes 786440 | tf_op jit(solution)/shard_map/ppermute | solution.py:339
  7.3 3.5 %collective-permute-start.1 = (bf16[2,128,512]{2,1,0:T(8,128)(2,1)S(1)}, bf16[2,128,512]{2,1,0:T(8,128)(2,1)S(1)}, u32[]{:S(2)}, u32[]{:S(2)}) collective-permute-start(bf16[2,128,512]{2,1,0:T(8,128)(2,1)S(1)} %get-tuple-element.44.mine_in.refs_0_), channel_id=1, source_target_pairs={{0,2},{8,10},{16,18},{24,26}} | collective-permute-start | bytes 786440 | tf_op jit(solution)/shard_map/ppermute | solution.py:339
  10.8 1.7 %collective-permute-start.2 = (bf16[2,128,512]{2,1,0:T(8,128)(2,1)S(1)}, bf16[2,128,512]{2,1,0:T(8,128)(2,1)S(1)}, u32[]{:S(2)}, u32[]{:S(2)}) collective-permute-start(bf16[2,128,512]{2,1,0:T(8,128)(2,1)S(1)} %get-tuple-element.44.mine_in.refs_0_), channel_id=1, source_target_pairs={{0,4},{8,12},{16,20},{24,28}} | collective-permute-start | bytes 786440 | tf_op jit(solution)/shard_map/ppermute | solution.py:339
  12.5 1.7 %collective-permute-start.3 = (bf16[2,128,512]{2,1,0:T(8,128)(2,1)S(1)}, bf16[2,128,512]{2,1,0:T(8,128)(2,1)S(1)}, u32[]{:S(2)}, u32[]{:S(2)}) collective-permute-start(bf16[2,128,512]{2,1,0:T(8,128)(2,1)S(1)} %get-tuple-element.44.mine_in.refs_0_), channel_id=1, source_target_pairs={{0,6},{8,14},{16,22},{24,30}} | collective-permute-start | bytes 786440 | tf_op jit(solution)/shard_map/ppermute | solution.py:339
  14.3 0.7 collective-permute-start.4
  15.0 1.7 %update_0.1.refs_6_.settled_ref = f32[2,128,512]{2,1,0:T(8,128)S(1)} custom-call(s32[1]{0:T(128)} %bitcast.place_ref, bf16[2,128,512]{2,1,0:T(8,128)(2,1)S(1)} %get-tuple-element.44.mine_in.refs_0_, bf16[1,2,512,4096]{3,2,1,0:T(8,128)(2,1)} %refs_1_.3, f32[2,128,512]{2,1,0:T(8,128)S(1)} %get-tuple-element.36.settled_ref.refs_2_), custom_call_target="tpu_custom_call" | custom-call | tf_op jit(solution)/shard_map/update_0/pallas_call | solution.py:273
  18.2 4.9 %collective-permute-done.2.refs_3_.refs_2_.refs_0_ = bf16[2,128,512]{2,1,0:T(8,128)(2,1)S(1)} collective-permute-done((bf16[2,128,512]{2,1,0:T(8,128)(2,1)S(1)}, bf16[2,128,512]{2,1,0:T(8,128)(2,1)S(1)}, u32[]{:S(2)}, u32[]{:S(2)}) %collective-permute-start.2) | collective-permute-done | bytes 262176 | tf_op jit(solution)/shard_map/ppermute | solution.py:339
  23.8 3.5 %collective-permute-done.3.refs_4_.refs_3_.refs_1_ = bf16[2,128,512]{2,1,0:T(8,128)(2,1)S(1)} collective-permute-done((bf16[2,128,512]{2,1,0:T(8,128)(2,1)S(1)}, bf16[2,128,512]{2,1,0:T(8,128)(2,1)S(1)}, u32[]{:S(2)}, u32[]{:S(2)}) %collective-permute-start.3) | collective-permute-done | bytes 262176 | tf_op jit(solution)/shard_map/ppermute | solution.py:339
  28.4 0.7 collective-permute-start.11
  29.8 0.7 collective-permute-start.10
  30.7 4.5 %collective-permute-done.9.urgent_ref.refs_1_.refs_0_ = bf16[2,128,512]{2,1,0:T(8,128)(2,1)S(1)} collective-permute-done((bf16[2,128,512]{2,1,0:T(8,128)(2,1)S(1)}, bf16[2,128,512]{2,1,0:T(8,128)(2,1)S(1)}, u32[]{:S(2)}, u32[]{:S(2)}) %collective-permute-start.9) | collective-permute-done | bytes 262176 | tf_op jit(solution)/shard_map/ppermute | solution.py:339
  36.0 0.7 collective-permute-start.14
  37.6 6.3 %collective-permute-start.16 = (bf16[2,128,512]{2,1,0:T(8,128)(2,1)S(1)}, bf16[2,128,512]{2,1,0:T(8,128)(2,1)S(1)}, u32[]{:S(2)}, u32[]{:S(2)}) collective-permute-start(bf16[2,128,512]{2,1,0:T(8,128)(2,1)S(1)} %get-tuple-element.55), channel_id=1, source_target_pairs={{0,1},{1,0},{2,3},{3,2},{4,5},{5,4},{6,7},{7,6},{8,9},{9,8},{10,11... | collective-permute-start | bytes 786440 | tf_op jit(solution)/shard_map/ppermute | solution.py:339
  44.6 1.8 %update_3.1.settled_ref.refs_5_ = f32[2,128,512]{2,1,0:T(8,128)S(1)} custom-call(s32[1]{0:T(128)} %bitcast.place_ref, bf16[2,128,512]{2,1,0:T(8,128)(2,1)S(1)} %get-tuple-element.52.refs_0_.mine_in, bf16[2,128,512]{2,1,0:T(8,128)(2,1)S(1)} %collective-permute-done.9.urgent_ref.refs_1_.refs_0_, ...), custom_call_target="tpu_custom_call" | custom-call | tf_op jit(solution)/shard_map/update_3/pallas_call | solution.py:273
  48.6 1.3 collective-permute-start.21
  50.7 1.3 collective-permute-start.19
  53.6 16.9 %collective-permute-done.21.refs_6_.refs_0_ = bf16[2,128,512]{2,1,0:T(8,128)(2,1)S(1)} collective-permute-done((bf16[2,128,512]{2,1,0:T(8,128)(2,1)S(1)}, bf16[2,128,512]{2,1,0:T(8,128)(2,1)S(1)}, u32[]{:S(2)}, u32[]{:S(2)}) %collective-permute-start.21) | collective-permute-done | bytes 262176 | tf_op jit(solution)/shard_map/ppermute | solution.py:339
  70.6 1.3 collective-permute-start.31
  71.9 2.3 %update_5.1.settled_ref.refs_6_ = f32[2,128,512]{2,1,0:T(8,128)S(1)} custom-call(s32[1]{0:T(128)} %bitcast.place_ref, bf16[2,128,512]{2,1,0:T(8,128)(2,1)S(1)} %get-tuple-element.58.refs_0_.mine_in, bf16[2,128,512]{2,1,0:T(8,128)(2,1)S(1)} %collective-permute-done.16.urgent_ref.refs_1_.refs_0_, ...), custom_call_target="tpu_custom_call" | custom-call | tf_op jit(solution)/shard_map/update_5/pallas_call | solution.py:273
  75.8 1.2 collective-permute-done.26.urgent_ref.refs_1_
  77.0 0.8 solve_7.1
  79.2 5.6 %collective-permute-done.31.refs_0_.refs_4_ = bf16[2,128,512]{2,1,0:T(8,128)(2,1)S(1)} collective-permute-done((bf16[2,128,512]{2,1,0:T(8,128)(2,1)S(1)}, bf16[2,128,512]{2,1,0:T(8,128)(2,1)S(1)}, u32[]{:S(2)}, u32[]{:S(2)}) %collective-permute-start.31) | collective-permute-done | bytes 262176 | tf_op jit(solution)/shard_map/ppermute | solution.py:339
  84.8 0.7 copy-done.1
  86.2 11.1 %collective-permute-start.35 = (bf16[2,128,512]{2,1,0:T(8,128)(2,1)}, bf16[2,128,512]{2,1,0:T(8,128)(2,1)}, u32[]{:S(2)}, u32[]{:S(2)}) collective-permute-start(bf16[2,128,512]{2,1,0:T(8,128)(2,1)} %copy-done.5), channel_id=1, source_target_pairs={{0,1},{1,0},{8,9},{9,8},{16,17},{17,16},{24,25},{25,24}} | collective-permute-start | bytes 786440 | tf_op jit(solution)/shard_map/ppermute | solution.py:339
  97.3 0.9 copy-done.2
  98.3 0.8 pick_first.1
  99.1 0.8 pick_second.1
  99.9 2.0 %collective-permute-start.30 = (bf16[2,128,512]{2,1,0:T(8,128)(2,1)}, bf16[2,128,512]{2,1,0:T(8,128)(2,1)}, u32[]{:S(2)}, u32[]{:S(2)}) collective-permute-start(bf16[2,128,512]{2,1,0:T(8,128)(2,1)} %pick_second.1), channel_id=1, source_target_pairs={{0,1},{1,0},{2,3},{3,2},{4,5},{5,4},{6,7},{7,6},{8,9},{9,8},{10,11... | collective-permute-start | bytes 786440 | tf_op jit(solution)/shard_map/ppermute | solution.py:339
  101.9 0.9 fusion.9
  102.9 1.0 collective-permute-done.35.refs_4_
  103.9 2.7 %update_6.1.refs_6_ = f32[2,128,512]{2,1,0:T(8,128)S(1)} custom-call(s32[1]{0:T(128)} %bitcast.place_ref, bf16[2,128,512]{2,1,0:T(8,128)(2,1)S(1)} %get-tuple-element.62.mine_in.refs_0_, bf16[2,128,512]{2,1,0:T(8,128)(2,1)S(1)} %collective-permute-done.23.refs_0_.urgent_ref.refs_1_, bf16[2,128,512]{2,1,0:T(8,128)(2,1)S(1)} %collective-permute-done.24.refs_1_.refs_7_.refs_2_, ...), custom_call_target="tpu_custom_call" | custom-call | tf_op jit(solution)/shard_map/update_6/pallas_call | solution.py:273
  106.6 1.8 %update_7.1.refs_5_ = f32[2,128,512]{2,1,0:T(8,128)S(1)} custom-call(s32[1]{0:T(128)} %bitcast.place_ref, bf16[2,128,512]{2,1,0:T(8,128)(2,1)S(1)} %get-tuple-element.64.refs_0_.refs_2_.refs_4_.refs_6_.refs_7_.refs_5_, bf16[2,128,512]{2,1,0:T(8,128)(2,1)S(1)} %collective-permute-done.26.urgent_ref.refs_1_, ...), custom_call_target="tpu_custom_call" | custom-call | tf_op jit(solution)/shard_map/update_7/pallas_call | solution.py:273
  108.4 2.7 %update_late.1.refs_2_ = f32[2,128,512]{2,1,0:T(8,128)S(1)} custom-call(s32[1]{0:T(128)} %bitcast.place_ref, bf16[2,128,512]{2,1,0:T(8,128)(2,1)S(1)} %collective-permute-done.29.refs_5_.refs_0_, bf16[2,128,512]{2,1,0:T(8,128)(2,1)S(1)} %collective-permute-done.28.refs_3_.refs_1_, bf16[2,128,512]{2,1,0:T(8,128)(2,1)S(1)} %collective-permute-done.27.refs_1_.refs_2_, ...), custom_call_target="tpu_custom_call" | custom-call | tf_op jit(solution)/shard_map/update_late/pallas_call | solution.py:273
  111.1 2.7 %update_last.1 = f32[2,128,512]{2,1,0:T(8,128)S(1)} custom-call(s32[1]{0:T(128)} %bitcast.place_ref, bf16[2,128,512]{2,1,0:T(8,128)(2,1)} %collective-permute-done.30.refs_0_, bf16[1,2,512,4096]{3,2,1,0:T(8,128)(2,1)} %refs_1_.3, f32[2,128,512]{2,1,0:T(8,128)S(1)} %update_late.1.refs_2_), custom_call_target="tpu_custom_call" | custom-call | tf_op jit(solution)/shard_map/update_last/pallas_call | solution.py:273
  113.9 1.8 %collective-permute-start.36 = (bf16[2,128,512]{2,1,0:T(8,128)(2,1)S(1)}, bf16[2,128,512]{2,1,0:T(8,128)(2,1)S(1)}, u32[]{:S(2)}, u32[]{:S(2)}) collective-permute-start(bf16[2,128,512]{2,1,0:T(8,128)(2,1)S(1)} %fusion.6.own_ref), channel_id=1, source_target_pairs={{0,1},{1,0},{2,3},{3,2},{4,5},{5,4},{6,7},{7,6},{8,9},{9,8},{10,11... | collective-permute-start | bytes 786440 | tf_op jit(solution)/shard_map/ppermute | solution.py:339
  115.7 0.9 compare_convert_fusion
  116.6 3.7 %collective-permute-done.36.other_ref = bf16[2,128,512]{2,1,0:T(8,128)(2,1)S(1)} collective-permute-done((bf16[2,128,512]{2,1,0:T(8,128)(2,1)S(1)}, bf16[2,128,512]{2,1,0:T(8,128)(2,1)S(1)}, u32[]{:S(2)}, u32[]{:S(2)}) %collective-permute-start.36) | collective-permute-done | bytes 262176 | tf_op jit(solution)/shard_map/ppermute | solution.py:339
  120.4 1.5 %place_rows.1 = (bf16[2,128,512]{2,1,0:T(8,128)(2,1)S(1)}, bf16[2,128,512]{2,1,0:T(8,128)(2,1)S(1)}, bf16[2,128,512]{2,1,0:T(8,128)(2,1)S(1)}, bf16[2,128,512]{2,1,0:T(8,128)(2,1)S(1)}, bf16[2,128,512]{2,1,0:T(8,128)(2,1)S(1)}) custom-call(bf16[2,128,512]{2,1,0:T(8,128)(2,1)S(1)} %fusion.6.own_ref, ...), custom_call_target="tpu_custom_call" | custom-call | tf_op jit(solution)/shard_map/place_rows/pallas_call | solution.py:302
  121.9 1.0 collective-permute-start.37
  122.9 3.5 %collective-permute-start.39 = (bf16[2,128,512]{2,1,0:T(8,128)(2,1)S(1)}, bf16[2,128,512]{2,1,0:T(8,128)(2,1)S(1)}, u32[]{:S(2)}, u32[]{:S(2)}) collective-permute-start(bf16[2,128,512]{2,1,0:T(8,128)(2,1)S(1)} %get-tuple-element.68), channel_id=1, source_target_pairs={{0,6},{1,7},{2,4},{3,5},{4,2},{5,3},{6,0},{7,1},{8,14},{9,15},{10,... | collective-permute-start | bytes 786440 | tf_op jit(solution)/shard_map/ppermute | solution.py:339
  126.3 3.5 %collective-permute-done.37 = bf16[2,128,512]{2,1,0:T(8,128)(2,1)S(1)} collective-permute-done((bf16[2,128,512]{2,1,0:T(8,128)(2,1)S(1)}, bf16[2,128,512]{2,1,0:T(8,128)(2,1)S(1)}, u32[]{:S(2)}, u32[]{:S(2)}) %collective-permute-start.37) | collective-permute-done | bytes 262176 | tf_op jit(solution)/shard_map/ppermute | solution.py:339
  129.9 7.8 %collective-permute-done.38 = bf16[2,128,512]{2,1,0:T(8,128)(2,1)S(1)} collective-permute-done((bf16[2,128,512]{2,1,0:T(8,128)(2,1)S(1)}, bf16[2,128,512]{2,1,0:T(8,128)(2,1)S(1)}, u32[]{:S(2)}, u32[]{:S(2)}) %collective-permute-start.38) | collective-permute-done | bytes 262176 | tf_op jit(solution)/shard_map/ppermute | solution.py:339
  138.1 0.7 copy.21
  138.8 0.8 collective-permute-done.40
  139.6 1.2 fusion.8
  (86 shorter events, 15.7 us)
Async XLA Ops:
  0.6 1.2 copy-start
  1.9 0.9 copy-start.4
  4.7 9.5 %collective-permute-start = (bf16[2,128,512]{2,1,0:T(8,128)(2,1)S(1)}, bf16[2,128,512]{2,1,0:T(8,128)(2,1)S(1)}, u32[]{:S(2)}, u32[]{:S(2)}) collective-permute-start(bf16[2,128,512]{2,1,0:T(8,128)(2,1)S(1)} %get-tuple-element.43), channel_id=1, source_target_pairs={{0,1},{1,0},{2,3},{3,2},{4,5},{5,4},{6,7},{7,6},{8,9},{9,8},{10,11... | collective-permute-start | bytes 786440 | tf_op jit(solution)/shard_map/ppermute | solution.py:339
  7.3 10.2 %collective-permute-start.1 = (bf16[2,128,512]{2,1,0:T(8,128)(2,1)S(1)}, bf16[2,128,512]{2,1,0:T(8,128)(2,1)S(1)}, u32[]{:S(2)}, u32[]{:S(2)}) collective-permute-start(bf16[2,128,512]{2,1,0:T(8,128)(2,1)S(1)} %get-tuple-element.44.mine_in.refs_0_), channel_id=1, source_target_pairs={{0,2},{8,10},{16,18},{24,26}} | collective-permute-start | bytes 786440 | tf_op jit(solution)/shard_map/ppermute | solution.py:339
  10.8 12.3 %collective-permute-start.2 = (bf16[2,128,512]{2,1,0:T(8,128)(2,1)S(1)}, bf16[2,128,512]{2,1,0:T(8,128)(2,1)S(1)}, u32[]{:S(2)}, u32[]{:S(2)}) collective-permute-start(bf16[2,128,512]{2,1,0:T(8,128)(2,1)S(1)} %get-tuple-element.44.mine_in.refs_0_), channel_id=1, source_target_pairs={{0,4},{8,12},{16,20},{24,28}} | collective-permute-start | bytes 786440 | tf_op jit(solution)/shard_map/ppermute | solution.py:339
  12.5 14.8 %collective-permute-start.3 = (bf16[2,128,512]{2,1,0:T(8,128)(2,1)S(1)}, bf16[2,128,512]{2,1,0:T(8,128)(2,1)S(1)}, u32[]{:S(2)}, u32[]{:S(2)}) collective-permute-start(bf16[2,128,512]{2,1,0:T(8,128)(2,1)S(1)} %get-tuple-element.44.mine_in.refs_0_), channel_id=1, source_target_pairs={{0,6},{8,14},{16,22},{24,30}} | collective-permute-start | bytes 786440 | tf_op jit(solution)/shard_map/ppermute | solution.py:339
  14.3 13.8 %collective-permute-start.4 = (bf16[2,128,512]{2,1,0:T(8,128)(2,1)S(1)}, bf16[2,128,512]{2,1,0:T(8,128)(2,1)S(1)}, u32[]{:S(2)}, u32[]{:S(2)}) collective-permute-start(bf16[2,128,512]{2,1,0:T(8,128)(2,1)S(1)} %get-tuple-element.47), channel_id=1, source_target_pairs={{1,2},{9,10},{17,18},{25,26}} | collective-permute-start | bytes 786440 | tf_op jit(solution)/shard_map/ppermute | solution.py:339
  16.7 11.7 %collective-permute-start.5 = (bf16[2,128,512]{2,1,0:T(8,128)(2,1)S(1)}, bf16[2,128,512]{2,1,0:T(8,128)(2,1)S(1)}, u32[]{:S(2)}, u32[]{:S(2)}) collective-permute-start(bf16[2,128,512]{2,1,0:T(8,128)(2,1)S(1)} %get-tuple-element.46.refs_0_.mine_in), channel_id=1, source_target_pairs={{1,3},{9,11},{17,19},{25,27}} | collective-permute-start | bytes 786440 | tf_op jit(solution)/shard_map/ppermute | solution.py:339
  17.5 11.6 %collective-permute-start.7 = (bf16[2,128,512]{2,1,0:T(8,128)(2,1)S(1)}, bf16[2,128,512]{2,1,0:T(8,128)(2,1)S(1)}, u32[]{:S(2)}, u32[]{:S(2)}) collective-permute-start(bf16[2,128,512]{2,1,0:T(8,128)(2,1)S(1)} %get-tuple-element.46.refs_0_.mine_in), channel_id=1, source_target_pairs={{1,5},{9,13},{17,21},{25,29}} | collective-permute-start | bytes 786440 | tf_op jit(solution)/shard_map/ppermute | solution.py:339
  23.2 6.6 %collective-permute-start.8 = (bf16[2,128,512]{2,1,0:T(8,128)(2,1)S(1)}, bf16[2,128,512]{2,1,0:T(8,128)(2,1)S(1)}, u32[]{:S(2)}, u32[]{:S(2)}) collective-permute-start(bf16[2,128,512]{2,1,0:T(8,128)(2,1)S(1)} %get-tuple-element.46.refs_0_.mine_in), channel_id=1, source_target_pairs={{1,7},{9,15},{17,23},{25,31}} | collective-permute-start | bytes 786440 | tf_op jit(solution)/shard_map/ppermute | solution.py:339
  27.3 3.2 %collective-permute-start.6 = (bf16[2,128,512]{2,1,0:T(8,128)(2,1)S(1)}, bf16[2,128,512]{2,1,0:T(8,128)(2,1)S(1)}, u32[]{:S(2)}, u32[]{:S(2)}) collective-permute-start(bf16[2,128,512]{2,1,0:T(8,128)(2,1)S(1)} %collective-permute-done.1.refs_2_.refs_1_), channel_id=1, source_target_pairs={{2,3},{10,11},{18,19},{26,27}} | collective-permute-start | bytes 786440 | tf_op jit(solution)/shard_map/ppermute | solution.py:339
  28.2 6.9 %collective-permute-start.9 = (bf16[2,128,512]{2,1,0:T(8,128)(2,1)S(1)}, bf16[2,128,512]{2,1,0:T(8,128)(2,1)S(1)}, u32[]{:S(2)}, u32[]{:S(2)}) collective-permute-start(bf16[2,128,512]{2,1,0:T(8,128)(2,1)S(1)} %get-tuple-element.49), channel_id=1, source_target_pairs={{0,1},{1,0},{2,3},{3,2},{4,5},{5,4},{6,7},{7,6},{8,9},{9,8},{10,11... | collective-permute-start | bytes 786440 | tf_op jit(solution)/shard_map/ppermute | solution.py:339
  28.4 8.3 %collective-permute-start.11 = (bf16[2,128,512]{2,1,0:T(8,128)(2,1)S(1)}, bf16[2,128,512]{2,1,0:T(8,128)(2,1)S(1)}, u32[]{:S(2)}, u32[]{:S(2)}) collective-permute-start(bf16[2,128,512]{2,1,0:T(8,128)(2,1)S(1)} %get-tuple-element.50.mine_in.refs_0_), channel_id=1, source_target_pairs={{2,4},{10,12},{18,20},{26,28}} | collective-permute-start | bytes 786440 | tf_op jit(solution)/shard_map/ppermute | solution.py:339
  29.1 8.3 %collective-permute-start.12 = (bf16[2,128,512]{2,1,0:T(8,128)(2,1)S(1)}, bf16[2,128,512]{2,1,0:T(8,128)(2,1)S(1)}, u32[]{:S(2)}, u32[]{:S(2)}) collective-permute-start(bf16[2,128,512]{2,1,0:T(8,128)(2,1)S(1)} %get-tuple-element.50.mine_in.refs_0_), channel_id=1, source_target_pairs={{2,6},{10,14},{18,22},{26,30}} | collective-permute-start | bytes 786440 | tf_op jit(solution)/shard_map/ppermute | solution.py:339
  29.8 7.6 %collective-permute-start.10 = (bf16[2,128,512]{2,1,0:T(8,128)(2,1)S(1)}, bf16[2,128,512]{2,1,0:T(8,128)(2,1)S(1)}, u32[]{:S(2)}, u32[]{:S(2)}) collective-permute-start(bf16[2,128,512]{2,1,0:T(8,128)(2,1)S(1)} %get-tuple-element.51.before_in), channel_id=1, source_target_pairs={{2,4},{10,12},{18,20},{26,28}} | collective-permute-start | bytes 786440 | tf_op jit(solution)/shard_map/ppermute | solution.py:339
  35.2 2.4 %collective-permute-start.13 = (bf16[2,128,512]{2,1,0:T(8,128)(2,1)S(1)}, bf16[2,128,512]{2,1,0:T(8,128)(2,1)S(1)}, u32[]{:S(2)}, u32[]{:S(2)}) collective-permute-start(bf16[2,128,512]{2,1,0:T(8,128)(2,1)S(1)} %get-tuple-element.53), channel_id=1, source_target_pairs={{3,4},{11,12},{19,20},{27,28}} | collective-permute-start | bytes 786440 | tf_op jit(solution)/shard_map/ppermute | solution.py:339
  36.0 11.0 %collective-permute-start.14 = (bf16[2,128,512]{2,1,0:T(8,128)(2,1)S(1)}, bf16[2,128,512]{2,1,0:T(8,128)(2,1)S(1)}, u32[]{:S(2)}, u32[]{:S(2)}) collective-permute-start(bf16[2,128,512]{2,1,0:T(8,128)(2,1)S(1)} %get-tuple-element.52.refs_0_.mine_in), channel_id=1, source_target_pairs={{3,5},{11,13},{19,21},{27,29}} | collective-permute-start | bytes 786440 | tf_op jit(solution)/shard_map/ppermute | solution.py:339
  36.7 11.0 %collective-permute-start.15 = (bf16[2,128,512]{2,1,0:T(8,128)(2,1)S(1)}, bf16[2,128,512]{2,1,0:T(8,128)(2,1)S(1)}, u32[]{:S(2)}, u32[]{:S(2)}) collective-permute-start(bf16[2,128,512]{2,1,0:T(8,128)(2,1)S(1)} %collective-permute-done.11.refs_3_.refs_2_), channel_id=1, source_target_pairs={{4,5},{12,13},{20,21},{28,29}} | collective-permute-start | bytes 786440 | tf_op jit(solution)/shard_map/ppermute | solution.py:339
  37.6 10.9 %collective-permute-start.16 = (bf16[2,128,512]{2,1,0:T(8,128)(2,1)S(1)}, bf16[2,128,512]{2,1,0:T(8,128)(2,1)S(1)}, u32[]{:S(2)}, u32[]{:S(2)}) collective-permute-start(bf16[2,128,512]{2,1,0:T(8,128)(2,1)S(1)} %get-tuple-element.55), channel_id=1, source_target_pairs={{0,1},{1,0},{2,3},{3,2},{4,5},{5,4},{6,7},{7,6},{8,9},{9,8},{10,11... | collective-permute-start | bytes 786440 | tf_op jit(solution)/shard_map/ppermute | solution.py:339
  43.9 6.0 %collective-permute-start.17 = (bf16[2,128,512]{2,1,0:T(8,128)(2,1)S(1)}, bf16[2,128,512]{2,1,0:T(8,128)(2,1)S(1)}, u32[]{:S(2)}, u32[]{:S(2)}) collective-permute-start(bf16[2,128,512]{2,1,0:T(8,128)(2,1)S(1)} %get-tuple-element.57.before_in), channel_id=1, source_target_pairs={{4,6},{12,14},{20,22},{28,30}} | collective-permute-start | bytes 786440 | tf_op jit(solution)/shard_map/ppermute | solution.py:339
  46.4 4.4 %collective-permute-start.18 = (bf16[2,128,512]{2,1,0:T(8,128)(2,1)S(1)}, bf16[2,128,512]{2,1,0:T(8,128)(2,1)S(1)}, u32[]{:S(2)}, u32[]{:S(2)}) collective-permute-start(bf16[2,128,512]{2,1,0:T(8,128)(2,1)S(1)} %get-tuple-element.56.mine_in.refs_0_), channel_id=1, source_target_pairs={{4,6},{12,14},{20,22},{28,30}} | collective-permute-start | bytes 786440 | tf_op jit(solution)/shard_map/ppermute | solution.py:339
  47.0 5.8 %collective-permute-start.20 = (bf16[2,128,512]{2,1,0:T(8,128)(2,1)S(1)}, bf16[2,128,512]{2,1,0:T(8,128)(2,1)S(1)}, u32[]{:S(2)}, u32[]{:S(2)}) collective-permute-start(bf16[2,128,512]{2,1,0:T(8,128)(2,1)S(1)} %get-tuple-element.56.mine_in.refs_0_), channel_id=1, source_target_pairs={{4,2},{12,10},{20,18},{28,26}} | collective-permute-start | bytes 786440 | tf_op jit(solution)/shard_map/ppermute | solution.py:339
  47.7 4.3 %collective-permute-start.22 = (bf16[2,128,512]{2,1,0:T(8,128)(2,1)S(1)}, bf16[2,128,512]{2,1,0:T(8,128)(2,1)S(1)}, u32[]{:S(2)}, u32[]{:S(2)}) collective-permute-start(bf16[2,128,512]{2,1,0:T(8,128)(2,1)S(1)} %collective-permute-done.14.refs_1_.refs_2_), channel_id=1, source_target_pairs={{5,7},{13,15},{21,23},{29,31}} | collective-permute-start | bytes 786440 | tf_op jit(solution)/shard_map/ppermute | solution.py:339
  48.6 21.9 %collective-permute-start.21 = (bf16[2,128,512]{2,1,0:T(8,128)(2,1)S(1)}, bf16[2,128,512]{2,1,0:T(8,128)(2,1)S(1)}, u32[]{:S(2)}, u32[]{:S(2)}) collective-permute-start(bf16[2,128,512]{2,1,0:T(8,128)(2,1)S(1)} %get-tuple-element.56.mine_in.refs_0_), channel_id=1, source_target_pairs={{4,0},{12,8},{20,16},{28,24}} | collective-permute-start | bytes 786440 | tf_op jit(solution)/shard_map/ppermute | solution.py:339
  49.9 20.5 %collective-permute-start.23 = (bf16[2,128,512]{2,1,0:T(8,128)(2,1)S(1)}, bf16[2,128,512]{2,1,0:T(8,128)(2,1)S(1)}, u32[]{:S(2)}, u32[]{:S(2)}) collective-permute-start(bf16[2,128,512]{2,1,0:T(8,128)(2,1)S(1)} %get-tuple-element.59), channel_id=1, source_target_pairs={{5,6},{13,14},{21,22},{29,30}} | collective-permute-start | bytes 786440 | tf_op jit(solution)/shard_map/ppermute | solution.py:339
  50.7 21.2 %collective-permute-start.19 = (bf16[2,128,512]{2,1,0:T(8,128)(2,1)S(1)}, bf16[2,128,512]{2,1,0:T(8,128)(2,1)S(1)}, u32[]{:S(2)}, u32[]{:S(2)}) collective-permute-start(bf16[2,128,512]{2,1,0:T(8,128)(2,1)S(1)} %get-tuple-element.56.mine_in.refs_0_), channel_id=1, source_target_pairs={{2,0},{3,1},{10,8},{11,9},{18,16},{19,17},{26,24},{27,25}} | collective-permute-start | bytes 786440 | tf_op jit(solution)/shard_map/ppermute | solution.py:339
  52.0 22.9 %collective-permute-start.24 = (bf16[2,128,512]{2,1,0:T(8,128)(2,1)S(1)}, bf16[2,128,512]{2,1,0:T(8,128)(2,1)S(1)}, u32[]{:S(2)}, u32[]{:S(2)}) collective-permute-start(bf16[2,128,512]{2,1,0:T(8,128)(2,1)S(1)} %get-tuple-element.58.refs_0_.mine_in), channel_id=1, source_target_pairs={{5,7},{13,15},{21,23},{29,31}} | collective-permute-start | bytes 786440 | tf_op jit(solution)/shard_map/ppermute | solution.py:339
  52.9 22.8 %collective-permute-start.25 = (bf16[2,128,512]{2,1,0:T(8,128)(2,1)S(1)}, bf16[2,128,512]{2,1,0:T(8,128)(2,1)S(1)}, u32[]{:S(2)}, u32[]{:S(2)}) collective-permute-start(bf16[2,128,512]{2,1,0:T(8,128)(2,1)S(1)} %collective-permute-done.18.refs_3_.refs_2_), channel_id=1, source_target_pairs={{6,7},{14,15},{22,23},{30,31}} | collective-permute-start | bytes 786440 | tf_op jit(solution)/shard_map/ppermute | solution.py:339
  70.5 6.4 %collective-permute-start.26 = (bf16[2,128,512]{2,1,0:T(8,128)(2,1)S(1)}, bf16[2,128,512]{2,1,0:T(8,128)(2,1)S(1)}, u32[]{:S(2)}, u32[]{:S(2)}) collective-permute-start(bf16[2,128,512]{2,1,0:T(8,128)(2,1)S(1)} %get-tuple-element.61), channel_id=1, source_target_pairs={{0,1},{1,0},{2,3},{3,2},{4,5},{5,4},{6,7},{7,6},{8,9},{9,8},{10,11... | collective-permute-start | bytes 786440 | tf_op jit(solution)/shard_map/ppermute | solution.py:339
  70.6 14.2 %collective-permute-start.31 = (bf16[2,128,512]{2,1,0:T(8,128)(2,1)S(1)}, bf16[2,128,512]{2,1,0:T(8,128)(2,1)S(1)}, u32[]{:S(2)}, u32[]{:S(2)}) collective-permute-start(bf16[2,128,512]{2,1,0:T(8,128)(2,1)S(1)} %get-tuple-element.62.mine_in.refs_0_), channel_id=1, source_target_pairs={{6,0},{14,8},{22,16},{30,24}} | collective-permute-start | bytes 786440 | tf_op jit(solution)/shard_map/ppermute | solution.py:339
  71.9 2.4 %copy-start.5 = (bf16[2,128,512]{2,1,0:T(8,128)(2,1)}, bf16[2,128,512]{2,1,0:T(8,128)(2,1)S(1)}, u32[]{:S(2)}) copy-start(bf16[2,128,512]{2,1,0:T(8,128)(2,1)S(1)} %collective-permute-done.19.refs_4_) | copy-start | bytes 786436
  74.3 11.9 %collective-permute-start.32 = (bf16[2,128,512]{2,1,0:T(8,128)(2,1)S(1)}, bf16[2,128,512]{2,1,0:T(8,128)(2,1)S(1)}, u32[]{:S(2)}, u32[]{:S(2)}) collective-permute-start(bf16[2,128,512]{2,1,0:T(8,128)(2,1)S(1)} %get-tuple-element.62.mine_in.refs_0_), channel_id=1, source_target_pairs={{6,2},{5,1},{14,10},{13,9},{22,18},{21,17},{30,26},{29,25}} | collective-permute-start | bytes 786440 | tf_op jit(solution)/shard_map/ppermute | solution.py:339
  75.0 22.4 %collective-permute-start.33 = (bf16[2,128,512]{2,1,0:T(8,128)(2,1)S(1)}, bf16[2,128,512]{2,1,0:T(8,128)(2,1)S(1)}, u32[]{:S(2)}, u32[]{:S(2)}) collective-permute-start(bf16[2,128,512]{2,1,0:T(8,128)(2,1)S(1)} %get-tuple-element.62.mine_in.refs_0_), channel_id=1, source_target_pairs={{6,4},{5,3},{14,12},{13,11},{22,20},{21,19},{30,28},{29,27}} | collective-permute-start | bytes 786440 | tf_op jit(solution)/shard_map/ppermute | solution.py:339
  77.8 21.3 %collective-permute-start.27 = (bf16[2,128,512]{2,1,0:T(8,128)(2,1)S(1)}, bf16[2,128,512]{2,1,0:T(8,128)(2,1)S(1)}, u32[]{:S(2)}, u32[]{:S(2)}) collective-permute-start(bf16[2,128,512]{2,1,0:T(8,128)(2,1)S(1)} %get-tuple-element.64.refs_0_.refs_2_.refs_4_.refs_6_.refs_7_.refs_5_), channel_id=1, source_target_pairs={{7,1},{15,9},{23,17},{31,25}} | collective-permute-start | bytes 786440 | tf_op jit(solution)/shard_map/ppermute | solution.py:339
  78.5 20.6 %collective-permute-start.28 = (bf16[2,128,512]{2,1,0:T(8,128)(2,1)S(1)}, bf16[2,128,512]{2,1,0:T(8,128)(2,1)S(1)}, u32[]{:S(2)}, u32[]{:S(2)}) collective-permute-start(bf16[2,128,512]{2,1,0:T(8,128)(2,1)S(1)} %get-tuple-element.64.refs_0_.refs_2_.refs_4_.refs_6_.refs_7_.refs_5_), channel_id=1, source_target_pairs={{7,3},{15,11},{23,19},{31,27}} | collective-permute-start | bytes 786440 | tf_op jit(solution)/shard_map/ppermute | solution.py:339
  85.5 13.6 %collective-permute-start.29 = (bf16[2,128,512]{2,1,0:T(8,128)(2,1)S(1)}, bf16[2,128,512]{2,1,0:T(8,128)(2,1)S(1)}, u32[]{:S(2)}, u32[]{:S(2)}) collective-permute-start(bf16[2,128,512]{2,1,0:T(8,128)(2,1)S(1)} %get-tuple-element.64.refs_0_.refs_2_.refs_4_.refs_6_.refs_7_.refs_5_), channel_id=1, source_target_pairs={{7,5},{15,13},{23,21},{31,29}} | collective-permute-start | bytes 786440 | tf_op jit(solution)/shard_map/ppermute | solution.py:339
  86.2 17.7 %collective-permute-start.35 = (bf16[2,128,512]{2,1,0:T(8,128)(2,1)}, bf16[2,128,512]{2,1,0:T(8,128)(2,1)}, u32[]{:S(2)}, u32[]{:S(2)}) collective-permute-start(bf16[2,128,512]{2,1,0:T(8,128)(2,1)} %copy-done.5), channel_id=1, source_target_pairs={{0,1},{1,0},{8,9},{9,8},{16,17},{17,16},{24,25},{25,24}} | collective-permute-start | bytes 786440 | tf_op jit(solution)/shard_map/ppermute | solution.py:339
  97.3 1.0 copy-start.2
  99.1 9.3 %collective-permute-start.34 = (bf16[2,128,512]{2,1,0:T(8,128)(2,1)}, bf16[2,128,512]{2,1,0:T(8,128)(2,1)}, u32[]{:S(2)}, u32[]{:S(2)}) collective-permute-start(bf16[2,128,512]{2,1,0:T(8,128)(2,1)} %pick_first.1), channel_id=1, source_target_pairs={{0,1},{1,0},{2,3},{3,2},{4,5},{5,4},{6,7},{7,6},{8,9},{9,8},{10,11... | collective-permute-start | bytes 786440 | tf_op jit(solution)/shard_map/ppermute | solution.py:339
  99.9 11.2 %collective-permute-start.30 = (bf16[2,128,512]{2,1,0:T(8,128)(2,1)}, bf16[2,128,512]{2,1,0:T(8,128)(2,1)}, u32[]{:S(2)}, u32[]{:S(2)}) collective-permute-start(bf16[2,128,512]{2,1,0:T(8,128)(2,1)} %pick_second.1), channel_id=1, source_target_pairs={{0,1},{1,0},{2,3},{3,2},{4,5},{5,4},{6,7},{7,6},{8,9},{9,8},{10,11... | collective-permute-start | bytes 786440 | tf_op jit(solution)/shard_map/ppermute | solution.py:339
  102.9 3.7 %copy-start.3 = (bf16[2,128,512]{2,1,0:T(8,128)(2,1)S(1)}, bf16[2,128,512]{2,1,0:T(8,128)(2,1)}, u32[]{:S(2)}) copy-start(bf16[2,128,512]{2,1,0:T(8,128)(2,1)} %copy-done.1) | copy-start | bytes 786436
  111.1 2.7 %copy-start.7 = (bf16[1,2,128,512]{3,2,1,0:T(8,128)(2,1)S(1)}, bf16[1,2,128,512]{3,2,1,0:T(8,128)(2,1)}, u32[]{:S(2)}) copy-start(bf16[1,2,128,512]{3,2,1,0:T(8,128)(2,1)} %param.11) | copy-start | bytes 786436
  113.9 6.4 %collective-permute-start.36 = (bf16[2,128,512]{2,1,0:T(8,128)(2,1)S(1)}, bf16[2,128,512]{2,1,0:T(8,128)(2,1)S(1)}, u32[]{:S(2)}, u32[]{:S(2)}) collective-permute-start(bf16[2,128,512]{2,1,0:T(8,128)(2,1)S(1)} %fusion.6.own_ref), channel_id=1, source_target_pairs={{0,1},{1,0},{2,3},{3,2},{4,5},{5,4},{6,7},{7,6},{8,9},{9,8},{10,11... | collective-permute-start | bytes 786440 | tf_op jit(solution)/shard_map/ppermute | solution.py:339
  120.4 19.2 %copy-start.6 = (f32[1,2,128,512]{3,2,1,0:T(8,128)S(1)}, f32[1,2,128,512]{3,2,1,0:T(8,128)}, u32[]{:S(2)}) copy-start(f32[1,2,128,512]{3,2,1,0:T(8,128)} %param.13) | copy-start | bytes 1572868
  121.9 8.0 %collective-permute-start.37 = (bf16[2,128,512]{2,1,0:T(8,128)(2,1)S(1)}, bf16[2,128,512]{2,1,0:T(8,128)(2,1)S(1)}, u32[]{:S(2)}, u32[]{:S(2)}) collective-permute-start(bf16[2,128,512]{2,1,0:T(8,128)(2,1)S(1)} %get-tuple-element.66), channel_id=1, source_target_pairs={{0,2},{1,3},{2,0},{3,1},{4,6},{5,7},{6,4},{7,5},{8,10},{9,11},{10,... | collective-permute-start | bytes 786440 | tf_op jit(solution)/shard_map/ppermute | solution.py:339
  122.9 14.8 %collective-permute-start.38 = (bf16[2,128,512]{2,1,0:T(8,128)(2,1)S(1)}, bf16[2,128,512]{2,1,0:T(8,128)(2,1)S(1)}, u32[]{:S(2)}, u32[]{:S(2)}) collective-permute-start(bf16[2,128,512]{2,1,0:T(8,128)(2,1)S(1)} %get-tuple-element.67), channel_id=1, source_target_pairs={{0,4},{1,5},{2,6},{3,7},{4,0},{5,1},{6,2},{7,3},{8,12},{9,13},{10,... | collective-permute-start | bytes 786440 | tf_op jit(solution)/shard_map/ppermute | solution.py:339
  122.9 14.8 %collective-permute-start.39 = (bf16[2,128,512]{2,1,0:T(8,128)(2,1)S(1)}, bf16[2,128,512]{2,1,0:T(8,128)(2,1)S(1)}, u32[]{:S(2)}, u32[]{:S(2)}) collective-permute-start(bf16[2,128,512]{2,1,0:T(8,128)(2,1)S(1)} %get-tuple-element.68), channel_id=1, source_target_pairs={{0,6},{1,7},{2,4},{3,5},{4,2},{5,3},{6,0},{7,1},{8,14},{9,15},{10,... | collective-permute-start | bytes 786440 | tf_op jit(solution)/shard_map/ppermute | solution.py:339
  138.0 1.6 %collective-permute-start.40 = (bf16[2,128,512]{2,1,0:T(8,128)(2,1)S(1)}, bf16[2,128,512]{2,1,0:T(8,128)(2,1)S(1)}, u32[]{:S(2)}, u32[]{:S(2)}) collective-permute-start(bf16[2,128,512]{2,1,0:T(8,128)(2,1)S(1)} %select_convert_fusion), channel_id=1, source_target_pairs={{0,8},{8,0},{16,24},{24,16},{1,9},{9,1},{17,25},{25,17},{2,10},{10... | collective-permute-start | bytes 786440 | tf_op jit(solution)/shard_map/ppermute | solution.py:396
  (1 other events, 0.7 us)

commit v4 on v3

--- a/solution.py
+++ b/solution.py
@@ -13,29 +13,37 @@
 BF16 = jnp.bfloat16
 
 SWAP = ((0, 1), (1, 0), (2, 3), (3, 2), (4, 5), (5, 4), (6, 7), (7, 6))
-CHAIN = (SWAP, ((1, 2),), SWAP, ((3, 4),), SWAP, ((5, 6),), SWAP)
+CHAIN = (
+    SWAP,
+    ((1, 2), (2, 3), (3, 0), (0, 1), (4, 5), (5, 4), (6, 7), (7, 6)),
+    SWAP,
+    ((3, 4), (4, 5), (5, 2), (2, 3), (0, 1), (1, 0), (6, 7), (7, 6)),
+    SWAP,
+    ((5, 6), (6, 7), (7, 4), (4, 5), (0, 1), (1, 0), (2, 3), (3, 2)),
+    SWAP,
+)
 RELAY = {
-    2: {4: (0, 1), 6: (0, 2)},
-    4: {6: (2, 2), 7: (1, 3)},
-    6: {0: (4, 4), 2: (4, 3)},
+    2: {4: (0, 1), 6: (0, 0)},
+    4: {7: (1, 0)},
+    6: {0: (5, 4), 2: (5, 3)},
 }
 OWN, PREV = "own", "prev"
 SPREAD = (
-    ((OWN, ((0, 2),)), (OWN, ((0, 4),)), (OWN, ((0, 6),))),
-    ((OWN, ((1, 3),)), ((0, 0), ((2, 3),)), (OWN, ((1, 5),)), (OWN, ((1, 7),))),
-    ((PREV, ((2, 4),)), (OWN, ((2, 4),)), (OWN, ((2, 6),))),
-    ((OWN, ((3, 5),)), ((2, 1), ((4, 5),))),
+    ((OWN, ((0, 6),), 1), (OWN, ((0, 4),), 1), (OWN, ((0, 2),), 1)),
+    ((OWN, ((1, 7),), 2), (OWN, ((1, 5),), 2), ((0, 2), ((2, 3),), 2), (OWN, ((1, 3),), 2)),
+    ((PREV, ((2, 4),), 3), (OWN, ((2, 4),), 3)),
+    ((OWN, ((3, 5), (2, 6)), 4), ((2, 1), ((4, 5),), 4)),
+    ((PREV, ((4, 6),), 5), (OWN, ((4, 6),), 5), (OWN, ((2, 0), (3, 1)), 5), ((3, 0), ((5, 7),), 5)),
     (
-        (PREV, ((4, 6),)),
-        (OWN, ((4, 6),)),
-        (OWN, ((2, 0), (3, 1))),
-        (OWN, ((4, 2),)),
-        (OWN, ((4, 0),)),
-        ((3, 0), ((5, 7),)),
+        (OWN, ((5, 7),), 6),
+        ((4, 1), ((6, 7),), 6),
+        ((3, 0), ((6, 7),), 6),
+        (OWN, ((5, 3), (4, 2)), 6),
+        (OWN, ((5, 1), (4, 0)), 6),
+        ((4, 2), ((0, 1), (1, 0)), 6),
     ),
-    ((OWN, ((5, 7),)), ((4, 1), ((6, 7),)), ((4, 2), ((0, 1), (1, 0)))),
-    ((OWN, ((6, 4), (5, 3))), (OWN, ((6, 2), (5, 1))), (OWN, ((6, 0),))),
-    ((OWN, ((7, 5),)), (OWN, ((7, 3),)), (OWN, ((7, 1),))),
+    ((OWN, ((6, 4),), 7), (OWN, ((6, 2),), 7), (OWN, ((6, 0),), 7)),
+    ((OWN, ((7, 5),), 8), (OWN, ((7, 3),), 8), (OWN, ((7, 1),), 8)),
 )
 
 
@@ -72,7 +80,7 @@
             keep(row)
             chain.append(row)
         rows = []
-        for value, edges in SPREAD[hop]:
+        for value, edges, _ in SPREAD[hop]:
             if value == OWN:
                 row = taken(edges, lambda source: source)
             elif value == PREV:
@@ -91,8 +99,8 @@
     assert all(held == set(range(count)) for held in have)
     for p in range(count):
         for hop, rows in enumerate(spread):
-            for row in rows:
-                assert row[p] < 0 or row[p] > p or hop + 1 < p
+            for (_, _, use), row in zip(SPREAD[hop], rows):
+                assert use > hop and (row[p] < 0 or row[p] > p or use < p)
         for hop, row in enumerate(chain):
             assert row[p] < 0 or row[p] > p or hop + 1 < p or (hop + 1 == p and row[p] == hop)
     return spread, chain, swaps
@@ -120,44 +128,62 @@
     )
 
 
-def setup_kernel(place_ref, lower_ref, inverse_ref, pivot_ref, near_ref, inv_ref, rhs_ref, acc_l_ref, acc_u_ref, mine_ref, before_ref, sems):
+def setup_kernel(place_ref, lower_ref, near_ref, acc_l_ref, acc_u_ref, zero_ref, sem):
     width = near_ref.shape[-1]
     block = jnp.maximum(place_ref[0] - 1, 0)
     columns = pl.ds(pl.multiple_of(block * width, width), width)
-    copies = (
-        pltpu.make_async_copy(pivot_ref.at[0], rhs_ref, sems.at[0]),
-        pltpu.make_async_copy(inverse_ref.at[0], inv_ref, sems.at[1]),
-        pltpu.make_async_copy(lower_ref.at[0, :, :, columns], near_ref, sems.at[2]),
-    )
-    for copy in copies:
-        copy.start()
-    for ref in (acc_l_ref, acc_u_ref, mine_ref, before_ref):
+    copy = pltpu.make_async_copy(lower_ref.at[0, :, :, columns], near_ref, sem)
+    copy.start()
+    for ref in (acc_l_ref, acc_u_ref, zero_ref):
         ref[...] = jnp.zeros_like(ref)
-    for copy in copies:
-        copy.wait()
-
-
-def setup(place, lower, inverse, pivot):
+    copy.wait()
+
+
+def setup(place, lower, shots):
     rows = lower.shape[2]
-    shots = pivot.shape[2]
-    hbm = pl.BlockSpec(memory_space=pltpu.HBM)
     vmem = pl.BlockSpec(memory_space=pltpu.VMEM)
-    weight = pltpu.VMEM((2, rows, CB), BF16)
-    block = pltpu.VMEM((2, shots, CB), BF16)
     acc = pltpu.VMEM((2, shots, rows), F32)
     return pl.pallas_call(
         setup_kernel,
-        out_shape=(weight, weight, block, acc, acc, block, block),
-        in_specs=[pl.BlockSpec(memory_space=pltpu.SMEM), hbm, hbm, hbm],
-        out_specs=(vmem,) * 7,
-        scratch_shapes=[pltpu.SemaphoreType.DMA((3,))],
+        out_shape=(pltpu.VMEM((2, rows, CB), BF16), acc, acc, pltpu.VMEM((2, shots, CB), BF16)),
+        in_specs=[pl.BlockSpec(memory_space=pltpu.SMEM), pl.BlockSpec(memory_space=pltpu.HBM)],
+        out_specs=(vmem,) * 4,
+        scratch_shapes=[pltpu.SemaphoreType.DMA(())],
         compiler_params=pltpu.CompilerParams(vmem_limit_bytes=46 * 2**20),
         name="setup",
-    )(place, lower, inverse, pivot)
-
-
-def solve_kernel(hop, relays, place_ref, settled_ref, rhs_ref, acc_ref, near_ref, inv_ref, urgent_ref, mine_in, before_in, *refs):
-    del settled_ref
+    )(place, lower)
+
+
+def first_kernel(place_ref, rhs_ref, inv_ref, out_ref, mine_ref):
+    shots = out_ref.shape[1]
+
+    @pl.when(place_ref[0] != 0)
+    def _():
+        out_ref[...] = jnp.zeros_like(out_ref)
+        mine_ref[...] = jnp.zeros_like(mine_ref)
+
+    @pl.when(place_ref[0] == 0)
+    def _():
+        term = apply_columns(stacked(rhs_ref[0]), inv_ref[0, 0], inv_ref[0, 1]).astype(BF16)
+        for ref in (out_ref, mine_ref):
+            ref[0] = term[:shots]
+            ref[1] = term[shots:]
+
+
+def solve_first(place, rhs, inv):
+    vmem = pl.BlockSpec(memory_space=pltpu.VMEM)
+    return pl.pallas_call(
+        first_kernel,
+        out_shape=(pltpu.VMEM(rhs.shape[1:], BF16),) * 2,
+        in_specs=[pl.BlockSpec(memory_space=pltpu.SMEM), vmem, vmem],
+        out_specs=(vmem,) * 2,
+        compiler_params=pltpu.CompilerParams(vmem_limit_bytes=16 * 2**20),
+        name="solve_0",
+    )(place, rhs, inv)
+
+
+def solve_kernel(hop, relays, settled, place_ref, *refs):
+    rhs_ref, acc_ref, near_ref, inv_ref, urgent_ref, mine_in, before_in, *refs = refs[settled:]
     relay_refs, (out_ref, mine_ref, before_ref) = refs[: len(relays)], refs[len(relays) :]
     place = place_ref[0]
     shots = out_ref.shape[1]
@@ -176,11 +202,9 @@
 
     @pl.when(place == hop)
     def _():
-        residual = stacked(rhs_ref[...]).astype(F32)
-        if hop > 0:
-            residual = residual - stacked(acc_ref[...])
-            residual = residual - apply_rows(stacked(urgent_ref[...]), near_ref[0], near_ref[1])
-        term = apply_columns(residual.astype(BF16), inv_ref[0], inv_ref[1]).astype(BF16)
+        residual = stacked(rhs_ref[0]).astype(F32) - stacked(acc_ref[...])
+        residual = residual - apply_rows(stacked(urgent_ref[...]), near_ref[0], near_ref[1])
+        term = apply_columns(residual.astype(BF16), inv_ref[0, 0], inv_ref[0, 1]).astype(BF16)
         for ref in (out_ref, mine_ref):
             ref[0] = term[:shots]
             ref[1] = term[shots:]
@@ -193,19 +217,23 @@
     block = pltpu.VMEM(mine.shape, BF16)
     args = [rhs, acc, near, inv, urgent, mine, before, *relays.values()]
     return pl.pallas_call(
-        functools.partial(solve_kernel, hop, tuple(relays)),
+        functools.partial(solve_kernel, hop, tuple(relays), len(settled)),
         out_shape=(block,) * 3,
-        in_specs=[smem, pl.BlockSpec(memory_space=pl.ANY)] + [vmem] * len(args),
+        in_specs=[smem] + [pl.BlockSpec(memory_space=pl.ANY)] * len(settled) + [vmem] * len(args),
         out_specs=(vmem,) * 3,
         compiler_params=pltpu.CompilerParams(vmem_limit_bytes=16 * 2**20),
         name=f"solve_{hop}",
-    )(place, settled, *args)
-
-
-def gather_kernel(arrivals, left, place_ref, *refs):
+    )(place, *settled, *args)
+
+
+def gather_kernel(arrivals, left, final, place_ref, *refs):
     count = len(arrivals)
     parts = refs[:count]
-    panel_ref, acc_in, acc_ref, buf, sems = refs[count:]
+    refs = refs[count:]
+    if final:
+        panel_ref, acc_in, rhs_ref, out_ref, buf, sems, acc_ref = refs
+    else:
+        panel_ref, acc_in, acc_ref, buf, sems = refs
     width = buf.shape[-1]
     shots = acc_ref.shape[1]
     place = place_ref[0]
@@ -237,49 +265,69 @@
             acc_ref[0] += product[:shots]
             acc_ref[1] += product[shots:]
 
-
-def pick_kernel(places, place_ref, *refs):
-    out_ref = refs[-1]
-
-    for p, ref in zip(places, refs):
-
-        @pl.when(place_ref[0] == p)
-        def _(ref=ref):
-            out_ref[...] = ref[...]
-
-
-def pick(name, place, values, default):
-    count = lax.axis_size("panel")
-    vmem = pl.BlockSpec(memory_space=pltpu.VMEM)
-    args = [values.get(p, default) for p in range(count)]
-    return pl.pallas_call(
-        functools.partial(pick_kernel, tuple(range(count))),
-        out_shape=pltpu.VMEM(default.shape, default.dtype),
-        in_specs=[pl.BlockSpec(memory_space=pltpu.SMEM)] + [vmem] * count,
-        out_specs=vmem,
-        compiler_params=pltpu.CompilerParams(vmem_limit_bytes=16 * 2**20),
-        name=name,
-    )(place, *args)
-
-
-def accumulate(name, left, place, items, panel, acc):
+    if final:
+        out_ref[...] = (rhs_ref[0].astype(F32) - acc_ref[...]).astype(BF16)
+
+
+def accumulate(name, left, place, items, panel, acc, rhs=None):
     items = [item for item in items if not left or any(0 <= block < p for p, block in enumerate(item[1]))]
     if not items:
         return acc
     parts = [item[0] for item in items]
     count = len(parts)
+    final = rhs is not None
     vmem = pl.BlockSpec(memory_space=pltpu.VMEM)
     hbm = pl.BlockSpec(memory_space=pltpu.HBM)
+    scratch = [pltpu.VMEM((count, 2, panel.shape[2], CB), BF16), pltpu.SemaphoreType.DMA((count,))]
     return pl.pallas_call(
-        functools.partial(gather_kernel, [item[1] for item in items], left),
-        out_shape=pltpu.VMEM(acc.shape, F32),
-        in_specs=[pl.BlockSpec(memory_space=pltpu.SMEM)] + [vmem] * count + [hbm, vmem],
+        functools.partial(gather_kernel, [item[1] for item in items], left, final),
+        out_shape=pltpu.VMEM(acc.shape, BF16 if final else F32),
+        in_specs=[pl.BlockSpec(memory_space=pltpu.SMEM)] + [vmem] * count + [hbm, vmem] + [vmem] * final,
         out_specs=vmem,
-        scratch_shapes=[pltpu.VMEM((count, 2, panel.shape[2], CB), BF16), pltpu.SemaphoreType.DMA((count,))],
+        scratch_shapes=scratch + [pltpu.VMEM(acc.shape, F32)] * final,
         input_output_aliases={count + 2: 0} if left else {},
         compiler_params=pltpu.CompilerParams(vmem_limit_bytes=46 * 2**20),
         name=name,
-    )(place, *parts, panel, acc)
+    )(place, *parts, panel, acc, *([rhs] if final else []))
+
+
+def pick_kernel(places, keep, place_ref, settled_ref, *refs):
+    del settled_ref
+    count = len(places)
+    out_ref, sems = refs[count + 1], refs[-1]
+    kept = pltpu.make_async_copy(refs[count], refs[count + 2].at[0], sems.at[1]) if keep else None
+    if keep:
+        kept.start()
+
+    for p, ref in zip(places, refs):
+
+        @pl.when(place_ref[0] == p)
+        def _(ref=ref):
+            copy = pltpu.make_async_copy(ref, out_ref, sems.at[0])
+            copy.start()
+            copy.wait()
+
+    if keep:
+        kept.wait()
+
+
+def pick(name, place, settled, values, default, keep):
+    count = lax.axis_size("panel")
+    vmem = pl.BlockSpec(memory_space=pltpu.VMEM)
+    anywhere = pl.BlockSpec(memory_space=pl.ANY)
+    args = [values.get(p, default) for p in range(count)] + [default]
+    out_shape = [pltpu.VMEM(default.shape, default.dtype)]
+    if keep:
+        out_shape.append(jax.ShapeDtypeStruct((1, *default.shape), default.dtype))
+    return pl.pallas_call(
+        functools.partial(pick_kernel, tuple(range(count)), keep),
+        out_shape=out_shape,
+        in_specs=[pl.BlockSpec(memory_space=pltpu.SMEM)] + [anywhere] * (1 + len(args)),
+        out_specs=[vmem] + [anywhere] * keep,
+        scratch_shapes=[pltpu.SemaphoreType.DMA((2,))],
+        compiler_params=pltpu.CompilerParams(vmem_limit_bytes=16 * 2**20),
+        name=name,
+    )(place, settled, *args)
 
 
 def place_kernel(own_ref, other_ref, own_hot_ref, other_hot_ref, *out_refs):
@@ -340,21 +388,29 @@
 
     place_ref = jnp.reshape(place, (1,))
     own_hot, other_hot = placements(row_maps, place, count, upd_rows)
-    near, inv, rhs, acc_l, acc_u, mine, before = setup(place_ref, lower_panel, inverse_cols, pivot_rhs)
-    urgent = mine
+    near, acc_l, acc_u, before = setup(place_ref, lower_panel, shots)
+    passed, mine = solve_first(place_ref, pivot_rhs, inverse_cols)
+    urgent = None
     came = []
     settled = [acc_u, acc_u]
     for hop in range(count):
         relays = {p: came[earlier][i] for p, (earlier, i) in RELAY.get(hop, {}).items()}
-        passed, mine, before = solve(hop, place_ref, settled[hop], rhs, acc_l, near, inv, urgent, mine, before, relays)
+        if hop:
+            after = [settled[hop]]
+            passed, mine, before = solve(
+                hop, place_ref, after, pivot_rhs, acc_l, near, inverse_cols, urgent, mine, before, relays
+            )
         parts = [(mine, [hop if p == hop else -1 for p in range(count)])]
         if hop:
             parts.append((urgent, chain_rows[hop - 1]))
-            parts += zip(came[hop - 1], spread_rows[hop - 1])
+        for earlier in range(hop):
+            for i, (_, _, use) in enumerate(SPREAD[earlier]):
+                if use == hop:
+                    parts.append((came[earlier][i], spread_rows[earlier][i]))
         if hop < len(CHAIN):
             urgent = send(passed, CHAIN[hop])
         came.append([])
-        for value, edges in SPREAD[hop]:
+        for value, edges, _ in SPREAD[hop]:
             if value not in (OWN, PREV):
                 value = came[value[0]][value[1]]
             else:
@@ -365,23 +421,23 @@
         acc_u = accumulate(f"update_{hop}", False, place_ref, parts, update_panel, acc_u)
         settled.append(acc_u)
 
-    def cross(name, blocks):
+    def cross(name, settled, blocks, keep):
         values = {}
         for earlier, rows in enumerate(spread_rows):
             for i, row in enumerate(rows):
                 for p in range(count):
                     if row[p] == blocks[p % 2]:
                         values[p] = came[earlier][i]
-        return send(pick(name, place_ref, values, mine), SWAP)
-
-    first = cross("pick_first", (count - 2, count - 3))
-    second = cross("pick_second", (None, count - 1))
+        value, *kept = pick(name, place_ref, settled, values, mine, keep)
+        return (send(value, SWAP), *kept)
+
+    first, solved = cross("pick_first", settled[count], (count - 2, count - 3), True)
+    (second,) = cross("pick_second", settled[count + 1], (None, count - 1), False)
     parts = [(came[-1][i], row) for i, row in enumerate(spread_rows[-1])]
     parts.append((first, swap_rows[0]))
     acc_u = accumulate("update_late", False, place_ref, parts, update_panel, acc_u)
     parts = [(second, swap_rows[1])]
-    acc_u = accumulate("update_last", False, place_ref, parts, update_panel, acc_u)
-    child = (update_rhs[0].astype(F32) - acc_u).astype(BF16)
+    child = accumulate("update_last", False, place_ref, parts, update_panel, acc_u, update_rhs)
     other = send(child, SWAP)
     placed = place_rows(child, other, own_hot, other_hot)
     sums = [placed[0].astype(F32), placed[1].astype(F32)]
@@ -395,7 +451,7 @@
     given = jnp.where(odd_front, sums[0], sums[1]).astype(BF16)
     sibling = lax.ppermute(given, "front", [(f, f ^ 1) for f in range(lax.axis_size("front"))])
     parent_out = parent_rhs[0] + kept + sibling.astype(F32)
-    return (mine[None], parent_out[None])
+    return (solved, parent_out[None])
 
 
 def select_rows(block_rows, index_map, base, owned):

time: 143 us -> 139 us (0.972)
  Pallas kernels: 23 us -> 20.6 us
    ppermute x40, waiting for transfers between devices: 52.8 us -> 50.7 us  [send(): return lax.ppermute(value, 'panel', edges)]
    pallas_call x16, Pallas kernels: 16.8 us -> 15.3 us  [accumulate(): pl.pallas_call(functools.partial(gather_kernel, [item[1] for item in item...]
    unnamed x17 -> x20, local copies, waits for them, and re-layouts: 4.54 us -> 4.79 us
  transfers between devices with their start and end apart: 41 -> 41, of which waited for: 12 -> 14; matrix products, arithmetic and copies ran while one was open for 2% -> 1% of each run, Pallas kernels for 12% -> 12%
where the time goes in v4:
time: 139 us; the launch traced here: 137 us
  starting transfers between devices  54.5 us (39%)
  waiting for transfers between devices  52.2 us (38%)
  Pallas kernels  20.6 us (15%)
  local copies, waits for them, and re-layouts  5.73 us (4%)
  other arithmetic  2.45 us (2%)
    ppermute x40, starting transfers between devices, send(): return lax.ppermute(value, 'panel', edges)  54.4 us
    ppermute x40, waiting for transfers between devices, send(): return lax.ppermute(value, 'panel', edges)  50.7 us
    pallas_call x16, Pallas kernels, accumulate(): pl.pallas_call(functools.partial(gather_kernel, [item[1] for item in item...  15.3 us
    unnamed x20, local copies, waits for them, and re-layouts  4.79 us
  transfers between devices with their start and end apart: 41, of which 14 were waited for; matrix products, arithmetic and copies ran while one was open for 1% of the time, Pallas kernels for 12%

profile of v4, /device:TPU:0, one launch (start us, length us, event | category | flops | bytes accessed | tf_op | source)
XLA Modules:
  0.0 136.8 jit_solution(10296808580681807262)
XLA Ops:
  0.6 1.2 copy-done
  1.9 0.9 copy-done.2
  3.3 2.6 %collective-permute-start = (bf16[2,128,512]{2,1,0:T(8,128)(2,1)S(1)}, bf16[2,128,512]{2,1,0:T(8,128)(2,1)S(1)}, u32[]{:S(2)}, u32[]{:S(2)}) collective-permute-start(bf16[2,128,512]{2,1,0:T(8,128)(2,1)S(1)} %get-tuple-element.36), channel_id=1, source_target_pairs={{0,1},{1,0},{2,3},{3,2},{4,5},{5,4},{6,7},{7,6},{8,9},{9,8},{10,11... | collective-permute-start | bytes 786440 | tf_op jit(solution)/shard_map/ppermute | solution.py:387
  5.9 3.6 %collective-permute-start.3 = (bf16[2,128,512]{2,1,0:T(8,128)(2,1)S(1)}, bf16[2,128,512]{2,1,0:T(8,128)(2,1)S(1)}, u32[]{:S(2)}, u32[]{:S(2)}) collective-permute-start(bf16[2,128,512]{2,1,0:T(8,128)(2,1)S(1)} %get-tuple-element.34.refs_0_.refs_6_), channel_id=1, source_target_pairs={{0,2},{8,10},{16,18},{24,26}} | collective-permute-start | bytes 786440 | tf_op jit(solution)/shard_map/ppermute | solution.py:387
  9.5 1.7 %collective-permute-start.2 = (bf16[2,128,512]{2,1,0:T(8,128)(2,1)S(1)}, bf16[2,128,512]{2,1,0:T(8,128)(2,1)S(1)}, u32[]{:S(2)}, u32[]{:S(2)}) collective-permute-start(bf16[2,128,512]{2,1,0:T(8,128)(2,1)S(1)} %get-tuple-element.34.refs_0_.refs_6_), channel_id=1, source_target_pairs={{0,4},{8,12},{16,20},{24,28}} | collective-permute-start | bytes 786440 | tf_op jit(solution)/shard_map/ppermute | solution.py:387
  11.2 1.7 %collective-permute-start.1 = (bf16[2,128,512]{2,1,0:T(8,128)(2,1)S(1)}, bf16[2,128,512]{2,1,0:T(8,128)(2,1)S(1)}, u32[]{:S(2)}, u32[]{:S(2)}) collective-permute-start(bf16[2,128,512]{2,1,0:T(8,128)(2,1)S(1)} %get-tuple-element.34.refs_0_.refs_6_), channel_id=1, source_target_pairs={{0,6},{8,14},{16,22},{24,30}} | collective-permute-start | bytes 786440 | tf_op jit(solution)/shard_map/ppermute | solution.py:387
  12.9 1.3 setup.1
  14.8 1.7 %update_0.1.refs_0_.refs_6_ = f32[2,128,512]{2,1,0:T(8,128)S(1)} custom-call(s32[1]{0:T(128)} %bitcast.place_ref, bf16[2,128,512]{2,1,0:T(8,128)(2,1)S(1)} %get-tuple-element.34.refs_0_.refs_6_, bf16[1,2,512,4096]{3,2,1,0:T(8,128)(2,1)} %refs_1_.17, f32[2,128,512]{2,1,0:T(8,128)S(1)} %get-tuple-element.35.refs_2_.refs_0_), custom_call_target="tpu_custom_call" | custom-call | tf_op jit(solution)/shard_map/update_0/pallas_call | solution.py:282
  17.9 3.9 %collective-permute-done.2.refs_2_.refs_8_.refs_3_ = bf16[2,128,512]{2,1,0:T(8,128)(2,1)S(1)} collective-permute-done((bf16[2,128,512]{2,1,0:T(8,128)(2,1)S(1)}, bf16[2,128,512]{2,1,0:T(8,128)(2,1)S(1)}, u32[]{:S(2)}, u32[]{:S(2)}) %collective-permute-start.2) | collective-permute-done | bytes 262176 | tf_op jit(solution)/shard_map/ppermute | solution.py:387
  22.5 3.5 %collective-permute-done.1.refs_1_.refs_9_.refs_2_ = bf16[2,128,512]{2,1,0:T(8,128)(2,1)S(1)} collective-permute-done((bf16[2,128,512]{2,1,0:T(8,128)(2,1)S(1)}, bf16[2,128,512]{2,1,0:T(8,128)(2,1)S(1)}, u32[]{:S(2)}, u32[]{:S(2)}) %collective-permute-start.1) | collective-permute-done | bytes 262176 | tf_op jit(solution)/shard_map/ppermute | solution.py:387
  28.6 5.2 %collective-permute-done.9.refs_0_.refs_5_.refs_1_ = bf16[2,128,512]{2,1,0:T(8,128)(2,1)S(1)} collective-permute-done((bf16[2,128,512]{2,1,0:T(8,128)(2,1)S(1)}, bf16[2,128,512]{2,1,0:T(8,128)(2,1)S(1)}, u32[]{:S(2)}, u32[]{:S(2)}) %collective-permute-start.9) | collective-permute-done | bytes 262176 | tf_op jit(solution)/shard_map/ppermute | solution.py:387
  33.9 3.6 %collective-permute-start.12 = (bf16[2,128,512]{2,1,0:T(8,128)(2,1)S(1)}, bf16[2,128,512]{2,1,0:T(8,128)(2,1)S(1)}, u32[]{:S(2)}, u32[]{:S(2)}) collective-permute-start(bf16[2,128,512]{2,1,0:T(8,128)(2,1)S(1)} %get-tuple-element.46), channel_id=1, source_target_pairs={{3,4},{4,5},{5,2},{2,3},{0,1},{1,0},{6,7},{7,6},{11,12},{12,13},{1... | collective-permute-start | bytes 786440 | tf_op jit(solution)/shard_map/ppermute | solution.py:387
  39.1 3.7 %collective-permute-done.12.refs_5_.refs_1_.refs_0_ = bf16[2,128,512]{2,1,0:T(8,128)(2,1)S(1)} collective-permute-done((bf16[2,128,512]{2,1,0:T(8,128)(2,1)S(1)}, bf16[2,128,512]{2,1,0:T(8,128)(2,1)S(1)}, u32[]{:S(2)}, u32[]{:S(2)}) %collective-permute-start.12) | collective-permute-done | bytes 262176 | tf_op jit(solution)/shard_map/ppermute | solution.py:387
  42.8 1.8 %collective-permute-start.15 = (bf16[2,128,512]{2,1,0:T(8,128)(2,1)S(1)}, bf16[2,128,512]{2,1,0:T(8,128)(2,1)S(1)}, u32[]{:S(2)}, u32[]{:S(2)}) collective-permute-start(bf16[2,128,512]{2,1,0:T(8,128)(2,1)S(1)} %get-tuple-element.50), channel_id=1, source_target_pairs={{0,1},{1,0},{2,3},{3,2},{4,5},{5,4},{6,7},{7,6},{8,9},{9,8},{10,11... | collective-permute-start | bytes 786440 | tf_op jit(solution)/shard_map/ppermute | solution.py:387
  46.7 1.8 %update_3.1.refs_5_.refs_0_ = f32[2,128,512]{2,1,0:T(8,128)S(1)} custom-call(s32[1]{0:T(128)} %bitcast.place_ref, bf16[2,128,512]{2,1,0:T(8,128)(2,1)S(1)} %get-tuple-element.47.refs_6_.refs_0_, bf16[2,128,512]{2,1,0:T(8,128)(2,1)S(1)} %collective-permute-done.9.refs_0_.refs_5_.refs_1_, bf16[2,128,512]{2,1,0:T(8,128)(2,1)S(1)} %collective-permute-done.10.refs_1_.refs_2_, ...), custom_call_target="tpu_custom_call" | custom-call | tf_op jit(solution)/shard_map/update_3/pallas_call | solution.py:282
  48.6 0.9 collective-permute-done.15.refs_0_.refs_5_.refs_1_
  49.6 2.0 %collective-permute-start.19 = (bf16[2,128,512]{2,1,0:T(8,128)(2,1)S(1)}, bf16[2,128,512]{2,1,0:T(8,128)(2,1)S(1)}, u32[]{:S(2)}, u32[]{:S(2)}) collective-permute-start(bf16[2,128,512]{2,1,0:T(8,128)(2,1)S(1)} %get-tuple-element.52), channel_id=1, source_target_pairs={{5,6},{6,7},{7,4},{4,5},{0,1},{1,0},{2,3},{3,2},{13,14},{14,15},{1... | collective-permute-start | bytes 786440 | tf_op jit(solution)/shard_map/ppermute | solution.py:387
  52.3 1.3 collective-permute-start.20
  53.6 1.3 collective-permute-start.25
  57.3 13.8 %collective-permute-done.20.refs_8_.refs_6_.refs_1_ = bf16[2,128,512]{2,1,0:T(8,128)(2,1)S(1)} collective-permute-done((bf16[2,128,512]{2,1,0:T(8,128)(2,1)S(1)}, bf16[2,128,512]{2,1,0:T(8,128)(2,1)S(1)}, u32[]{:S(2)}, u32[]{:S(2)}) %collective-permute-start.20) | collective-permute-done | bytes 262176 | tf_op jit(solution)/shard_map/ppermute | solution.py:387
  71.5 3.6 %collective-permute-start.26 = (bf16[2,128,512]{2,1,0:T(8,128)(2,1)S(1)}, bf16[2,128,512]{2,1,0:T(8,128)(2,1)S(1)}, u32[]{:S(2)}, u32[]{:S(2)}) collective-permute-start(bf16[2,128,512]{2,1,0:T(8,128)(2,1)S(1)} %collective-permute-done.25.refs_4_), channel_id=1, source_target_pairs={{0,1},{1,0},{8,9},{9,8},{16,17},{17,16},{24,25},{25,24}} | collective-permute-start | bytes 786440 | tf_op jit(solution)/shard_map/ppermute | solution.py:387
  75.9 1.8 %update_5.1.refs_9_.refs_0_ = f32[2,128,512]{2,1,0:T(8,128)S(1)} custom-call(s32[1]{0:T(128)} %bitcast.place_ref, bf16[2,128,512]{2,1,0:T(8,128)(2,1)S(1)} %get-tuple-element.53.refs_6_.refs_0_, bf16[2,128,512]{2,1,0:T(8,128)(2,1)S(1)} %collective-permute-done.15.refs_0_.refs_5_.refs_1_, bf16[2,128,512]{2,1,0:T(8,128)(2,1)S(1)} %collective-permute-done.16.refs_1_.refs_2_, ...), custom_call_target="tpu_custom_call" | custom-call | tf_op jit(solution)/shard_map/update_5/pallas_call | solution.py:282
  78.4 1.3 collective-permute-start.27
  79.8 0.9 solve_7.1
  80.7 1.4 collective-permute-start.33
  82.6 0.7 copy-done.7
  83.3 1.4 %collective-permute-start.32 = (bf16[2,128,512]{2,1,0:T(8,128)(2,1)S(1)}, bf16[2,128,512]{2,1,0:T(8,128)(2,1)}, u32[]{:S(2)}, u32[]{:S(2)}) collective-permute-start(bf16[2,128,512]{2,1,0:T(8,128)(2,1)S(1)} %get-tuple-element.58.refs_5_.refs_6_.refs_8_.refs_0_.refs_2_.refs_4_.refs_7_), channel_id=1, source_target_pairs={{7,3},{15,11},{23,19},{31,27}} | collective-permute-start | bytes 786440 | tf_op jit(solution)/shard_map/ppermute | solution.py:387
  84.6 1.4 %collective-permute-start.31 = (bf16[2,128,512]{2,1,0:T(8,128)(2,1)S(1)}, bf16[2,128,512]{2,1,0:T(8,128)(2,1)}, u32[]{:S(2)}, u32[]{:S(2)}) collective-permute-start(bf16[2,128,512]{2,1,0:T(8,128)(2,1)S(1)} %get-tuple-element.58.refs_5_.refs_6_.refs_8_.refs_0_.refs_2_.refs_4_.refs_7_), channel_id=1, source_target_pairs={{7,1},{15,9},{23,17},{31,25}} | collective-permute-start | bytes 786440 | tf_op jit(solution)/shard_map/ppermute | solution.py:387
  86.0 0.9 copy-done.5
  87.0 0.9 copy-done.8
  87.9 2.5 %update_6.1.settled_ref.refs_6_ = f32[2,128,512]{2,1,0:T(8,128)S(1)} custom-call(s32[1]{0:T(128)} %bitcast.place_ref, bf16[2,128,512]{2,1,0:T(8,128)(2,1)S(1)} %get-tuple-element.55.refs_0_.refs_6_, bf16[2,128,512]{2,1,0:T(8,128)(2,1)S(1)} %collective-permute-done.19.refs_5_.refs_1_.refs_0_, ...), custom_call_target="tpu_custom_call" | custom-call | tf_op jit(solution)/shard_map/update_6/pallas_call | solution.py:282
  90.4 0.7 collective-permute-done.27.refs_0_.refs_4_
  91.1 0.7 pick_first.1
  92.0 1.8 %update_7.1.settled_ref.refs_5_ = f32[2,128,512]{2,1,0:T(8,128)S(1)} custom-call(s32[1]{0:T(128)} %bitcast.place_ref, bf16[2,128,512]{2,1,0:T(8,128)(2,1)S(1)} %get-tuple-element.58.refs_5_.refs_6_.refs_8_.refs_0_.refs_2_.refs_4_.refs_7_, bf16[2,128,512]{2,1,0:T(8,128)(2,1)S(1)} %collective-permute-done.30.refs_5_.refs_1_, ...), custom_call_target="tpu_custom_call" | custom-call | tf_op jit(solution)/shard_map/update_7/pallas_call | solution.py:282
  93.9 7.9 %collective-permute-start.34 = (bf16[2,128,512]{2,1,0:T(8,128)(2,1)S(1)}, bf16[2,128,512]{2,1,0:T(8,128)(2,1)S(1)}, u32[]{:S(2)}, u32[]{:S(2)}) collective-permute-start(bf16[2,128,512]{2,1,0:T(8,128)(2,1)S(1)} %pick_second.1), channel_id=1, source_target_pairs={{0,1},{1,0},{2,3},{3,2},{4,5},{5,4},{6,7},{7,6},{8,9},{9,8},{10,11... | collective-permute-start | bytes 786440 | tf_op jit(solution)/shard_map/ppermute | solution.py:387
  101.8 0.9 fusion.8
  102.9 2.9 %update_late.1.refs_2_ = f32[2,128,512]{2,1,0:T(8,128)S(1)} custom-call(s32[1]{0:T(128)} %bitcast.place_ref, bf16[2,128,512]{2,1,0:T(8,128)(2,1)} %collective-permute-done.33.refs_5_.refs_0_, bf16[2,128,512]{2,1,0:T(8,128)(2,1)} %collective-permute-done.32.refs_3_.refs_1_, bf16[2,128,512]{2,1,0:T(8,128)(2,1)} %collective-permute-done.31.refs_1_.refs_2_, ...), custom_call_target="tpu_custom_call" | custom-call | tf_op jit(solution)/shard_map/update_late/pallas_call | solution.py:282
  105.8 2.5 %collective-permute-done.34.refs_0_ = bf16[2,128,512]{2,1,0:T(8,128)(2,1)S(1)} collective-permute-done((bf16[2,128,512]{2,1,0:T(8,128)(2,1)S(1)}, bf16[2,128,512]{2,1,0:T(8,128)(2,1)S(1)}, u32[]{:S(2)}, u32[]{:S(2)}) %collective-permute-start.34) | collective-permute-done | bytes 262176 | tf_op jit(solution)/shard_map/ppermute | solution.py:387
  108.3 1.8 %update_last.1.own_ref = bf16[2,128,512]{2,1,0:T(8,128)(2,1)S(1)} custom-call(s32[1]{0:T(128)} %bitcast.place_ref, bf16[2,128,512]{2,1,0:T(8,128)(2,1)S(1)} %collective-permute-done.34.refs_0_, bf16[1,2,512,4096]{3,2,1,0:T(8,128)(2,1)} %refs_1_.17, f32[2,128,512]{2,1,0:T(8,128)S(1)} %update_late.1.refs_2_, bf16[1,2,128,512]{3,2,1,0:T(8,128)(2,1)S(1)} %copy-done.6), custom_call_target="tpu_custom_call" | custom-call | tf_op jit(solution)/shard_map/update_last/pallas_call | solution.py:282
  110.1 0.9 collective-permute-start.36
  110.9 0.9 compare_convert_fusion
  111.9 4.6 %collective-permute-done.36.other_ref = bf16[2,128,512]{2,1,0:T(8,128)(2,1)S(1)} collective-permute-done((bf16[2,128,512]{2,1,0:T(8,128)(2,1)S(1)}, bf16[2,128,512]{2,1,0:T(8,128)(2,1)S(1)}, u32[]{:S(2)}, u32[]{:S(2)}) %collective-permute-start.36) | collective-permute-done | bytes 262176 | tf_op jit(solution)/shard_map/ppermute | solution.py:387
  116.5 1.5 %place_rows.1 = (bf16[2,128,512]{2,1,0:T(8,128)(2,1)S(1)}, bf16[2,128,512]{2,1,0:T(8,128)(2,1)S(1)}, bf16[2,128,512]{2,1,0:T(8,128)(2,1)S(1)}, bf16[2,128,512]{2,1,0:T(8,128)(2,1)S(1)}, bf16[2,128,512]{2,1,0:T(8,128)(2,1)S(1)}) custom-call(bf16[2,128,512]{2,1,0:T(8,128)(2,1)S(1)} %update_last.1.own_ref, ...), custom_call_target="tpu_custom_call" | custom-call | tf_op jit(solution)/shard_map/place_rows/pallas_call | solution.py:350
  118.2 4.3 %collective-permute-start.39 = (bf16[2,128,512]{2,1,0:T(8,128)(2,1)S(1)}, bf16[2,128,512]{2,1,0:T(8,128)(2,1)S(1)}, u32[]{:S(2)}, u32[]{:S(2)}) collective-permute-start(bf16[2,128,512]{2,1,0:T(8,128)(2,1)S(1)} %get-tuple-element.64), channel_id=1, source_target_pairs={{0,6},{1,7},{2,4},{3,5},{4,2},{5,3},{6,0},{7,1},{8,14},{9,15},{10,... | collective-permute-start | bytes 786440 | tf_op jit(solution)/shard_map/ppermute | solution.py:387
  122.5 3.4 %collective-permute-done.37 = bf16[2,128,512]{2,1,0:T(8,128)(2,1)S(1)} collective-permute-done((bf16[2,128,512]{2,1,0:T(8,128)(2,1)S(1)}, bf16[2,128,512]{2,1,0:T(8,128)(2,1)S(1)}, u32[]{:S(2)}, u32[]{:S(2)}) %collective-permute-start.37) | collective-permute-done | bytes 262176 | tf_op jit(solution)/shard_map/ppermute | solution.py:387
  125.9 7.8 %collective-permute-done.38 = bf16[2,128,512]{2,1,0:T(8,128)(2,1)S(1)} collective-permute-done((bf16[2,128,512]{2,1,0:T(8,128)(2,1)S(1)}, bf16[2,128,512]{2,1,0:T(8,128)(2,1)S(1)}, u32[]{:S(2)}, u32[]{:S(2)}) %collective-permute-start.38) | collective-permute-done | bytes 262176 | tf_op jit(solution)/shard_map/ppermute | solution.py:387
  134.1 1.5 %collective-permute-done.40 = bf16[2,128,512]{2,1,0:T(8,128)(2,1)S(1)} collective-permute-done((bf16[2,128,512]{2,1,0:T(8,128)(2,1)S(1)}, bf16[2,128,512]{2,1,0:T(8,128)(2,1)S(1)}, u32[]{:S(2)}, u32[]{:S(2)}) %collective-permute-start.40) | collective-permute-done | bytes 262176 | tf_op jit(solution)/shard_map/ppermute | solution.py:452
  135.6 1.2 fusion.7
  (88 shorter events, 15.9 us)
Async XLA Ops:
  0.6 1.2 copy-start
  1.9 0.9 copy-start.2
  3.3 11.0 %collective-permute-start = (bf16[2,128,512]{2,1,0:T(8,128)(2,1)S(1)}, bf16[2,128,512]{2,1,0:T(8,128)(2,1)S(1)}, u32[]{:S(2)}, u32[]{:S(2)}) collective-permute-start(bf16[2,128,512]{2,1,0:T(8,128)(2,1)S(1)} %get-tuple-element.36), channel_id=1, source_target_pairs={{0,1},{1,0},{2,3},{3,2},{4,5},{5,4},{6,7},{7,6},{8,9},{9,8},{10,11... | collective-permute-start | bytes 786440 | tf_op jit(solution)/shard_map/ppermute | solution.py:387
  5.9 8.4 %copy-start.1 = (bf16[1,2,512,512]{3,2,1,0:T(8,128)(2,1)S(1)}, bf16[1,2,512,512]{3,2,1,0:T(8,128)(2,1)}, u32[]{:S(2)}) copy-start(bf16[1,2,512,512]{3,2,1,0:T(8,128)(2,1)} %refs_4_.24) | copy-start | bytes 3145732
  5.9 8.4 %copy-start.3 = (bf16[1,2,128,512]{3,2,1,0:T(8,128)(2,1)S(1)}, bf16[1,2,128,512]{3,2,1,0:T(8,128)(2,1)}, u32[]{:S(2)}) copy-start(bf16[1,2,128,512]{3,2,1,0:T(8,128)(2,1)} %refs_1_.16) | copy-start | bytes 786436
  5.9 11.4 %collective-permute-start.3 = (bf16[2,128,512]{2,1,0:T(8,128)(2,1)S(1)}, bf16[2,128,512]{2,1,0:T(8,128)(2,1)S(1)}, u32[]{:S(2)}, u32[]{:S(2)}) collective-permute-start(bf16[2,128,512]{2,1,0:T(8,128)(2,1)S(1)} %get-tuple-element.34.refs_0_.refs_6_), channel_id=1, source_target_pairs={{0,2},{8,10},{16,18},{24,26}} | collective-permute-start | bytes 786440 | tf_op jit(solution)/shard_map/ppermute | solution.py:387
  9.5 12.3 %collective-permute-start.2 = (bf16[2,128,512]{2,1,0:T(8,128)(2,1)S(1)}, bf16[2,128,512]{2,1,0:T(8,128)(2,1)S(1)}, u32[]{:S(2)}, u32[]{:S(2)}) collective-permute-start(bf16[2,128,512]{2,1,0:T(8,128)(2,1)S(1)} %get-tuple-element.34.refs_0_.refs_6_), channel_id=1, source_target_pairs={{0,4},{8,12},{16,20},{24,28}} | collective-permute-start | bytes 786440 | tf_op jit(solution)/shard_map/ppermute | solution.py:387
  11.2 14.8 %collective-permute-start.1 = (bf16[2,128,512]{2,1,0:T(8,128)(2,1)S(1)}, bf16[2,128,512]{2,1,0:T(8,128)(2,1)S(1)}, u32[]{:S(2)}, u32[]{:S(2)}) collective-permute-start(bf16[2,128,512]{2,1,0:T(8,128)(2,1)S(1)} %get-tuple-element.34.refs_0_.refs_6_), channel_id=1, source_target_pairs={{0,6},{8,14},{16,22},{24,30}} | collective-permute-start | bytes 786440 | tf_op jit(solution)/shard_map/ppermute | solution.py:387
  14.3 12.5 %collective-permute-start.4 = (bf16[2,128,512]{2,1,0:T(8,128)(2,1)S(1)}, bf16[2,128,512]{2,1,0:T(8,128)(2,1)S(1)}, u32[]{:S(2)}, u32[]{:S(2)}) collective-permute-start(bf16[2,128,512]{2,1,0:T(8,128)(2,1)S(1)} %get-tuple-element.40), channel_id=1, source_target_pairs={{1,2},{2,3},{3,0},{0,1},{4,5},{5,4},{6,7},{7,6},{9,10},{10,11},{11... | collective-permute-start | bytes 786440 | tf_op jit(solution)/shard_map/ppermute | solution.py:387
  16.6 11.2 %collective-permute-start.8 = (bf16[2,128,512]{2,1,0:T(8,128)(2,1)S(1)}, bf16[2,128,512]{2,1,0:T(8,128)(2,1)S(1)}, u32[]{:S(2)}, u32[]{:S(2)}) collective-permute-start(bf16[2,128,512]{2,1,0:T(8,128)(2,1)S(1)} %get-tuple-element.41.refs_6_.refs_0_), channel_id=1, source_target_pairs={{1,3},{9,11},{17,19},{25,27}} | collective-permute-start | bytes 786440 | tf_op jit(solution)/shard_map/ppermute | solution.py:387
  17.3 9.8 %collective-permute-start.7 = (bf16[2,128,512]{2,1,0:T(8,128)(2,1)S(1)}, bf16[2,128,512]{2,1,0:T(8,128)(2,1)S(1)}, u32[]{:S(2)}, u32[]{:S(2)}) collective-permute-start(bf16[2,128,512]{2,1,0:T(8,128)(2,1)S(1)} %collective-permute-done.3.refs_3_.refs_4_), channel_id=1, source_target_pairs={{2,3},{10,11},{18,19},{26,27}} | collective-permute-start | bytes 786440 | tf_op jit(solution)/shard_map/ppermute | solution.py:387
  21.8 6.6 %collective-permute-start.6 = (bf16[2,128,512]{2,1,0:T(8,128)(2,1)S(1)}, bf16[2,128,512]{2,1,0:T(8,128)(2,1)S(1)}, u32[]{:S(2)}, u32[]{:S(2)}) collective-permute-start(bf16[2,128,512]{2,1,0:T(8,128)(2,1)S(1)} %get-tuple-element.41.refs_6_.refs_0_), channel_id=1, source_target_pairs={{1,5},{9,13},{17,21},{25,29}} | collective-permute-start | bytes 786440 | tf_op jit(solution)/shard_map/ppermute | solution.py:387
  26.0 2.5 %collective-permute-start.5 = (bf16[2,128,512]{2,1,0:T(8,128)(2,1)S(1)}, bf16[2,128,512]{2,1,0:T(8,128)(2,1)S(1)}, u32[]{:S(2)}, u32[]{:S(2)}) collective-permute-start(bf16[2,128,512]{2,1,0:T(8,128)(2,1)S(1)} %get-tuple-element.41.refs_6_.refs_0_), channel_id=1, source_target_pairs={{1,7},{9,15},{17,23},{25,31}} | collective-permute-start | bytes 786440 | tf_op jit(solution)/shard_map/ppermute | solution.py:387
  26.9 6.9 %collective-permute-start.9 = (bf16[2,128,512]{2,1,0:T(8,128)(2,1)S(1)}, bf16[2,128,512]{2,1,0:T(8,128)(2,1)S(1)}, u32[]{:S(2)}, u32[]{:S(2)}) collective-permute-start(bf16[2,128,512]{2,1,0:T(8,128)(2,1)S(1)} %get-tuple-element.44), channel_id=1, source_target_pairs={{0,1},{1,0},{2,3},{3,2},{4,5},{5,4},{6,7},{7,6},{8,9},{9,8},{10,11... | collective-permute-start | bytes 786440 | tf_op jit(solution)/shard_map/ppermute | solution.py:387
  27.1 11.9 %collective-permute-start.10 = (bf16[2,128,512]{2,1,0:T(8,128)(2,1)S(1)}, bf16[2,128,512]{2,1,0:T(8,128)(2,1)S(1)}, u32[]{:S(2)}, u32[]{:S(2)}) collective-permute-start(bf16[2,128,512]{2,1,0:T(8,128)(2,1)S(1)} %get-tuple-element.45.refs_7_), channel_id=1, source_target_pairs={{2,4},{10,12},{18,20},{26,28}} | collective-permute-start | bytes 786440 | tf_op jit(solution)/shard_map/ppermute | solution.py:387
  27.8 10.5 %collective-permute-start.11 = (bf16[2,128,512]{2,1,0:T(8,128)(2,1)S(1)}, bf16[2,128,512]{2,1,0:T(8,128)(2,1)S(1)}, u32[]{:S(2)}, u32[]{:S(2)}) collective-permute-start(bf16[2,128,512]{2,1,0:T(8,128)(2,1)S(1)} %get-tuple-element.43.refs_0_.refs_6_), channel_id=1, source_target_pairs={{2,4},{10,12},{18,20},{26,28}} | collective-permute-start | bytes 786440 | tf_op jit(solution)/shard_map/ppermute | solution.py:387
  33.9 8.9 %collective-permute-start.12 = (bf16[2,128,512]{2,1,0:T(8,128)(2,1)S(1)}, bf16[2,128,512]{2,1,0:T(8,128)(2,1)S(1)}, u32[]{:S(2)}, u32[]{:S(2)}) collective-permute-start(bf16[2,128,512]{2,1,0:T(8,128)(2,1)S(1)} %get-tuple-element.46), channel_id=1, source_target_pairs={{3,4},{4,5},{5,2},{2,3},{0,1},{1,0},{6,7},{7,6},{11,12},{12,13},{1... | collective-permute-start | bytes 786440 | tf_op jit(solution)/shard_map/ppermute | solution.py:387
  37.5 8.5 %collective-permute-start.13 = (bf16[2,128,512]{2,1,0:T(8,128)(2,1)S(1)}, bf16[2,128,512]{2,1,0:T(8,128)(2,1)S(1)}, u32[]{:S(2)}, u32[]{:S(2)}) collective-permute-start(bf16[2,128,512]{2,1,0:T(8,128)(2,1)S(1)} %get-tuple-element.47.refs_6_.refs_0_), channel_id=1, source_target_pairs={{3,5},{2,6},{11,13},{10,14},{19,21},{18,22},{27,29},{26,30}} | collective-permute-start | bytes 786440 | tf_op jit(solution)/shard_map/ppermute | solution.py:387
  38.3 10.2 %collective-permute-start.14 = (bf16[2,128,512]{2,1,0:T(8,128)(2,1)S(1)}, bf16[2,128,512]{2,1,0:T(8,128)(2,1)S(1)}, u32[]{:S(2)}, u32[]{:S(2)}) collective-permute-start(bf16[2,128,512]{2,1,0:T(8,128)(2,1)S(1)} %collective-permute-done.11.refs_2_.refs_3_), channel_id=1, source_target_pairs={{4,5},{12,13},{20,21},{28,29}} | collective-permute-start | bytes 786440 | tf_op jit(solution)/shard_map/ppermute | solution.py:387
  42.8 6.7 %collective-permute-start.15 = (bf16[2,128,512]{2,1,0:T(8,128)(2,1)S(1)}, bf16[2,128,512]{2,1,0:T(8,128)(2,1)S(1)}, u32[]{:S(2)}, u32[]{:S(2)}) collective-permute-start(bf16[2,128,512]{2,1,0:T(8,128)(2,1)S(1)} %get-tuple-element.50), channel_id=1, source_target_pairs={{0,1},{1,0},{2,3},{3,2},{4,5},{5,4},{6,7},{7,6},{8,9},{9,8},{10,11... | collective-permute-start | bytes 786440 | tf_op jit(solution)/shard_map/ppermute | solution.py:387
  44.6 7.6 %collective-permute-start.16 = (bf16[2,128,512]{2,1,0:T(8,128)(2,1)S(1)}, bf16[2,128,512]{2,1,0:T(8,128)(2,1)S(1)}, u32[]{:S(2)}, u32[]{:S(2)}) collective-permute-start(bf16[2,128,512]{2,1,0:T(8,128)(2,1)S(1)} %get-tuple-element.51.refs_7_), channel_id=1, source_target_pairs={{4,6},{12,14},{20,22},{28,30}} | collective-permute-start | bytes 786440 | tf_op jit(solution)/shard_map/ppermute | solution.py:387
  45.3 8.3 %collective-permute-start.17 = (bf16[2,128,512]{2,1,0:T(8,128)(2,1)S(1)}, bf16[2,128,512]{2,1,0:T(8,128)(2,1)S(1)}, u32[]{:S(2)}, u32[]{:S(2)}) collective-permute-start(bf16[2,128,512]{2,1,0:T(8,128)(2,1)S(1)} %get-tuple-element.49.refs_0_.refs_6_), channel_id=1, source_target_pairs={{4,6},{12,14},{20,22},{28,30}} | collective-permute-start | bytes 786440 | tf_op jit(solution)/shard_map/ppermute | solution.py:387
  46.0 8.9 %collective-permute-start.18 = (bf16[2,128,512]{2,1,0:T(8,128)(2,1)S(1)}, bf16[2,128,512]{2,1,0:T(8,128)(2,1)S(1)}, u32[]{:S(2)}, u32[]{:S(2)}) collective-permute-start(bf16[2,128,512]{2,1,0:T(8,128)(2,1)S(1)} %collective-permute-done.13.refs_2_.refs_1_), channel_id=1, source_target_pairs={{5,7},{13,15},{21,23},{29,31}} | collective-permute-start | bytes 786440 | tf_op jit(solution)/shard_map/ppermute | solution.py:387
  49.6 6.4 %collective-permute-start.19 = (bf16[2,128,512]{2,1,0:T(8,128)(2,1)S(1)}, bf16[2,128,512]{2,1,0:T(8,128)(2,1)S(1)}, u32[]{:S(2)}, u32[]{:S(2)}) collective-permute-start(bf16[2,128,512]{2,1,0:T(8,128)(2,1)S(1)} %get-tuple-element.52), channel_id=1, source_target_pairs={{5,6},{6,7},{7,4},{4,5},{0,1},{1,0},{2,3},{3,2},{13,14},{14,15},{1... | collective-permute-start | bytes 786440 | tf_op jit(solution)/shard_map/ppermute | solution.py:387
  51.6 5.1 %collective-permute-start.21 = (bf16[2,128,512]{2,1,0:T(8,128)(2,1)S(1)}, bf16[2,128,512]{2,1,0:T(8,128)(2,1)S(1)}, u32[]{:S(2)}, u32[]{:S(2)}) collective-permute-start(bf16[2,128,512]{2,1,0:T(8,128)(2,1)S(1)} %get-tuple-element.53.refs_6_.refs_0_), channel_id=1, source_target_pairs={{5,3},{4,2},{13,11},{12,10},{21,19},{20,18},{29,27},{28,26}} | collective-permute-start | bytes 786440 | tf_op jit(solution)/shard_map/ppermute | solution.py:387
  52.3 18.8 %collective-permute-start.20 = (bf16[2,128,512]{2,1,0:T(8,128)(2,1)S(1)}, bf16[2,128,512]{2,1,0:T(8,128)(2,1)S(1)}, u32[]{:S(2)}, u32[]{:S(2)}) collective-permute-start(bf16[2,128,512]{2,1,0:T(8,128)(2,1)S(1)} %get-tuple-element.53.refs_6_.refs_0_), channel_id=1, source_target_pairs={{5,1},{4,0},{13,9},{12,8},{21,17},{20,16},{29,25},{28,24}} | collective-permute-start | bytes 786440 | tf_op jit(solution)/shard_map/ppermute | solution.py:387
  53.6 18.0 %collective-permute-start.25 = (bf16[2,128,512]{2,1,0:T(8,128)(2,1)S(1)}, bf16[2,128,512]{2,1,0:T(8,128)(2,1)S(1)}, u32[]{:S(2)}, u32[]{:S(2)}) collective-permute-start(bf16[2,128,512]{2,1,0:T(8,128)(2,1)S(1)} %get-tuple-element.49.refs_0_.refs_6_), channel_id=1, source_target_pairs={{2,0},{3,1},{10,8},{11,9},{18,16},{19,17},{26,24},{27,25}} | collective-permute-start | bytes 786440 | tf_op jit(solution)/shard_map/ppermute | solution.py:387
  54.9 20.3 %collective-permute-start.24 = (bf16[2,128,512]{2,1,0:T(8,128)(2,1)S(1)}, bf16[2,128,512]{2,1,0:T(8,128)(2,1)S(1)}, u32[]{:S(2)}, u32[]{:S(2)}) collective-permute-start(bf16[2,128,512]{2,1,0:T(8,128)(2,1)S(1)} %collective-permute-done.13.refs_2_.refs_1_), channel_id=1, source_target_pairs={{6,7},{14,15},{22,23},{30,31}} | collective-permute-start | bytes 786440 | tf_op jit(solution)/shard_map/ppermute | solution.py:387
  56.0 22.4 %collective-permute-start.22 = (bf16[2,128,512]{2,1,0:T(8,128)(2,1)S(1)}, bf16[2,128,512]{2,1,0:T(8,128)(2,1)S(1)}, u32[]{:S(2)}, u32[]{:S(2)}) collective-permute-start(bf16[2,128,512]{2,1,0:T(8,128)(2,1)S(1)} %get-tuple-element.53.refs_6_.refs_0_), channel_id=1, source_target_pairs={{5,7},{13,15},{21,23},{29,31}} | collective-permute-start | bytes 786440 | tf_op jit(solution)/shard_map/ppermute | solution.py:387
  56.7 21.0 %collective-permute-start.23 = (bf16[2,128,512]{2,1,0:T(8,128)(2,1)S(1)}, bf16[2,128,512]{2,1,0:T(8,128)(2,1)S(1)}, u32[]{:S(2)}, u32[]{:S(2)}) collective-permute-start(bf16[2,128,512]{2,1,0:T(8,128)(2,1)S(1)} %collective-permute-done.17.refs_2_.refs_3_), channel_id=1, source_target_pairs={{6,7},{14,15},{22,23},{30,31}} | collective-permute-start | bytes 786440 | tf_op jit(solution)/shard_map/ppermute | solution.py:387
  71.2 8.7 %collective-permute-start.30 = (bf16[2,128,512]{2,1,0:T(8,128)(2,1)S(1)}, bf16[2,128,512]{2,1,0:T(8,128)(2,1)S(1)}, u32[]{:S(2)}, u32[]{:S(2)}) collective-permute-start(bf16[2,128,512]{2,1,0:T(8,128)(2,1)S(1)} %get-tuple-element.56), channel_id=1, source_target_pairs={{0,1},{1,0},{2,3},{3,2},{4,5},{5,4},{6,7},{7,6},{8,9},{9,8},{10,11... | collective-permute-start | bytes 786440 | tf_op jit(solution)/shard_map/ppermute | solution.py:387
  71.5 11.0 %collective-permute-start.26 = (bf16[2,128,512]{2,1,0:T(8,128)(2,1)S(1)}, bf16[2,128,512]{2,1,0:T(8,128)(2,1)S(1)}, u32[]{:S(2)}, u32[]{:S(2)}) collective-permute-start(bf16[2,128,512]{2,1,0:T(8,128)(2,1)S(1)} %collective-permute-done.25.refs_4_), channel_id=1, source_target_pairs={{0,1},{1,0},{8,9},{9,8},{16,17},{17,16},{24,25},{25,24}} | collective-permute-start | bytes 786440 | tf_op jit(solution)/shard_map/ppermute | solution.py:387
  75.2 9.4 %collective-permute-start.29 = (bf16[2,128,512]{2,1,0:T(8,128)(2,1)S(1)}, bf16[2,128,512]{2,1,0:T(8,128)(2,1)S(1)}, u32[]{:S(2)}, u32[]{:S(2)}) collective-permute-start(bf16[2,128,512]{2,1,0:T(8,128)(2,1)S(1)} %get-tuple-element.55.refs_0_.refs_6_), channel_id=1, source_target_pairs={{6,4},{14,12},{22,20},{30,28}} | collective-permute-start | bytes 786440 | tf_op jit(solution)/shard_map/ppermute | solution.py:387
  77.7 2.1 %copy-start.4 = (bf16[2,128,512]{2,1,0:T(8,128)(2,1)}, bf16[2,128,512]{2,1,0:T(8,128)(2,1)S(1)}, u32[]{:S(2)}) copy-start(bf16[2,128,512]{2,1,0:T(8,128)(2,1)S(1)} %collective-permute-done.23.refs_3_.refs_2_) | copy-start | bytes 786436
  77.7 12.7 %collective-permute-start.28 = (bf16[2,128,512]{2,1,0:T(8,128)(2,1)S(1)}, bf16[2,128,512]{2,1,0:T(8,128)(2,1)S(1)}, u32[]{:S(2)}, u32[]{:S(2)}) collective-permute-start(bf16[2,128,512]{2,1,0:T(8,128)(2,1)S(1)} %get-tuple-element.55.refs_0_.refs_6_), channel_id=1, source_target_pairs={{6,2},{14,10},{22,18},{30,26}} | collective-permute-start | bytes 786440 | tf_op jit(solution)/shard_map/ppermute | solution.py:387
  78.4 12.8 %collective-permute-start.27 = (bf16[2,128,512]{2,1,0:T(8,128)(2,1)S(1)}, bf16[2,128,512]{2,1,0:T(8,128)(2,1)S(1)}, u32[]{:S(2)}, u32[]{:S(2)}) collective-permute-start(bf16[2,128,512]{2,1,0:T(8,128)(2,1)S(1)} %get-tuple-element.55.refs_0_.refs_6_), channel_id=1, source_target_pairs={{6,0},{14,8},{22,16},{30,24}} | collective-permute-start | bytes 786440 | tf_op jit(solution)/shard_map/ppermute | solution.py:387
  80.7 13.1 %collective-permute-start.33 = (bf16[2,128,512]{2,1,0:T(8,128)(2,1)S(1)}, bf16[2,128,512]{2,1,0:T(8,128)(2,1)}, u32[]{:S(2)}, u32[]{:S(2)}) collective-permute-start(bf16[2,128,512]{2,1,0:T(8,128)(2,1)S(1)} %get-tuple-element.58.refs_5_.refs_6_.refs_8_.refs_0_.refs_2_.refs_4_.refs_7_), channel_id=1, source_target_pairs={{7,5},{15,13},{23,21},{31,29}} | collective-permute-start | bytes 786440 | tf_op jit(solution)/shard_map/ppermute | solution.py:387
  83.3 10.5 %collective-permute-start.32 = (bf16[2,128,512]{2,1,0:T(8,128)(2,1)S(1)}, bf16[2,128,512]{2,1,0:T(8,128)(2,1)}, u32[]{:S(2)}, u32[]{:S(2)}) collective-permute-start(bf16[2,128,512]{2,1,0:T(8,128)(2,1)S(1)} %get-tuple-element.58.refs_5_.refs_6_.refs_8_.refs_0_.refs_2_.refs_4_.refs_7_), channel_id=1, source_target_pairs={{7,3},{15,11},{23,19},{31,27}} | collective-permute-start | bytes 786440 | tf_op jit(solution)/shard_map/ppermute | solution.py:387
  84.6 9.2 %collective-permute-start.31 = (bf16[2,128,512]{2,1,0:T(8,128)(2,1)S(1)}, bf16[2,128,512]{2,1,0:T(8,128)(2,1)}, u32[]{:S(2)}, u32[]{:S(2)}) collective-permute-start(bf16[2,128,512]{2,1,0:T(8,128)(2,1)S(1)} %get-tuple-element.58.refs_5_.refs_6_.refs_8_.refs_0_.refs_2_.refs_4_.refs_7_), channel_id=1, source_target_pairs={{7,1},{15,9},{23,17},{31,25}} | collective-permute-start | bytes 786440 | tf_op jit(solution)/shard_map/ppermute | solution.py:387
  91.9 11.0 %collective-permute-start.35 = (bf16[2,128,512]{2,1,0:T(8,128)(2,1)S(1)}, bf16[2,128,512]{2,1,0:T(8,128)(2,1)S(1)}, u32[]{:S(2)}, u32[]{:S(2)}) collective-permute-start(bf16[2,128,512]{2,1,0:T(8,128)(2,1)S(1)} %get-tuple-element.60), channel_id=1, source_target_pairs={{0,1},{1,0},{2,3},{3,2},{4,5},{5,4},{6,7},{7,6},{8,9},{9,8},{10,11... | collective-permute-start | bytes 786440 | tf_op jit(solution)/shard_map/ppermute | solution.py:387
  93.9 14.4 %collective-permute-start.34 = (bf16[2,128,512]{2,1,0:T(8,128)(2,1)S(1)}, bf16[2,128,512]{2,1,0:T(8,128)(2,1)S(1)}, u32[]{:S(2)}, u32[]{:S(2)}) collective-permute-start(bf16[2,128,512]{2,1,0:T(8,128)(2,1)S(1)} %pick_second.1), channel_id=1, source_target_pairs={{0,1},{1,0},{2,3},{3,2},{4,5},{5,4},{6,7},{7,6},{8,9},{9,8},{10,11... | collective-permute-start | bytes 786440 | tf_op jit(solution)/shard_map/ppermute | solution.py:387
  102.9 5.4 %copy-start.6 = (bf16[1,2,128,512]{3,2,1,0:T(8,128)(2,1)S(1)}, bf16[1,2,128,512]{3,2,1,0:T(8,128)(2,1)}, u32[]{:S(2)}) copy-start(bf16[1,2,128,512]{3,2,1,0:T(8,128)(2,1)} %refs_3_.5) | copy-start | bytes 786436
  110.1 6.4 %collective-permute-start.36 = (bf16[2,128,512]{2,1,0:T(8,128)(2,1)S(1)}, bf16[2,128,512]{2,1,0:T(8,128)(2,1)S(1)}, u32[]{:S(2)}, u32[]{:S(2)}) collective-permute-start(bf16[2,128,512]{2,1,0:T(8,128)(2,1)S(1)} %update_last.1.own_ref), channel_id=1, source_target_pairs={{0,1},{1,0},{2,3},{3,2},{4,5},{5,4},{6,7},{7,6},{8,9},{9,8},{10,11... | collective-permute-start | bytes 786440 | tf_op jit(solution)/shard_map/ppermute | solution.py:387
  116.5 19.1 %copy-start.9 = (f32[1,2,128,512]{3,2,1,0:T(8,128)S(1)}, f32[1,2,128,512]{3,2,1,0:T(8,128)}, u32[]{:S(2)}) copy-start(f32[1,2,128,512]{3,2,1,0:T(8,128)} %param.13) | copy-start | bytes 1572868
  118.0 7.9 %collective-permute-start.37 = (bf16[2,128,512]{2,1,0:T(8,128)(2,1)S(1)}, bf16[2,128,512]{2,1,0:T(8,128)(2,1)S(1)}, u32[]{:S(2)}, u32[]{:S(2)}) collective-permute-start(bf16[2,128,512]{2,1,0:T(8,128)(2,1)S(1)} %get-tuple-element.62), channel_id=1, source_target_pairs={{0,2},{1,3},{2,0},{3,1},{4,6},{5,7},{6,4},{7,5},{8,10},{9,11},{10,... | collective-permute-start | bytes 786440 | tf_op jit(solution)/shard_map/ppermute | solution.py:387
  118.1 15.6 %collective-permute-start.38 = (bf16[2,128,512]{2,1,0:T(8,128)(2,1)S(1)}, bf16[2,128,512]{2,1,0:T(8,128)(2,1)S(1)}, u32[]{:S(2)}, u32[]{:S(2)}) collective-permute-start(bf16[2,128,512]{2,1,0:T(8,128)(2,1)S(1)} %get-tuple-element.63), channel_id=1, source_target_pairs={{0,4},{1,5},{2,6},{3,7},{4,0},{5,1},{6,2},{7,3},{8,12},{9,13},{10,... | collective-permute-start | bytes 786440 | tf_op jit(solution)/shard_map/ppermute | solution.py:387
  118.2 15.5 %collective-permute-start.39 = (bf16[2,128,512]{2,1,0:T(8,128)(2,1)S(1)}, bf16[2,128,512]{2,1,0:T(8,128)(2,1)S(1)}, u32[]{:S(2)}, u32[]{:S(2)}) collective-permute-start(bf16[2,128,512]{2,1,0:T(8,128)(2,1)S(1)} %get-tuple-element.64), channel_id=1, source_target_pairs={{0,6},{1,7},{2,4},{3,5},{4,2},{5,3},{6,0},{7,1},{8,14},{9,15},{10,... | collective-permute-start | bytes 786440 | tf_op jit(solution)/shard_map/ppermute | solution.py:387
  134.0 1.6 %collective-permute-start.40 = (bf16[2,128,512]{2,1,0:T(8,128)(2,1)S(1)}, bf16[2,128,512]{2,1,0:T(8,128)(2,1)S(1)}, u32[]{:S(2)}, u32[]{:S(2)}) collective-permute-start(bf16[2,128,512]{2,1,0:T(8,128)(2,1)S(1)} %select_convert_fusion), channel_id=1, source_target_pairs={{0,8},{8,0},{16,24},{24,16},{1,9},{9,1},{17,25},{25,17},{2,10},{10... | collective-permute-start | bytes 786440 | tf_op jit(solution)/shard_map/ppermute | solution.py:452
  (3 other events, 2.6 us)

commit v5 on v4

--- a/solution.py
+++ b/solution.py
@@ -47,6 +47,9 @@
 )
 
 
+PARTS = 2
+
+
 def spread_plan(count):
     have = [{p} for p in range(count)]
 
@@ -226,10 +229,11 @@
     )(place, *settled, *args)
 
 
-def gather_kernel(arrivals, left, final, place_ref, *refs):
+def gather_kernel(arrivals, left, part, place_ref, *refs):
     count = len(arrivals)
     parts = refs[:count]
     refs = refs[count:]
+    final = part is not None
     if final:
         panel_ref, acc_in, rhs_ref, out_ref, buf, sems, acc_ref = refs
     else:
@@ -255,7 +259,8 @@
         def _(i=i):
             copy_of(i).start()
 
-    acc_ref[...] = acc_in[...]
+    rows = slice(part * shots, (part + 1) * shots) if final else slice(None)
+    acc_ref[...] = acc_in[:, rows]
     for i in range(count):
 
         @pl.when(blocks[i] >= 0)
@@ -266,25 +271,26 @@
             acc_ref[1] += product[shots:]
 
     if final:
-        out_ref[...] = (rhs_ref[0].astype(F32) - acc_ref[...]).astype(BF16)
-
-
-def accumulate(name, left, place, items, panel, acc, rhs=None):
+        out_ref[...] = (rhs_ref[0, :, rows].astype(F32) - acc_ref[...]).astype(BF16)
+
+
+def accumulate(name, left, place, items, panel, acc, rhs=None, part=None):
     items = [item for item in items if not left or any(0 <= block < p for p, block in enumerate(item[1]))]
     if not items:
         return acc
     parts = [item[0] for item in items]
     count = len(parts)
-    final = rhs is not None
+    final = part is not None
+    shape = (2, acc.shape[1] // PARTS, acc.shape[2]) if final else acc.shape
     vmem = pl.BlockSpec(memory_space=pltpu.VMEM)
     hbm = pl.BlockSpec(memory_space=pltpu.HBM)
     scratch = [pltpu.VMEM((count, 2, panel.shape[2], CB), BF16), pltpu.SemaphoreType.DMA((count,))]
     return pl.pallas_call(
-        functools.partial(gather_kernel, [item[1] for item in items], left, final),
-        out_shape=pltpu.VMEM(acc.shape, BF16 if final else F32),
+        functools.partial(gather_kernel, [item[1] for item in items], left, part),
+        out_shape=pltpu.VMEM(shape, BF16 if final else F32),
         in_specs=[pl.BlockSpec(memory_space=pltpu.SMEM)] + [vmem] * count + [hbm, vmem] + [vmem] * final,
         out_specs=vmem,
-        scratch_shapes=scratch + [pltpu.VMEM(acc.shape, F32)] * final,
+        scratch_shapes=scratch + [pltpu.VMEM(shape, F32)] * final,
         input_output_aliases={count + 2: 0} if left else {},
         compiler_params=pltpu.CompilerParams(vmem_limit_bytes=46 * 2**20),
         name=name,
@@ -294,67 +300,81 @@
 def pick_kernel(places, keep, place_ref, settled_ref, *refs):
     del settled_ref
     count = len(places)
-    out_ref, sems = refs[count + 1], refs[-1]
-    kept = pltpu.make_async_copy(refs[count], refs[count + 2].at[0], sems.at[1]) if keep else None
+    sems = refs[-1]
+    out_refs = refs[count + 1 : -1]
     if keep:
+        out_refs, kept_ref = out_refs[:-1], out_refs[-1]
+        kept = pltpu.make_async_copy(refs[count], kept_ref.at[0], sems.at[len(out_refs)])
         kept.start()
+    size = out_refs[0].shape[1]
 
     for p, ref in zip(places, refs):
 
         @pl.when(place_ref[0] == p)
         def _(ref=ref):
-            copy = pltpu.make_async_copy(ref, out_ref, sems.at[0])
-            copy.start()
-            copy.wait()
+            copies = [
+                pltpu.make_async_copy(ref.at[:, pl.ds(i * size, size)], out_ref, sems.at[i])
+                for i, out_ref in enumerate(out_refs)
+            ]
+            for copy in copies:
+                copy.start()
+            for copy in copies:
+                copy.wait()
 
     if keep:
         kept.wait()
 
 
-def pick(name, place, settled, values, default, keep):
+def pick(name, place, settled, values, default, keep, cuts):
     count = lax.axis_size("panel")
     vmem = pl.BlockSpec(memory_space=pltpu.VMEM)
     anywhere = pl.BlockSpec(memory_space=pl.ANY)
     args = [values.get(p, default) for p in range(count)] + [default]
-    out_shape = [pltpu.VMEM(default.shape, default.dtype)]
+    shots = default.shape[1]
+    out_shape = [pltpu.VMEM((2, shots // cuts, CB), default.dtype)] * cuts
     if keep:
         out_shape.append(jax.ShapeDtypeStruct((1, *default.shape), default.dtype))
     return pl.pallas_call(
         functools.partial(pick_kernel, tuple(range(count)), keep),
         out_shape=out_shape,
         in_specs=[pl.BlockSpec(memory_space=pltpu.SMEM)] + [anywhere] * (1 + len(args)),
-        out_specs=[vmem] + [anywhere] * keep,
-        scratch_shapes=[pltpu.SemaphoreType.DMA((2,))],
+        out_specs=[vmem] * cuts + [anywhere] * keep,
+        scratch_shapes=[pltpu.SemaphoreType.DMA((cuts + 1,))],
         compiler_params=pltpu.CompilerParams(vmem_limit_bytes=16 * 2**20),
         name=name,
     )(place, settled, *args)
 
 
-def place_kernel(own_ref, other_ref, own_hot_ref, other_hot_ref, *out_refs):
-    own = stacked(own_ref[...])
-    other = stacked(other_ref[...])
-    shots = own_ref.shape[1]
-    for i, out_ref in enumerate(out_refs):
-        rows = jnp.dot(own, own_hot_ref[i], preferred_element_type=F32) + jnp.dot(
-            other, other_hot_ref[i], preferred_element_type=F32
-        )
-        rows = rows.astype(BF16)
-        out_ref[0] = rows[:shots]
-        out_ref[1] = rows[shots:]
+def place_kernel(cuts, *refs):
+    own_refs, other_refs = refs[:cuts], refs[cuts : 2 * cuts]
+    own_hot_ref, other_hot_ref = refs[2 * cuts : 2 * cuts + 2]
+    out_refs = refs[2 * cuts + 2 :]
+    size = own_refs[0].shape[1]
+    for cut in range(cuts):
+        own = stacked(own_refs[cut][...])
+        other = stacked(other_refs[cut][...])
+        for i, out_ref in enumerate(out_refs):
+            rows = jnp.dot(own, own_hot_ref[i], preferred_element_type=F32) + jnp.dot(
+                other, other_hot_ref[i], preferred_element_type=F32
+            )
+            rows = rows.astype(BF16)
+            out_ref[0, cut * size : (cut + 1) * size] = rows[:size]
+            out_ref[1, cut * size : (cut + 1) * size] = rows[size:]
 
 
 def place_rows(own, other, own_hot, other_hot):
     vmem = pl.BlockSpec(memory_space=pltpu.VMEM)
-    shape = jax.ShapeDtypeStruct(own.shape, BF16)
+    cuts = len(own)
+    shape = jax.ShapeDtypeStruct((2, cuts * own[0].shape[1], own[0].shape[2]), BF16)
     count = own_hot.shape[0]
     return pl.pallas_call(
-        place_kernel,
+        functools.partial(place_kernel, cuts),
         out_shape=(shape,) * count,
-        in_specs=[vmem] * 4,
+        in_specs=[vmem] * (2 * cuts + 2),
         out_specs=(vmem,) * count,
         compiler_params=pltpu.CompilerParams(vmem_limit_bytes=24 * 2**20),
         name="place_rows",
-    )(own, other, own_hot, other_hot)
+    )(*own, *other, own_hot, other_hot)
 
 
 def placements(row_maps, place, count, rows):
@@ -421,25 +441,28 @@
         acc_u = accumulate(f"update_{hop}", False, place_ref, parts, update_panel, acc_u)
         settled.append(acc_u)
 
-    def cross(name, settled, blocks, keep):
+    def cross(name, settled, blocks, keep, cuts):
         values = {}
         for earlier, rows in enumerate(spread_rows):
             for i, row in enumerate(rows):
                 for p in range(count):
                     if row[p] == blocks[p % 2]:
                         values[p] = came[earlier][i]
-        value, *kept = pick(name, place_ref, settled, values, mine, keep)
-        return (send(value, SWAP), *kept)
-
-    first, solved = cross("pick_first", settled[count], (count - 2, count - 3), True)
-    (second,) = cross("pick_second", settled[count + 1], (None, count - 1), False)
+        outs = pick(name, place_ref, settled, values, mine, keep, cuts)
+        return [send(value, SWAP) for value in outs[:cuts]] + list(outs[cuts:])
+
+    first, solved = cross("pick_first", settled[count], (count - 2, count - 3), True, 1)
+    acc_u = accumulate("update_mid", False, place_ref, [(first, swap_rows[0])], update_panel, acc_u)
+    seconds = cross("pick_second", settled[count + 1], (None, count - 1), False, PARTS)
     parts = [(came[-1][i], row) for i, row in enumerate(spread_rows[-1])]
-    parts.append((first, swap_rows[0]))
     acc_u = accumulate("update_late", False, place_ref, parts, update_panel, acc_u)
-    parts = [(second, swap_rows[1])]
-    child = accumulate("update_last", False, place_ref, parts, update_panel, acc_u, update_rhs)
-    other = send(child, SWAP)
-    placed = place_rows(child, other, own_hot, other_hot)
+    children = [
+        accumulate(
+            f"update_last_{i}", False, place_ref, [(second, swap_rows[1])], update_panel, acc_u, update_rhs, i
+        )
+        for i, second in enumerate(seconds)
+    ]
+    placed = place_rows(children, [send(child, SWAP) for child in children], own_hot, other_hot)
     sums = [placed[0].astype(F32), placed[1].astype(F32)]
     for step in range(1, count // 2):
         moved = send(placed[1 + step], [(p, p ^ (2 * step)) for p in range(count)]).astype(F32)

time: 139 us -> 139 us (level)
  starting transfers between devices: 54.5 us -> 51.4 us
  Pallas kernels: 20.6 us -> 22.6 us
    ppermute x40 -> x42, starting transfers between devices: 54.4 us -> 51.4 us  [send(): return lax.ppermute(value, 'panel', edges)]
    pallas_call x16 -> x18, Pallas kernels: 15.3 us -> 16.7 us  [accumulate(): pl.pallas_call(functools.partial(gather_kernel, [item[1] for item in item...]
    unnamed x20 -> x24, local copies, waits for them, and re-layouts: 4.79 us -> 5.75 us
    ppermute x40 -> x42, waiting for transfers between devices: 50.7 us -> 50.8 us  [send(): return lax.ppermute(value, 'panel', edges)]
  transfers between devices with their start and end apart: 41 -> 43, of which waited for: 14 -> 16; matrix products, arithmetic and copies ran while one was open for 1% -> 1% of each run, Pallas kernels for 12% -> 15%
where the time goes in v5:
time: 139 us; the launch traced here: 137 us
  waiting for transfers between devices  52.3 us (38%)
  starting transfers between devices  51.4 us (37%)
  Pallas kernels  22.6 us (16%)
  local copies, waits for them, and re-layouts  6.69 us (5%)
  other arithmetic  2.45 us (2%)
  between operations  1.44 us (1%)
    ppermute x42, starting transfers between devices, send(): return lax.ppermute(value, 'panel', edges)  51.4 us
    ppermute x42, waiting for transfers between devices, send(): return lax.ppermute(value, 'panel', edges)  50.8 us
    pallas_call x18, Pallas kernels, accumulate(): pl.pallas_call(functools.partial(gather_kernel, [item[1] for item in item...  16.7 us
    unnamed x24, local copies, waits for them, and re-layouts  5.75 us
  transfers between devices with their start and end apart: 43, of which 16 were waited for; matrix products, arithmetic and copies ran while one was open for 1% of the time, Pallas kernels for 15%

profile of v5, /device:TPU:0, one launch (start us, length us, event | category | flops | bytes accessed | tf_op | source)
XLA Modules:
  0.0 136.9 jit_solution(1347886084227696730)
XLA Ops:
  0.6 1.2 copy-done
  1.9 0.9 copy-done.2
  3.3 2.6 %collective-permute-start = (bf16[2,128,512]{2,1,0:T(8,128)(2,1)S(1)}, bf16[2,128,512]{2,1,0:T(8,128)(2,1)S(1)}, u32[]{:S(2)}, u32[]{:S(2)}) collective-permute-start(bf16[2,128,512]{2,1,0:T(8,128)(2,1)S(1)} %get-tuple-element.38), channel_id=1, source_target_pairs={{0,1},{1,0},{2,3},{3,2},{4,5},{5,4},{6,7},{7,6},{8,9},{9,8},{10,11... | collective-permute-start | bytes 786440 | tf_op jit(solution)/shard_map/ppermute | solution.py:407
  5.9 3.6 %collective-permute-start.3 = (bf16[2,128,512]{2,1,0:T(8,128)(2,1)S(1)}, bf16[2,128,512]{2,1,0:T(8,128)(2,1)S(1)}, u32[]{:S(2)}, u32[]{:S(2)}) collective-permute-start(bf16[2,128,512]{2,1,0:T(8,128)(2,1)S(1)} %get-tuple-element.36.refs_0_.refs_6_), channel_id=1, source_target_pairs={{0,2},{8,10},{16,18},{24,26}} | collective-permute-start | bytes 786440 | tf_op jit(solution)/shard_map/ppermute | solution.py:407
  9.5 1.7 %collective-permute-start.2 = (bf16[2,128,512]{2,1,0:T(8,128)(2,1)S(1)}, bf16[2,128,512]{2,1,0:T(8,128)(2,1)S(1)}, u32[]{:S(2)}, u32[]{:S(2)}) collective-permute-start(bf16[2,128,512]{2,1,0:T(8,128)(2,1)S(1)} %get-tuple-element.36.refs_0_.refs_6_), channel_id=1, source_target_pairs={{0,4},{8,12},{16,20},{24,28}} | collective-permute-start | bytes 786440 | tf_op jit(solution)/shard_map/ppermute | solution.py:407
  11.2 1.7 %collective-permute-start.1 = (bf16[2,128,512]{2,1,0:T(8,128)(2,1)S(1)}, bf16[2,128,512]{2,1,0:T(8,128)(2,1)S(1)}, u32[]{:S(2)}, u32[]{:S(2)}) collective-permute-start(bf16[2,128,512]{2,1,0:T(8,128)(2,1)S(1)} %get-tuple-element.36.refs_0_.refs_6_), channel_id=1, source_target_pairs={{0,6},{8,14},{16,22},{24,30}} | collective-permute-start | bytes 786440 | tf_op jit(solution)/shard_map/ppermute | solution.py:407
  12.9 1.3 setup.1
  14.8 1.7 %update_0.1.refs_0_.refs_6_ = f32[2,128,512]{2,1,0:T(8,128)S(1)} custom-call(s32[1]{0:T(128)} %bitcast.place_ref, bf16[2,128,512]{2,1,0:T(8,128)(2,1)S(1)} %get-tuple-element.36.refs_0_.refs_6_, bf16[1,2,512,4096]{3,2,1,0:T(8,128)(2,1)} %refs_1_.21, f32[2,128,512]{2,1,0:T(8,128)S(1)} %get-tuple-element.37.refs_2_.refs_0_), custom_call_target="tpu_custom_call" | custom-call | tf_op jit(solution)/shard_map/update_0/pallas_call | solution.py:288
  17.9 3.9 %collective-permute-done.2.refs_2_.refs_8_.refs_3_ = bf16[2,128,512]{2,1,0:T(8,128)(2,1)S(1)} collective-permute-done((bf16[2,128,512]{2,1,0:T(8,128)(2,1)S(1)}, bf16[2,128,512]{2,1,0:T(8,128)(2,1)S(1)}, u32[]{:S(2)}, u32[]{:S(2)}) %collective-permute-start.2) | collective-permute-done | bytes 262176 | tf_op jit(solution)/shard_map/ppermute | solution.py:407
  22.5 3.5 %collective-permute-done.1.refs_1_.refs_9_.refs_2_ = bf16[2,128,512]{2,1,0:T(8,128)(2,1)S(1)} collective-permute-done((bf16[2,128,512]{2,1,0:T(8,128)(2,1)S(1)}, bf16[2,128,512]{2,1,0:T(8,128)(2,1)S(1)}, u32[]{:S(2)}, u32[]{:S(2)}) %collective-permute-start.1) | collective-permute-done | bytes 262176 | tf_op jit(solution)/shard_map/ppermute | solution.py:407
  28.6 5.2 %collective-permute-done.9.refs_0_.refs_5_.refs_1_ = bf16[2,128,512]{2,1,0:T(8,128)(2,1)S(1)} collective-permute-done((bf16[2,128,512]{2,1,0:T(8,128)(2,1)S(1)}, bf16[2,128,512]{2,1,0:T(8,128)(2,1)S(1)}, u32[]{:S(2)}, u32[]{:S(2)}) %collective-permute-start.9) | collective-permute-done | bytes 262176 | tf_op jit(solution)/shard_map/ppermute | solution.py:407
  33.9 3.6 %collective-permute-start.12 = (bf16[2,128,512]{2,1,0:T(8,128)(2,1)S(1)}, bf16[2,128,512]{2,1,0:T(8,128)(2,1)S(1)}, u32[]{:S(2)}, u32[]{:S(2)}) collective-permute-start(bf16[2,128,512]{2,1,0:T(8,128)(2,1)S(1)} %get-tuple-element.48), channel_id=1, source_target_pairs={{3,4},{4,5},{5,2},{2,3},{0,1},{1,0},{6,7},{7,6},{11,12},{12,13},{1... | collective-permute-start | bytes 786440 | tf_op jit(solution)/shard_map/ppermute | solution.py:407
  39.1 3.7 %collective-permute-done.12.refs_5_.refs_1_.refs_0_ = bf16[2,128,512]{2,1,0:T(8,128)(2,1)S(1)} collective-permute-done((bf16[2,128,512]{2,1,0:T(8,128)(2,1)S(1)}, bf16[2,128,512]{2,1,0:T(8,128)(2,1)S(1)}, u32[]{:S(2)}, u32[]{:S(2)}) %collective-permute-start.12) | collective-permute-done | bytes 262176 | tf_op jit(solution)/shard_map/ppermute | solution.py:407
  42.8 1.8 %collective-permute-start.15 = (bf16[2,128,512]{2,1,0:T(8,128)(2,1)S(1)}, bf16[2,128,512]{2,1,0:T(8,128)(2,1)S(1)}, u32[]{:S(2)}, u32[]{:S(2)}) collective-permute-start(bf16[2,128,512]{2,1,0:T(8,128)(2,1)S(1)} %get-tuple-element.52), channel_id=1, source_target_pairs={{0,1},{1,0},{2,3},{3,2},{4,5},{5,4},{6,7},{7,6},{8,9},{9,8},{10,11... | collective-permute-start | bytes 786440 | tf_op jit(solution)/shard_map/ppermute | solution.py:407
  46.7 1.8 %update_3.1.refs_5_.refs_0_ = f32[2,128,512]{2,1,0:T(8,128)S(1)} custom-call(s32[1]{0:T(128)} %bitcast.place_ref, bf16[2,128,512]{2,1,0:T(8,128)(2,1)S(1)} %get-tuple-element.49.refs_6_.refs_0_, bf16[2,128,512]{2,1,0:T(8,128)(2,1)S(1)} %collective-permute-done.9.refs_0_.refs_5_.refs_1_, bf16[2,128,512]{2,1,0:T(8,128)(2,1)S(1)} %collective-permute-done.10.refs_1_.refs_2_, ...), custom_call_target="tpu_custom_call" | custom-call | tf_op jit(solution)/shard_map/update_3/pallas_call | solution.py:288
  48.6 0.9 collective-permute-done.15.refs_0_.refs_5_.refs_1_
  49.6 2.0 %collective-permute-start.19 = (bf16[2,128,512]{2,1,0:T(8,128)(2,1)S(1)}, bf16[2,128,512]{2,1,0:T(8,128)(2,1)S(1)}, u32[]{:S(2)}, u32[]{:S(2)}) collective-permute-start(bf16[2,128,512]{2,1,0:T(8,128)(2,1)S(1)} %get-tuple-element.54), channel_id=1, source_target_pairs={{5,6},{6,7},{7,4},{4,5},{0,1},{1,0},{2,3},{3,2},{13,14},{14,15},{1... | collective-permute-start | bytes 786440 | tf_op jit(solution)/shard_map/ppermute | solution.py:407
  52.3 1.3 collective-permute-start.20
  53.6 1.3 collective-permute-start.25
  57.3 13.8 %collective-permute-done.20.refs_8_.refs_6_.refs_1_ = bf16[2,128,512]{2,1,0:T(8,128)(2,1)S(1)} collective-permute-done((bf16[2,128,512]{2,1,0:T(8,128)(2,1)S(1)}, bf16[2,128,512]{2,1,0:T(8,128)(2,1)S(1)}, u32[]{:S(2)}, u32[]{:S(2)}) %collective-permute-start.20) | collective-permute-done | bytes 262176 | tf_op jit(solution)/shard_map/ppermute | solution.py:407
  71.5 3.6 %collective-permute-start.26 = (bf16[2,128,512]{2,1,0:T(8,128)(2,1)S(1)}, bf16[2,128,512]{2,1,0:T(8,128)(2,1)S(1)}, u32[]{:S(2)}, u32[]{:S(2)}) collective-permute-start(bf16[2,128,512]{2,1,0:T(8,128)(2,1)S(1)} %collective-permute-done.25.refs_4_), channel_id=1, source_target_pairs={{0,1},{1,0},{8,9},{9,8},{16,17},{17,16},{24,25},{25,24}} | collective-permute-start | bytes 786440 | tf_op jit(solution)/shard_map/ppermute | solution.py:407
  75.9 1.8 %update_5.1.refs_9_.refs_0_ = f32[2,128,512]{2,1,0:T(8,128)S(1)} custom-call(s32[1]{0:T(128)} %bitcast.place_ref, bf16[2,128,512]{2,1,0:T(8,128)(2,1)S(1)} %get-tuple-element.55.refs_6_.refs_0_, bf16[2,128,512]{2,1,0:T(8,128)(2,1)S(1)} %collective-permute-done.15.refs_0_.refs_5_.refs_1_, bf16[2,128,512]{2,1,0:T(8,128)(2,1)S(1)} %collective-permute-done.16.refs_1_.refs_2_, ...), custom_call_target="tpu_custom_call" | custom-call | tf_op jit(solution)/shard_map/update_5/pallas_call | solution.py:288
  77.7 1.4 %collective-permute-start.28 = (bf16[2,128,512]{2,1,0:T(8,128)(2,1)S(1)}, bf16[2,128,512]{2,1,0:T(8,128)(2,1)}, u32[]{:S(2)}, u32[]{:S(2)}) collective-permute-start(bf16[2,128,512]{2,1,0:T(8,128)(2,1)S(1)} %get-tuple-element.57.refs_0_.refs_6_), channel_id=1, source_target_pairs={{6,2},{14,10},{22,18},{30,26}} | collective-permute-start | bytes 786440 | tf_op jit(solution)/shard_map/ppermute | solution.py:407
  79.1 1.3 collective-permute-start.27
  80.6 0.8 solve_7.1
  84.8 0.9 copy-done.6
  85.7 0.9 copy-done.8
  86.7 0.9 copy-done.10
  87.6 2.3 %update_6.1.settled_ref.refs_6_ = f32[2,128,512]{2,1,0:T(8,128)S(1)} custom-call(s32[1]{0:T(128)} %bitcast.place_ref, bf16[2,128,512]{2,1,0:T(8,128)(2,1)S(1)} %get-tuple-element.57.refs_0_.refs_6_, bf16[2,128,512]{2,1,0:T(8,128)(2,1)S(1)} %collective-permute-done.19.refs_5_.refs_1_.refs_0_, ...), custom_call_target="tpu_custom_call" | custom-call | tf_op jit(solution)/shard_map/update_6/pallas_call | solution.py:288
  89.9 1.4 collective-permute-done.27.refs_0_.refs_4_
  91.3 1.1 pick_first.1
  92.4 2.8 %update_7.1.settled_ref.refs_2_ = f32[2,128,512]{2,1,0:T(8,128)S(1)} custom-call(s32[1]{0:T(128)} %bitcast.place_ref, bf16[2,128,512]{2,1,0:T(8,128)(2,1)S(1)} %get-tuple-element.60.refs_5_.refs_6_.refs_8_.refs_0_.refs_2_.refs_4_.refs_7_, bf16[2,128,512]{2,1,0:T(8,128)(2,1)S(1)} %collective-permute-done.30.refs_5_.refs_1_, ...), custom_call_target="tpu_custom_call" | custom-call | tf_op jit(solution)/shard_map/update_7/pallas_call | solution.py:288
  95.5 6.3 %collective-permute-start.34 = (bf16[2,64,512]{2,1,0:T(8,128)(2,1)S(1)}, bf16[2,64,512]{2,1,0:T(8,128)(2,1)S(1)}, u32[]{:S(2)}, u32[]{:S(2)}) collective-permute-start(bf16[2,64,512]{2,1,0:T(8,128)(2,1)S(1)} %get-tuple-element.62), channel_id=1, source_target_pairs={{0,1},{1,0},{2,3},{3,2},{4,5},{5,4},{6,7},{7,6},{8,9},{9,8},{10,11... | collective-permute-start | bytes 393224 | tf_op jit(solution)/shard_map/ppermute | solution.py:407
  102.0 0.9 fusion.8
  102.8 1.7 %update_mid.1.refs_4_ = f32[2,128,512]{2,1,0:T(8,128)S(1)} custom-call(s32[1]{0:T(128)} %bitcast.place_ref, bf16[2,128,512]{2,1,0:T(8,128)(2,1)S(1)} %collective-permute-done.35.refs_0_, bf16[1,2,512,4096]{3,2,1,0:T(8,128)(2,1)} %refs_1_.21, f32[2,128,512]{2,1,0:T(8,128)S(1)} %update_7.1.settled_ref.refs_2_), custom_call_target="tpu_custom_call" | custom-call | tf_op jit(solution)/shard_map/update_mid/pallas_call | solution.py:288
  104.7 1.3 collective-permute-done.34.refs_0_
  106.0 1.8 %update_last_0.1.refs_0_ = bf16[2,64,512]{2,1,0:T(8,128)(2,1)S(1)} custom-call(s32[1]{0:T(128)} %bitcast.place_ref, bf16[2,64,512]{2,1,0:T(8,128)(2,1)S(1)} %collective-permute-done.34.refs_0_, bf16[1,2,512,4096]{3,2,1,0:T(8,128)(2,1)} %refs_1_.21, f32[2,128,512]{2,1,0:T(8,128)S(1)} %update_late.1.refs_2_, bf16[1,2,128,512]{3,2,1,0:T(8,128)(2,1)S(1)} %copy-done.4), custom_call_target="tpu_custom_call" | custom-call | tf_op jit(solution)/shard_map/update_last_0/pallas_call | solution.py:288
  108.8 1.8 %update_last_1.1.refs_1_ = bf16[2,64,512]{2,1,0:T(8,128)(2,1)S(1)} custom-call(s32[1]{0:T(128)} %bitcast.place_ref, bf16[2,64,512]{2,1,0:T(8,128)(2,1)S(1)} %collective-permute-done.36.refs_0_, bf16[1,2,512,4096]{3,2,1,0:T(8,128)(2,1)} %refs_1_.21, f32[2,128,512]{2,1,0:T(8,128)S(1)} %update_late.1.refs_2_, bf16[1,2,128,512]{3,2,1,0:T(8,128)(2,1)S(1)} %copy-done.4), custom_call_target="tpu_custom_call" | custom-call | tf_op jit(solution)/shard_map/update_last_1/pallas_call | solution.py:288
  110.6 0.9 compare_convert_fusion
  111.5 1.2 collective-permute-done.37.refs_2_
  112.8 2.8 %collective-permute-done.38.refs_3_ = bf16[2,64,512]{2,1,0:T(8,128)(2,1)S(1)} collective-permute-done((bf16[2,64,512]{2,1,0:T(8,128)(2,1)S(1)}, bf16[2,64,512]{2,1,0:T(8,128)(2,1)S(1)}, u32[]{:S(2)}, u32[]{:S(2)}) %collective-permute-start.38) | collective-permute-done | bytes 131104 | tf_op jit(solution)/shard_map/ppermute | solution.py:407
  115.6 1.6 %place_rows.1 = (bf16[2,128,512]{2,1,0:T(8,128)(2,1)S(1)}, bf16[2,128,512]{2,1,0:T(8,128)(2,1)S(1)}, bf16[2,128,512]{2,1,0:T(8,128)(2,1)S(1)}, bf16[2,128,512]{2,1,0:T(8,128)(2,1)S(1)}, bf16[2,128,512]{2,1,0:T(8,128)(2,1)S(1)}) custom-call(bf16[2,64,512]{2,1,0:T(8,128)(2,1)S(1)} %update_last_0.1.refs_0_, bf16[2,64,512]{2,1,0:T(8,128)(2,1)S(1)} %update_last_1.1.refs_1_, ...), custom_call_target="tpu_custom_call" | custom-call | tf_op jit(solution)/shard_map/place_rows/pallas_call | solution.py:370
  117.2 2.6 %collective-permute-start.40 = (bf16[2,128,512]{2,1,0:T(8,128)(2,1)S(1)}, bf16[2,128,512]{2,1,0:T(8,128)(2,1)S(1)}, u32[]{:S(2)}, u32[]{:S(2)}) collective-permute-start(bf16[2,128,512]{2,1,0:T(8,128)(2,1)S(1)} %get-tuple-element.67), channel_id=1, source_target_pairs={{0,4},{1,5},{2,6},{3,7},{4,0},{5,1},{6,2},{7,3},{8,12},{9,13},{10,... | collective-permute-start | bytes 786440 | tf_op jit(solution)/shard_map/ppermute | solution.py:407
  119.9 1.7 %collective-permute-start.41 = (bf16[2,128,512]{2,1,0:T(8,128)(2,1)S(1)}, bf16[2,128,512]{2,1,0:T(8,128)(2,1)S(1)}, u32[]{:S(2)}, u32[]{:S(2)}) collective-permute-start(bf16[2,128,512]{2,1,0:T(8,128)(2,1)S(1)} %get-tuple-element.68), channel_id=1, source_target_pairs={{0,6},{1,7},{2,4},{3,5},{4,2},{5,3},{6,0},{7,1},{8,14},{9,15},{10,... | collective-permute-start | bytes 786440 | tf_op jit(solution)/shard_map/ppermute | solution.py:407
  121.6 5.0 %collective-permute-done.39 = bf16[2,128,512]{2,1,0:T(8,128)(2,1)S(1)} collective-permute-done((bf16[2,128,512]{2,1,0:T(8,128)(2,1)S(1)}, bf16[2,128,512]{2,1,0:T(8,128)(2,1)S(1)}, u32[]{:S(2)}, u32[]{:S(2)}) %collective-permute-start.39) | collective-permute-done | bytes 262176 | tf_op jit(solution)/shard_map/ppermute | solution.py:407
  126.6 7.2 %collective-permute-done.40 = bf16[2,128,512]{2,1,0:T(8,128)(2,1)S(1)} collective-permute-done((bf16[2,128,512]{2,1,0:T(8,128)(2,1)S(1)}, bf16[2,128,512]{2,1,0:T(8,128)(2,1)S(1)}, u32[]{:S(2)}, u32[]{:S(2)}) %collective-permute-start.40) | collective-permute-done | bytes 262176 | tf_op jit(solution)/shard_map/ppermute | solution.py:407
  134.2 1.5 %collective-permute-done.42 = bf16[2,128,512]{2,1,0:T(8,128)(2,1)S(1)} collective-permute-done((bf16[2,128,512]{2,1,0:T(8,128)(2,1)S(1)}, bf16[2,128,512]{2,1,0:T(8,128)(2,1)S(1)}, u32[]{:S(2)}, u32[]{:S(2)}) %collective-permute-start.42) | collective-permute-done | bytes 262176 | tf_op jit(solution)/shard_map/ppermute | solution.py:475
  135.7 1.2 fusion.7
  (98 shorter events, 19.3 us)
Async XLA Ops:
  3.3 11.0 %collective-permute-start = (bf16[2,128,512]{2,1,0:T(8,128)(2,1)S(1)}, bf16[2,128,512]{2,1,0:T(8,128)(2,1)S(1)}, u32[]{:S(2)}, u32[]{:S(2)}) collective-permute-start(bf16[2,128,512]{2,1,0:T(8,128)(2,1)S(1)} %get-tuple-element.38), channel_id=1, source_target_pairs={{0,1},{1,0},{2,3},{3,2},{4,5},{5,4},{6,7},{7,6},{8,9},{9,8},{10,11... | collective-permute-start | bytes 786440 | tf_op jit(solution)/shard_map/ppermute | solution.py:407
  5.9 8.4 %copy-start.1 = (bf16[1,2,512,512]{3,2,1,0:T(8,128)(2,1)S(1)}, bf16[1,2,512,512]{3,2,1,0:T(8,128)(2,1)}, u32[]{:S(2)}) copy-start(bf16[1,2,512,512]{3,2,1,0:T(8,128)(2,1)} %refs_4_.23) | copy-start | bytes 3145732
  5.9 8.4 %copy-start.3 = (bf16[1,2,128,512]{3,2,1,0:T(8,128)(2,1)S(1)}, bf16[1,2,128,512]{3,2,1,0:T(8,128)(2,1)}, u32[]{:S(2)}) copy-start(bf16[1,2,128,512]{3,2,1,0:T(8,128)(2,1)} %refs_1_.18) | copy-start | bytes 786436
  5.9 11.4 %collective-permute-start.3 = (bf16[2,128,512]{2,1,0:T(8,128)(2,1)S(1)}, bf16[2,128,512]{2,1,0:T(8,128)(2,1)S(1)}, u32[]{:S(2)}, u32[]{:S(2)}) collective-permute-start(bf16[2,128,512]{2,1,0:T(8,128)(2,1)S(1)} %get-tuple-element.36.refs_0_.refs_6_), channel_id=1, source_target_pairs={{0,2},{8,10},{16,18},{24,26}} | collective-permute-start | bytes 786440 | tf_op jit(solution)/shard_map/ppermute | solution.py:407
  9.5 12.3 %collective-permute-start.2 = (bf16[2,128,512]{2,1,0:T(8,128)(2,1)S(1)}, bf16[2,128,512]{2,1,0:T(8,128)(2,1)S(1)}, u32[]{:S(2)}, u32[]{:S(2)}) collective-permute-start(bf16[2,128,512]{2,1,0:T(8,128)(2,1)S(1)} %get-tuple-element.36.refs_0_.refs_6_), channel_id=1, source_target_pairs={{0,4},{8,12},{16,20},{24,28}} | collective-permute-start | bytes 786440 | tf_op jit(solution)/shard_map/ppermute | solution.py:407
  11.2 14.8 %collective-permute-start.1 = (bf16[2,128,512]{2,1,0:T(8,128)(2,1)S(1)}, bf16[2,128,512]{2,1,0:T(8,128)(2,1)S(1)}, u32[]{:S(2)}, u32[]{:S(2)}) collective-permute-start(bf16[2,128,512]{2,1,0:T(8,128)(2,1)S(1)} %get-tuple-element.36.refs_0_.refs_6_), channel_id=1, source_target_pairs={{0,6},{8,14},{16,22},{24,30}} | collective-permute-start | bytes 786440 | tf_op jit(solution)/shard_map/ppermute | solution.py:407
  14.3 12.5 %collective-permute-start.4 = (bf16[2,128,512]{2,1,0:T(8,128)(2,1)S(1)}, bf16[2,128,512]{2,1,0:T(8,128)(2,1)S(1)}, u32[]{:S(2)}, u32[]{:S(2)}) collective-permute-start(bf16[2,128,512]{2,1,0:T(8,128)(2,1)S(1)} %get-tuple-element.42), channel_id=1, source_target_pairs={{1,2},{2,3},{3,0},{0,1},{4,5},{5,4},{6,7},{7,6},{9,10},{10,11},{11... | collective-permute-start | bytes 786440 | tf_op jit(solution)/shard_map/ppermute | solution.py:407
  16.6 11.2 %collective-permute-start.8 = (bf16[2,128,512]{2,1,0:T(8,128)(2,1)S(1)}, bf16[2,128,512]{2,1,0:T(8,128)(2,1)S(1)}, u32[]{:S(2)}, u32[]{:S(2)}) collective-permute-start(bf16[2,128,512]{2,1,0:T(8,128)(2,1)S(1)} %get-tuple-element.43.refs_6_.refs_0_), channel_id=1, source_target_pairs={{1,3},{9,11},{17,19},{25,27}} | collective-permute-start | bytes 786440 | tf_op jit(solution)/shard_map/ppermute | solution.py:407
  17.3 9.8 %collective-permute-start.7 = (bf16[2,128,512]{2,1,0:T(8,128)(2,1)S(1)}, bf16[2,128,512]{2,1,0:T(8,128)(2,1)S(1)}, u32[]{:S(2)}, u32[]{:S(2)}) collective-permute-start(bf16[2,128,512]{2,1,0:T(8,128)(2,1)S(1)} %collective-permute-done.3.refs_3_.refs_4_), channel_id=1, source_target_pairs={{2,3},{10,11},{18,19},{26,27}} | collective-permute-start | bytes 786440 | tf_op jit(solution)/shard_map/ppermute | solution.py:407
  21.8 6.6 %collective-permute-start.6 = (bf16[2,128,512]{2,1,0:T(8,128)(2,1)S(1)}, bf16[2,128,512]{2,1,0:T(8,128)(2,1)S(1)}, u32[]{:S(2)}, u32[]{:S(2)}) collective-permute-start(bf16[2,128,512]{2,1,0:T(8,128)(2,1)S(1)} %get-tuple-element.43.refs_6_.refs_0_), channel_id=1, source_target_pairs={{1,5},{9,13},{17,21},{25,29}} | collective-permute-start | bytes 786440 | tf_op jit(solution)/shard_map/ppermute | solution.py:407
  26.0 2.5 %collective-permute-start.5 = (bf16[2,128,512]{2,1,0:T(8,128)(2,1)S(1)}, bf16[2,128,512]{2,1,0:T(8,128)(2,1)S(1)}, u32[]{:S(2)}, u32[]{:S(2)}) collective-permute-start(bf16[2,128,512]{2,1,0:T(8,128)(2,1)S(1)} %get-tuple-element.43.refs_6_.refs_0_), channel_id=1, source_target_pairs={{1,7},{9,15},{17,23},{25,31}} | collective-permute-start | bytes 786440 | tf_op jit(solution)/shard_map/ppermute | solution.py:407
  26.9 6.9 %collective-permute-start.9 = (bf16[2,128,512]{2,1,0:T(8,128)(2,1)S(1)}, bf16[2,128,512]{2,1,0:T(8,128)(2,1)S(1)}, u32[]{:S(2)}, u32[]{:S(2)}) collective-permute-start(bf16[2,128,512]{2,1,0:T(8,128)(2,1)S(1)} %get-tuple-element.46), channel_id=1, source_target_pairs={{0,1},{1,0},{2,3},{3,2},{4,5},{5,4},{6,7},{7,6},{8,9},{9,8},{10,11... | collective-permute-start | bytes 786440 | tf_op jit(solution)/shard_map/ppermute | solution.py:407
  27.1 11.9 %collective-permute-start.10 = (bf16[2,128,512]{2,1,0:T(8,128)(2,1)S(1)}, bf16[2,128,512]{2,1,0:T(8,128)(2,1)S(1)}, u32[]{:S(2)}, u32[]{:S(2)}) collective-permute-start(bf16[2,128,512]{2,1,0:T(8,128)(2,1)S(1)} %get-tuple-element.47.refs_7_), channel_id=1, source_target_pairs={{2,4},{10,12},{18,20},{26,28}} | collective-permute-start | bytes 786440 | tf_op jit(solution)/shard_map/ppermute | solution.py:407
  27.8 10.5 %collective-permute-start.11 = (bf16[2,128,512]{2,1,0:T(8,128)(2,1)S(1)}, bf16[2,128,512]{2,1,0:T(8,128)(2,1)S(1)}, u32[]{:S(2)}, u32[]{:S(2)}) collective-permute-start(bf16[2,128,512]{2,1,0:T(8,128)(2,1)S(1)} %get-tuple-element.45.refs_0_.refs_6_), channel_id=1, source_target_pairs={{2,4},{10,12},{18,20},{26,28}} | collective-permute-start | bytes 786440 | tf_op jit(solution)/shard_map/ppermute | solution.py:407
  33.9 8.9 %collective-permute-start.12 = (bf16[2,128,512]{2,1,0:T(8,128)(2,1)S(1)}, bf16[2,128,512]{2,1,0:T(8,128)(2,1)S(1)}, u32[]{:S(2)}, u32[]{:S(2)}) collective-permute-start(bf16[2,128,512]{2,1,0:T(8,128)(2,1)S(1)} %get-tuple-element.48), channel_id=1, source_target_pairs={{3,4},{4,5},{5,2},{2,3},{0,1},{1,0},{6,7},{7,6},{11,12},{12,13},{1... | collective-permute-start | bytes 786440 | tf_op jit(solution)/shard_map/ppermute | solution.py:407
  37.5 8.5 %collective-permute-start.13 = (bf16[2,128,512]{2,1,0:T(8,128)(2,1)S(1)}, bf16[2,128,512]{2,1,0:T(8,128)(2,1)S(1)}, u32[]{:S(2)}, u32[]{:S(2)}) collective-permute-start(bf16[2,128,512]{2,1,0:T(8,128)(2,1)S(1)} %get-tuple-element.49.refs_6_.refs_0_), channel_id=1, source_target_pairs={{3,5},{2,6},{11,13},{10,14},{19,21},{18,22},{27,29},{26,30}} | collective-permute-start | bytes 786440 | tf_op jit(solution)/shard_map/ppermute | solution.py:407
  38.3 10.2 %collective-permute-start.14 = (bf16[2,128,512]{2,1,0:T(8,128)(2,1)S(1)}, bf16[2,128,512]{2,1,0:T(8,128)(2,1)S(1)}, u32[]{:S(2)}, u32[]{:S(2)}) collective-permute-start(bf16[2,128,512]{2,1,0:T(8,128)(2,1)S(1)} %collective-permute-done.11.refs_2_.refs_3_), channel_id=1, source_target_pairs={{4,5},{12,13},{20,21},{28,29}} | collective-permute-start | bytes 786440 | tf_op jit(solution)/shard_map/ppermute | solution.py:407
  42.8 6.7 %collective-permute-start.15 = (bf16[2,128,512]{2,1,0:T(8,128)(2,1)S(1)}, bf16[2,128,512]{2,1,0:T(8,128)(2,1)S(1)}, u32[]{:S(2)}, u32[]{:S(2)}) collective-permute-start(bf16[2,128,512]{2,1,0:T(8,128)(2,1)S(1)} %get-tuple-element.52), channel_id=1, source_target_pairs={{0,1},{1,0},{2,3},{3,2},{4,5},{5,4},{6,7},{7,6},{8,9},{9,8},{10,11... | collective-permute-start | bytes 786440 | tf_op jit(solution)/shard_map/ppermute | solution.py:407
  44.6 7.6 %collective-permute-start.16 = (bf16[2,128,512]{2,1,0:T(8,128)(2,1)S(1)}, bf16[2,128,512]{2,1,0:T(8,128)(2,1)S(1)}, u32[]{:S(2)}, u32[]{:S(2)}) collective-permute-start(bf16[2,128,512]{2,1,0:T(8,128)(2,1)S(1)} %get-tuple-element.53.refs_7_), channel_id=1, source_target_pairs={{4,6},{12,14},{20,22},{28,30}} | collective-permute-start | bytes 786440 | tf_op jit(solution)/shard_map/ppermute | solution.py:407
  45.3 8.3 %collective-permute-start.17 = (bf16[2,128,512]{2,1,0:T(8,128)(2,1)S(1)}, bf16[2,128,512]{2,1,0:T(8,128)(2,1)S(1)}, u32[]{:S(2)}, u32[]{:S(2)}) collective-permute-start(bf16[2,128,512]{2,1,0:T(8,128)(2,1)S(1)} %get-tuple-element.51.refs_0_.refs_6_), channel_id=1, source_target_pairs={{4,6},{12,14},{20,22},{28,30}} | collective-permute-start | bytes 786440 | tf_op jit(solution)/shard_map/ppermute | solution.py:407
  46.0 8.9 %collective-permute-start.18 = (bf16[2,128,512]{2,1,0:T(8,128)(2,1)S(1)}, bf16[2,128,512]{2,1,0:T(8,128)(2,1)S(1)}, u32[]{:S(2)}, u32[]{:S(2)}) collective-permute-start(bf16[2,128,512]{2,1,0:T(8,128)(2,1)S(1)} %collective-permute-done.13.refs_2_.refs_1_), channel_id=1, source_target_pairs={{5,7},{13,15},{21,23},{29,31}} | collective-permute-start | bytes 786440 | tf_op jit(solution)/shard_map/ppermute | solution.py:407
  49.6 6.4 %collective-permute-start.19 = (bf16[2,128,512]{2,1,0:T(8,128)(2,1)S(1)}, bf16[2,128,512]{2,1,0:T(8,128)(2,1)S(1)}, u32[]{:S(2)}, u32[]{:S(2)}) collective-permute-start(bf16[2,128,512]{2,1,0:T(8,128)(2,1)S(1)} %get-tuple-element.54), channel_id=1, source_target_pairs={{5,6},{6,7},{7,4},{4,5},{0,1},{1,0},{2,3},{3,2},{13,14},{14,15},{1... | collective-permute-start | bytes 786440 | tf_op jit(solution)/shard_map/ppermute | solution.py:407
  51.6 5.1 %collective-permute-start.21 = (bf16[2,128,512]{2,1,0:T(8,128)(2,1)S(1)}, bf16[2,128,512]{2,1,0:T(8,128)(2,1)S(1)}, u32[]{:S(2)}, u32[]{:S(2)}) collective-permute-start(bf16[2,128,512]{2,1,0:T(8,128)(2,1)S(1)} %get-tuple-element.55.refs_6_.refs_0_), channel_id=1, source_target_pairs={{5,3},{4,2},{13,11},{12,10},{21,19},{20,18},{29,27},{28,26}} | collective-permute-start | bytes 786440 | tf_op jit(solution)/shard_map/ppermute | solution.py:407
  52.3 18.8 %collective-permute-start.20 = (bf16[2,128,512]{2,1,0:T(8,128)(2,1)S(1)}, bf16[2,128,512]{2,1,0:T(8,128)(2,1)S(1)}, u32[]{:S(2)}, u32[]{:S(2)}) collective-permute-start(bf16[2,128,512]{2,1,0:T(8,128)(2,1)S(1)} %get-tuple-element.55.refs_6_.refs_0_), channel_id=1, source_target_pairs={{5,1},{4,0},{13,9},{12,8},{21,17},{20,16},{29,25},{28,24}} | collective-permute-start | bytes 786440 | tf_op jit(solution)/shard_map/ppermute | solution.py:407
  53.6 18.0 %collective-permute-start.25 = (bf16[2,128,512]{2,1,0:T(8,128)(2,1)S(1)}, bf16[2,128,512]{2,1,0:T(8,128)(2,1)S(1)}, u32[]{:S(2)}, u32[]{:S(2)}) collective-permute-start(bf16[2,128,512]{2,1,0:T(8,128)(2,1)S(1)} %get-tuple-element.51.refs_0_.refs_6_), channel_id=1, source_target_pairs={{2,0},{3,1},{10,8},{11,9},{18,16},{19,17},{26,24},{27,25}} | collective-permute-start | bytes 786440 | tf_op jit(solution)/shard_map/ppermute | solution.py:407
  54.9 20.3 %collective-permute-start.24 = (bf16[2,128,512]{2,1,0:T(8,128)(2,1)S(1)}, bf16[2,128,512]{2,1,0:T(8,128)(2,1)S(1)}, u32[]{:S(2)}, u32[]{:S(2)}) collective-permute-start(bf16[2,128,512]{2,1,0:T(8,128)(2,1)S(1)} %collective-permute-done.13.refs_2_.refs_1_), channel_id=1, source_target_pairs={{6,7},{14,15},{22,23},{30,31}} | collective-permute-start | bytes 786440 | tf_op jit(solution)/shard_map/ppermute | solution.py:407
  56.0 23.1 %collective-permute-start.22 = (bf16[2,128,512]{2,1,0:T(8,128)(2,1)S(1)}, bf16[2,128,512]{2,1,0:T(8,128)(2,1)S(1)}, u32[]{:S(2)}, u32[]{:S(2)}) collective-permute-start(bf16[2,128,512]{2,1,0:T(8,128)(2,1)S(1)} %get-tuple-element.55.refs_6_.refs_0_), channel_id=1, source_target_pairs={{5,7},{13,15},{21,23},{29,31}} | collective-permute-start | bytes 786440 | tf_op jit(solution)/shard_map/ppermute | solution.py:407
  56.7 21.0 %collective-permute-start.23 = (bf16[2,128,512]{2,1,0:T(8,128)(2,1)S(1)}, bf16[2,128,512]{2,1,0:T(8,128)(2,1)S(1)}, u32[]{:S(2)}, u32[]{:S(2)}) collective-permute-start(bf16[2,128,512]{2,1,0:T(8,128)(2,1)S(1)} %collective-permute-done.17.refs_2_.refs_3_), channel_id=1, source_target_pairs={{6,7},{14,15},{22,23},{30,31}} | collective-permute-start | bytes 786440 | tf_op jit(solution)/shard_map/ppermute | solution.py:407
  71.2 9.4 %collective-permute-start.30 = (bf16[2,128,512]{2,1,0:T(8,128)(2,1)S(1)}, bf16[2,128,512]{2,1,0:T(8,128)(2,1)S(1)}, u32[]{:S(2)}, u32[]{:S(2)}) collective-permute-start(bf16[2,128,512]{2,1,0:T(8,128)(2,1)S(1)} %get-tuple-element.58), channel_id=1, source_target_pairs={{0,1},{1,0},{2,3},{3,2},{4,5},{5,4},{6,7},{7,6},{8,9},{9,8},{10,11... | collective-permute-start | bytes 786440 | tf_op jit(solution)/shard_map/ppermute | solution.py:407
  71.5 11.0 %collective-permute-start.26 = (bf16[2,128,512]{2,1,0:T(8,128)(2,1)S(1)}, bf16[2,128,512]{2,1,0:T(8,128)(2,1)S(1)}, u32[]{:S(2)}, u32[]{:S(2)}) collective-permute-start(bf16[2,128,512]{2,1,0:T(8,128)(2,1)S(1)} %collective-permute-done.25.refs_4_), channel_id=1, source_target_pairs={{0,1},{1,0},{8,9},{9,8},{16,17},{17,16},{24,25},{25,24}} | collective-permute-start | bytes 786440 | tf_op jit(solution)/shard_map/ppermute | solution.py:407
  75.2 5.2 %copy-start.5 = (bf16[2,128,512]{2,1,0:T(8,128)(2,1)}, bf16[2,128,512]{2,1,0:T(8,128)(2,1)S(1)}, u32[]{:S(2)}) copy-start(bf16[2,128,512]{2,1,0:T(8,128)(2,1)S(1)} %collective-permute-done.24.refs_4_.refs_3_) | copy-start | bytes 786436
  75.2 8.7 %collective-permute-start.29 = (bf16[2,128,512]{2,1,0:T(8,128)(2,1)S(1)}, bf16[2,128,512]{2,1,0:T(8,128)(2,1)S(1)}, u32[]{:S(2)}, u32[]{:S(2)}) collective-permute-start(bf16[2,128,512]{2,1,0:T(8,128)(2,1)S(1)} %get-tuple-element.57.refs_0_.refs_6_), channel_id=1, source_target_pairs={{6,4},{14,12},{22,20},{30,28}} | collective-permute-start | bytes 786440 | tf_op jit(solution)/shard_map/ppermute | solution.py:407
  77.7 2.8 %copy-start.7 = (bf16[2,128,512]{2,1,0:T(8,128)(2,1)}, bf16[2,128,512]{2,1,0:T(8,128)(2,1)S(1)}, u32[]{:S(2)}) copy-start(bf16[2,128,512]{2,1,0:T(8,128)(2,1)S(1)} %collective-permute-done.23.refs_3_.refs_2_) | copy-start | bytes 786436
  77.7 12.2 %collective-permute-start.28 = (bf16[2,128,512]{2,1,0:T(8,128)(2,1)S(1)}, bf16[2,128,512]{2,1,0:T(8,128)(2,1)}, u32[]{:S(2)}, u32[]{:S(2)}) collective-permute-start(bf16[2,128,512]{2,1,0:T(8,128)(2,1)S(1)} %get-tuple-element.57.refs_0_.refs_6_), channel_id=1, source_target_pairs={{6,2},{14,10},{22,18},{30,26}} | collective-permute-start | bytes 786440 | tf_op jit(solution)/shard_map/ppermute | solution.py:407
  79.1 12.2 %collective-permute-start.27 = (bf16[2,128,512]{2,1,0:T(8,128)(2,1)S(1)}, bf16[2,128,512]{2,1,0:T(8,128)(2,1)}, u32[]{:S(2)}, u32[]{:S(2)}) collective-permute-start(bf16[2,128,512]{2,1,0:T(8,128)(2,1)S(1)} %get-tuple-element.57.refs_0_.refs_6_), channel_id=1, source_target_pairs={{6,0},{14,8},{22,16},{30,24}} | collective-permute-start | bytes 786440 | tf_op jit(solution)/shard_map/ppermute | solution.py:407
  81.4 13.8 %collective-permute-start.33 = (bf16[2,128,512]{2,1,0:T(8,128)(2,1)S(1)}, bf16[2,128,512]{2,1,0:T(8,128)(2,1)S(1)}, u32[]{:S(2)}, u32[]{:S(2)}) collective-permute-start(bf16[2,128,512]{2,1,0:T(8,128)(2,1)S(1)} %get-tuple-element.60.refs_5_.refs_6_.refs_8_.refs_0_.refs_2_.refs_4_.refs_7_), channel_id=1, source_target_pairs={{7,5},{15,13},{23,21},{31,29}} | collective-permute-start | bytes 786440 | tf_op jit(solution)/shard_map/ppermute | solution.py:407
  83.3 12.0 %collective-permute-start.32 = (bf16[2,128,512]{2,1,0:T(8,128)(2,1)S(1)}, bf16[2,128,512]{2,1,0:T(8,128)(2,1)S(1)}, u32[]{:S(2)}, u32[]{:S(2)}) collective-permute-start(bf16[2,128,512]{2,1,0:T(8,128)(2,1)S(1)} %get-tuple-element.60.refs_5_.refs_6_.refs_8_.refs_0_.refs_2_.refs_4_.refs_7_), channel_id=1, source_target_pairs={{7,3},{15,11},{23,19},{31,27}} | collective-permute-start | bytes 786440 | tf_op jit(solution)/shard_map/ppermute | solution.py:407
  83.9 11.3 %collective-permute-start.31 = (bf16[2,128,512]{2,1,0:T(8,128)(2,1)S(1)}, bf16[2,128,512]{2,1,0:T(8,128)(2,1)S(1)}, u32[]{:S(2)}, u32[]{:S(2)}) collective-permute-start(bf16[2,128,512]{2,1,0:T(8,128)(2,1)S(1)} %get-tuple-element.60.refs_5_.refs_6_.refs_8_.refs_0_.refs_2_.refs_4_.refs_7_), channel_id=1, source_target_pairs={{7,1},{15,9},{23,17},{31,25}} | collective-permute-start | bytes 786440 | tf_op jit(solution)/shard_map/ppermute | solution.py:407
  92.3 10.5 %collective-permute-start.35 = (bf16[2,128,512]{2,1,0:T(8,128)(2,1)S(1)}, bf16[2,128,512]{2,1,0:T(8,128)(2,1)S(1)}, u32[]{:S(2)}, u32[]{:S(2)}) collective-permute-start(bf16[2,128,512]{2,1,0:T(8,128)(2,1)S(1)} %get-tuple-element.63), channel_id=1, source_target_pairs={{0,1},{1,0},{2,3},{3,2},{4,5},{5,4},{6,7},{7,6},{8,9},{9,8},{10,11... | collective-permute-start | bytes 786440 | tf_op jit(solution)/shard_map/ppermute | solution.py:407
  95.5 10.5 %collective-permute-start.34 = (bf16[2,64,512]{2,1,0:T(8,128)(2,1)S(1)}, bf16[2,64,512]{2,1,0:T(8,128)(2,1)S(1)}, u32[]{:S(2)}, u32[]{:S(2)}) collective-permute-start(bf16[2,64,512]{2,1,0:T(8,128)(2,1)S(1)} %get-tuple-element.62), channel_id=1, source_target_pairs={{0,1},{1,0},{2,3},{3,2},{4,5},{5,4},{6,7},{7,6},{8,9},{9,8},{10,11... | collective-permute-start | bytes 393224 | tf_op jit(solution)/shard_map/ppermute | solution.py:407
  101.8 6.9 %collective-permute-start.36 = (bf16[2,64,512]{2,1,0:T(8,128)(2,1)S(1)}, bf16[2,64,512]{2,1,0:T(8,128)(2,1)S(1)}, u32[]{:S(2)}, u32[]{:S(2)}) collective-permute-start(bf16[2,64,512]{2,1,0:T(8,128)(2,1)S(1)} %get-tuple-element.64), channel_id=1, source_target_pairs={{0,1},{1,0},{2,3},{3,2},{4,5},{5,4},{6,7},{7,6},{8,9},{9,8},{10,11... | collective-permute-start | bytes 393224 | tf_op jit(solution)/shard_map/ppermute | solution.py:407
  107.7 5.0 %collective-permute-start.37 = (bf16[2,64,512]{2,1,0:T(8,128)(2,1)S(1)}, bf16[2,64,512]{2,1,0:T(8,128)(2,1)S(1)}, u32[]{:S(2)}, u32[]{:S(2)}) collective-permute-start(bf16[2,64,512]{2,1,0:T(8,128)(2,1)S(1)} %update_last_0.1.refs_0_), channel_id=1, source_target_pairs={{0,1},{1,0},{2,3},{3,2},{4,5},{5,4},{6,7},{7,6},{8,9},{9,8},{10,11... | collective-permute-start | bytes 393224 | tf_op jit(solution)/shard_map/ppermute | solution.py:407
  110.5 5.0 %collective-permute-start.38 = (bf16[2,64,512]{2,1,0:T(8,128)(2,1)S(1)}, bf16[2,64,512]{2,1,0:T(8,128)(2,1)S(1)}, u32[]{:S(2)}, u32[]{:S(2)}) collective-permute-start(bf16[2,64,512]{2,1,0:T(8,128)(2,1)S(1)} %update_last_1.1.refs_1_), channel_id=1, source_target_pairs={{0,1},{1,0},{2,3},{3,2},{4,5},{5,4},{6,7},{7,6},{8,9},{9,8},{10,11... | collective-permute-start | bytes 393224 | tf_op jit(solution)/shard_map/ppermute | solution.py:407
  115.6 20.2 %copy-start.11 = (f32[1,2,128,512]{3,2,1,0:T(8,128)S(1)}, f32[1,2,128,512]{3,2,1,0:T(8,128)}, u32[]{:S(2)}) copy-start(f32[1,2,128,512]{3,2,1,0:T(8,128)} %param.13) | copy-start | bytes 1572868
  117.1 9.5 %collective-permute-start.39 = (bf16[2,128,512]{2,1,0:T(8,128)(2,1)S(1)}, bf16[2,128,512]{2,1,0:T(8,128)(2,1)S(1)}, u32[]{:S(2)}, u32[]{:S(2)}) collective-permute-start(bf16[2,128,512]{2,1,0:T(8,128)(2,1)S(1)} %get-tuple-element.66), channel_id=1, source_target_pairs={{0,2},{1,3},{2,0},{3,1},{4,6},{5,7},{6,4},{7,5},{8,10},{9,11},{10,... | collective-permute-start | bytes 786440 | tf_op jit(solution)/shard_map/ppermute | solution.py:407
  117.2 16.6 %collective-permute-start.40 = (bf16[2,128,512]{2,1,0:T(8,128)(2,1)S(1)}, bf16[2,128,512]{2,1,0:T(8,128)(2,1)S(1)}, u32[]{:S(2)}, u32[]{:S(2)}) collective-permute-start(bf16[2,128,512]{2,1,0:T(8,128)(2,1)S(1)} %get-tuple-element.67), channel_id=1, source_target_pairs={{0,4},{1,5},{2,6},{3,7},{4,0},{5,1},{6,2},{7,3},{8,12},{9,13},{10,... | collective-permute-start | bytes 786440 | tf_op jit(solution)/shard_map/ppermute | solution.py:407
  119.9 13.9 %collective-permute-start.41 = (bf16[2,128,512]{2,1,0:T(8,128)(2,1)S(1)}, bf16[2,128,512]{2,1,0:T(8,128)(2,1)S(1)}, u32[]{:S(2)}, u32[]{:S(2)}) collective-permute-start(bf16[2,128,512]{2,1,0:T(8,128)(2,1)S(1)} %get-tuple-element.68), channel_id=1, source_target_pairs={{0,6},{1,7},{2,4},{3,5},{4,2},{5,3},{6,0},{7,1},{8,14},{9,15},{10,... | collective-permute-start | bytes 786440 | tf_op jit(solution)/shard_map/ppermute | solution.py:407
  134.1 1.6 %collective-permute-start.42 = (bf16[2,128,512]{2,1,0:T(8,128)(2,1)S(1)}, bf16[2,128,512]{2,1,0:T(8,128)(2,1)S(1)}, u32[]{:S(2)}, u32[]{:S(2)}) collective-permute-start(bf16[2,128,512]{2,1,0:T(8,128)(2,1)S(1)} %select_convert_fusion), channel_id=1, source_target_pairs={{0,8},{8,0},{16,24},{24,16},{1,9},{9,1},{17,25},{25,17},{2,10},{10... | collective-permute-start | bytes 786440 | tf_op jit(solution)/shard_map/ppermute | solution.py:475
  (7 other events, 7.1 us)

commit v6 on v5

--- a/solution.py
+++ b/solution.py
@@ -43,7 +43,7 @@
         ((4, 2), ((0, 1), (1, 0)), 6),
     ),
     ((OWN, ((6, 4),), 7), (OWN, ((6, 2),), 7), (OWN, ((6, 0),), 7)),
-    ((OWN, ((7, 5),), 8), (OWN, ((7, 3),), 8), (OWN, ((7, 1),), 8)),
+    ((OWN, ((7, 1),), 8), (OWN, ((7, 3),), 8), (OWN, ((7, 5),), 8)),
 )
 
 

time: 139 us -> 139 us (level)
  no operation moved by 1% of the time
where the time goes in v6:
time: 139 us; the launch traced here: 137 us
  waiting for transfers between devices  52.3 us (38%)
  starting transfers between devices  51.4 us (37%)
  Pallas kernels  22.6 us (16%)
  local copies, waits for them, and re-layouts  6.69 us (5%)
  other arithmetic  2.45 us (2%)
  between operations  1.44 us (1%)
    ppermute x42, starting transfers between devices, send(): return lax.ppermute(value, 'panel', edges)  51.3 us
    ppermute x42, waiting for transfers between devices, send(): return lax.ppermute(value, 'panel', edges)  50.8 us
    pallas_call x18, Pallas kernels, accumulate(): pl.pallas_call(functools.partial(gather_kernel, [item[1] for item in item...  16.7 us
    unnamed x24, local copies, waits for them, and re-layouts  5.75 us
  transfers between devices with their start and end apart: 43, of which 16 were waited for; matrix products, arithmetic and copies ran while one was open for 1% of the time, Pallas kernels for 15%

profile of v6, /device:TPU:0, one launch (start us, length us, event | category | flops | bytes accessed | tf_op | source)
XLA Modules:
  0.0 136.9 jit_solution(12344781933066044074)
XLA Ops:
  0.6 1.2 copy-done
  1.9 0.9 copy-done.2
  3.3 2.6 %collective-permute-start = (bf16[2,128,512]{2,1,0:T(8,128)(2,1)S(1)}, bf16[2,128,512]{2,1,0:T(8,128)(2,1)S(1)}, u32[]{:S(2)}, u32[]{:S(2)}) collective-permute-start(bf16[2,128,512]{2,1,0:T(8,128)(2,1)S(1)} %get-tuple-element.38), channel_id=1, source_target_pairs={{0,1},{1,0},{2,3},{3,2},{4,5},{5,4},{6,7},{7,6},{8,9},{9,8},{10,11... | collective-permute-start | bytes 786440 | tf_op jit(solution)/shard_map/ppermute | solution.py:407
  5.9 3.6 %collective-permute-start.3 = (bf16[2,128,512]{2,1,0:T(8,128)(2,1)S(1)}, bf16[2,128,512]{2,1,0:T(8,128)(2,1)S(1)}, u32[]{:S(2)}, u32[]{:S(2)}) collective-permute-start(bf16[2,128,512]{2,1,0:T(8,128)(2,1)S(1)} %get-tuple-element.36.refs_0_.refs_6_), channel_id=1, source_target_pairs={{0,2},{8,10},{16,18},{24,26}} | collective-permute-start | bytes 786440 | tf_op jit(solution)/shard_map/ppermute | solution.py:407
  9.5 1.7 %collective-permute-start.2 = (bf16[2,128,512]{2,1,0:T(8,128)(2,1)S(1)}, bf16[2,128,512]{2,1,0:T(8,128)(2,1)S(1)}, u32[]{:S(2)}, u32[]{:S(2)}) collective-permute-start(bf16[2,128,512]{2,1,0:T(8,128)(2,1)S(1)} %get-tuple-element.36.refs_0_.refs_6_), channel_id=1, source_target_pairs={{0,4},{8,12},{16,20},{24,28}} | collective-permute-start | bytes 786440 | tf_op jit(solution)/shard_map/ppermute | solution.py:407
  11.2 1.7 %collective-permute-start.1 = (bf16[2,128,512]{2,1,0:T(8,128)(2,1)S(1)}, bf16[2,128,512]{2,1,0:T(8,128)(2,1)S(1)}, u32[]{:S(2)}, u32[]{:S(2)}) collective-permute-start(bf16[2,128,512]{2,1,0:T(8,128)(2,1)S(1)} %get-tuple-element.36.refs_0_.refs_6_), channel_id=1, source_target_pairs={{0,6},{8,14},{16,22},{24,30}} | collective-permute-start | bytes 786440 | tf_op jit(solution)/shard_map/ppermute | solution.py:407
  12.9 1.3 setup.1
  14.8 1.7 %update_0.1.refs_0_.refs_6_ = f32[2,128,512]{2,1,0:T(8,128)S(1)} custom-call(s32[1]{0:T(128)} %bitcast.place_ref, bf16[2,128,512]{2,1,0:T(8,128)(2,1)S(1)} %get-tuple-element.36.refs_0_.refs_6_, bf16[1,2,512,4096]{3,2,1,0:T(8,128)(2,1)} %refs_1_.21, f32[2,128,512]{2,1,0:T(8,128)S(1)} %get-tuple-element.37.refs_2_.refs_0_), custom_call_target="tpu_custom_call" | custom-call | tf_op jit(solution)/shard_map/update_0/pallas_call | solution.py:288
  17.9 3.9 %collective-permute-done.2.refs_2_.refs_8_.refs_3_ = bf16[2,128,512]{2,1,0:T(8,128)(2,1)S(1)} collective-permute-done((bf16[2,128,512]{2,1,0:T(8,128)(2,1)S(1)}, bf16[2,128,512]{2,1,0:T(8,128)(2,1)S(1)}, u32[]{:S(2)}, u32[]{:S(2)}) %collective-permute-start.2) | collective-permute-done | bytes 262176 | tf_op jit(solution)/shard_map/ppermute | solution.py:407
  22.5 3.5 %collective-permute-done.1.refs_1_.refs_9_.refs_2_ = bf16[2,128,512]{2,1,0:T(8,128)(2,1)S(1)} collective-permute-done((bf16[2,128,512]{2,1,0:T(8,128)(2,1)S(1)}, bf16[2,128,512]{2,1,0:T(8,128)(2,1)S(1)}, u32[]{:S(2)}, u32[]{:S(2)}) %collective-permute-start.1) | collective-permute-done | bytes 262176 | tf_op jit(solution)/shard_map/ppermute | solution.py:407
  28.6 5.2 %collective-permute-done.9.refs_0_.refs_5_.refs_1_ = bf16[2,128,512]{2,1,0:T(8,128)(2,1)S(1)} collective-permute-done((bf16[2,128,512]{2,1,0:T(8,128)(2,1)S(1)}, bf16[2,128,512]{2,1,0:T(8,128)(2,1)S(1)}, u32[]{:S(2)}, u32[]{:S(2)}) %collective-permute-start.9) | collective-permute-done | bytes 262176 | tf_op jit(solution)/shard_map/ppermute | solution.py:407
  33.9 3.6 %collective-permute-start.12 = (bf16[2,128,512]{2,1,0:T(8,128)(2,1)S(1)}, bf16[2,128,512]{2,1,0:T(8,128)(2,1)S(1)}, u32[]{:S(2)}, u32[]{:S(2)}) collective-permute-start(bf16[2,128,512]{2,1,0:T(8,128)(2,1)S(1)} %get-tuple-element.48), channel_id=1, source_target_pairs={{3,4},{4,5},{5,2},{2,3},{0,1},{1,0},{6,7},{7,6},{11,12},{12,13},{1... | collective-permute-start | bytes 786440 | tf_op jit(solution)/shard_map/ppermute | solution.py:407
  39.1 3.7 %collective-permute-done.12.refs_5_.refs_1_.refs_0_ = bf16[2,128,512]{2,1,0:T(8,128)(2,1)S(1)} collective-permute-done((bf16[2,128,512]{2,1,0:T(8,128)(2,1)S(1)}, bf16[2,128,512]{2,1,0:T(8,128)(2,1)S(1)}, u32[]{:S(2)}, u32[]{:S(2)}) %collective-permute-start.12) | collective-permute-done | bytes 262176 | tf_op jit(solution)/shard_map/ppermute | solution.py:407
  42.8 1.8 %collective-permute-start.15 = (bf16[2,128,512]{2,1,0:T(8,128)(2,1)S(1)}, bf16[2,128,512]{2,1,0:T(8,128)(2,1)S(1)}, u32[]{:S(2)}, u32[]{:S(2)}) collective-permute-start(bf16[2,128,512]{2,1,0:T(8,128)(2,1)S(1)} %get-tuple-element.52), channel_id=1, source_target_pairs={{0,1},{1,0},{2,3},{3,2},{4,5},{5,4},{6,7},{7,6},{8,9},{9,8},{10,11... | collective-permute-start | bytes 786440 | tf_op jit(solution)/shard_map/ppermute | solution.py:407
  46.7 1.8 %update_3.1.refs_5_.refs_0_ = f32[2,128,512]{2,1,0:T(8,128)S(1)} custom-call(s32[1]{0:T(128)} %bitcast.place_ref, bf16[2,128,512]{2,1,0:T(8,128)(2,1)S(1)} %get-tuple-element.49.refs_6_.refs_0_, bf16[2,128,512]{2,1,0:T(8,128)(2,1)S(1)} %collective-permute-done.9.refs_0_.refs_5_.refs_1_, bf16[2,128,512]{2,1,0:T(8,128)(2,1)S(1)} %collective-permute-done.10.refs_1_.refs_2_, ...), custom_call_target="tpu_custom_call" | custom-call | tf_op jit(solution)/shard_map/update_3/pallas_call | solution.py:288
  48.6 0.9 collective-permute-done.15.refs_0_.refs_5_.refs_1_
  49.6 2.0 %collective-permute-start.19 = (bf16[2,128,512]{2,1,0:T(8,128)(2,1)S(1)}, bf16[2,128,512]{2,1,0:T(8,128)(2,1)S(1)}, u32[]{:S(2)}, u32[]{:S(2)}) collective-permute-start(bf16[2,128,512]{2,1,0:T(8,128)(2,1)S(1)} %get-tuple-element.54), channel_id=1, source_target_pairs={{5,6},{6,7},{7,4},{4,5},{0,1},{1,0},{2,3},{3,2},{13,14},{14,15},{1... | collective-permute-start | bytes 786440 | tf_op jit(solution)/shard_map/ppermute | solution.py:407
  52.3 1.3 collective-permute-start.20
  53.6 1.3 collective-permute-start.25
  57.3 13.8 %collective-permute-done.20.refs_8_.refs_6_.refs_1_ = bf16[2,128,512]{2,1,0:T(8,128)(2,1)S(1)} collective-permute-done((bf16[2,128,512]{2,1,0:T(8,128)(2,1)S(1)}, bf16[2,128,512]{2,1,0:T(8,128)(2,1)S(1)}, u32[]{:S(2)}, u32[]{:S(2)}) %collective-permute-start.20) | collective-permute-done | bytes 262176 | tf_op jit(solution)/shard_map/ppermute | solution.py:407
  71.5 3.6 %collective-permute-start.26 = (bf16[2,128,512]{2,1,0:T(8,128)(2,1)S(1)}, bf16[2,128,512]{2,1,0:T(8,128)(2,1)S(1)}, u32[]{:S(2)}, u32[]{:S(2)}) collective-permute-start(bf16[2,128,512]{2,1,0:T(8,128)(2,1)S(1)} %collective-permute-done.25.refs_4_), channel_id=1, source_target_pairs={{0,1},{1,0},{8,9},{9,8},{16,17},{17,16},{24,25},{25,24}} | collective-permute-start | bytes 786440 | tf_op jit(solution)/shard_map/ppermute | solution.py:407
  75.9 1.8 %update_5.1.refs_9_.refs_0_ = f32[2,128,512]{2,1,0:T(8,128)S(1)} custom-call(s32[1]{0:T(128)} %bitcast.place_ref, bf16[2,128,512]{2,1,0:T(8,128)(2,1)S(1)} %get-tuple-element.55.refs_6_.refs_0_, bf16[2,128,512]{2,1,0:T(8,128)(2,1)S(1)} %collective-permute-done.15.refs_0_.refs_5_.refs_1_, bf16[2,128,512]{2,1,0:T(8,128)(2,1)S(1)} %collective-permute-done.16.refs_1_.refs_2_, ...), custom_call_target="tpu_custom_call" | custom-call | tf_op jit(solution)/shard_map/update_5/pallas_call | solution.py:288
  77.7 1.4 %collective-permute-start.28 = (bf16[2,128,512]{2,1,0:T(8,128)(2,1)S(1)}, bf16[2,128,512]{2,1,0:T(8,128)(2,1)}, u32[]{:S(2)}, u32[]{:S(2)}) collective-permute-start(bf16[2,128,512]{2,1,0:T(8,128)(2,1)S(1)} %get-tuple-element.57.refs_0_.refs_6_), channel_id=1, source_target_pairs={{6,2},{14,10},{22,18},{30,26}} | collective-permute-start | bytes 786440 | tf_op jit(solution)/shard_map/ppermute | solution.py:407
  79.1 1.3 collective-permute-start.27
  80.6 0.8 solve_7.1
  84.8 0.9 copy-done.6
  85.7 0.9 copy-done.8
  86.7 0.9 copy-done.10
  87.6 2.3 %update_6.1.settled_ref.refs_6_ = f32[2,128,512]{2,1,0:T(8,128)S(1)} custom-call(s32[1]{0:T(128)} %bitcast.place_ref, bf16[2,128,512]{2,1,0:T(8,128)(2,1)S(1)} %get-tuple-element.57.refs_0_.refs_6_, bf16[2,128,512]{2,1,0:T(8,128)(2,1)S(1)} %collective-permute-done.19.refs_5_.refs_1_.refs_0_, ...), custom_call_target="tpu_custom_call" | custom-call | tf_op jit(solution)/shard_map/update_6/pallas_call | solution.py:288
  89.9 1.4 collective-permute-done.27.refs_0_.refs_4_
  91.3 1.1 pick_first.1
  92.4 2.8 %update_7.1.settled_ref.refs_2_ = f32[2,128,512]{2,1,0:T(8,128)S(1)} custom-call(s32[1]{0:T(128)} %bitcast.place_ref, bf16[2,128,512]{2,1,0:T(8,128)(2,1)S(1)} %get-tuple-element.60.refs_5_.refs_6_.refs_8_.refs_0_.refs_2_.refs_4_.refs_7_, bf16[2,128,512]{2,1,0:T(8,128)(2,1)S(1)} %collective-permute-done.30.refs_5_.refs_1_, ...), custom_call_target="tpu_custom_call" | custom-call | tf_op jit(solution)/shard_map/update_7/pallas_call | solution.py:288
  95.5 6.3 %collective-permute-start.34 = (bf16[2,64,512]{2,1,0:T(8,128)(2,1)S(1)}, bf16[2,64,512]{2,1,0:T(8,128)(2,1)S(1)}, u32[]{:S(2)}, u32[]{:S(2)}) collective-permute-start(bf16[2,64,512]{2,1,0:T(8,128)(2,1)S(1)} %get-tuple-element.62), channel_id=1, source_target_pairs={{0,1},{1,0},{2,3},{3,2},{4,5},{5,4},{6,7},{7,6},{8,9},{9,8},{10,11... | collective-permute-start | bytes 393224 | tf_op jit(solution)/shard_map/ppermute | solution.py:407
  102.0 0.9 fusion.8
  102.8 1.7 %update_mid.1.refs_4_ = f32[2,128,512]{2,1,0:T(8,128)S(1)} custom-call(s32[1]{0:T(128)} %bitcast.place_ref, bf16[2,128,512]{2,1,0:T(8,128)(2,1)S(1)} %collective-permute-done.35.refs_0_, bf16[1,2,512,4096]{3,2,1,0:T(8,128)(2,1)} %refs_1_.21, f32[2,128,512]{2,1,0:T(8,128)S(1)} %update_7.1.settled_ref.refs_2_), custom_call_target="tpu_custom_call" | custom-call | tf_op jit(solution)/shard_map/update_mid/pallas_call | solution.py:288
  104.7 1.3 collective-permute-done.34.refs_0_
  106.0 1.8 %update_last_0.1.refs_0_ = bf16[2,64,512]{2,1,0:T(8,128)(2,1)S(1)} custom-call(s32[1]{0:T(128)} %bitcast.place_ref, bf16[2,64,512]{2,1,0:T(8,128)(2,1)S(1)} %collective-permute-done.34.refs_0_, bf16[1,2,512,4096]{3,2,1,0:T(8,128)(2,1)} %refs_1_.21, f32[2,128,512]{2,1,0:T(8,128)S(1)} %update_late.1.refs_2_, bf16[1,2,128,512]{3,2,1,0:T(8,128)(2,1)S(1)} %copy-done.4), custom_call_target="tpu_custom_call" | custom-call | tf_op jit(solution)/shard_map/update_last_0/pallas_call | solution.py:288
  108.8 1.8 %update_last_1.1.refs_1_ = bf16[2,64,512]{2,1,0:T(8,128)(2,1)S(1)} custom-call(s32[1]{0:T(128)} %bitcast.place_ref, bf16[2,64,512]{2,1,0:T(8,128)(2,1)S(1)} %collective-permute-done.36.refs_0_, bf16[1,2,512,4096]{3,2,1,0:T(8,128)(2,1)} %refs_1_.21, f32[2,128,512]{2,1,0:T(8,128)S(1)} %update_late.1.refs_2_, bf16[1,2,128,512]{3,2,1,0:T(8,128)(2,1)S(1)} %copy-done.4), custom_call_target="tpu_custom_call" | custom-call | tf_op jit(solution)/shard_map/update_last_1/pallas_call | solution.py:288
  110.6 0.9 compare_convert_fusion
  111.5 1.2 collective-permute-done.37.refs_2_
  112.8 2.8 %collective-permute-done.38.refs_3_ = bf16[2,64,512]{2,1,0:T(8,128)(2,1)S(1)} collective-permute-done((bf16[2,64,512]{2,1,0:T(8,128)(2,1)S(1)}, bf16[2,64,512]{2,1,0:T(8,128)(2,1)S(1)}, u32[]{:S(2)}, u32[]{:S(2)}) %collective-permute-start.38) | collective-permute-done | bytes 131104 | tf_op jit(solution)/shard_map/ppermute | solution.py:407
  115.6 1.6 %place_rows.1 = (bf16[2,128,512]{2,1,0:T(8,128)(2,1)S(1)}, bf16[2,128,512]{2,1,0:T(8,128)(2,1)S(1)}, bf16[2,128,512]{2,1,0:T(8,128)(2,1)S(1)}, bf16[2,128,512]{2,1,0:T(8,128)(2,1)S(1)}, bf16[2,128,512]{2,1,0:T(8,128)(2,1)S(1)}) custom-call(bf16[2,64,512]{2,1,0:T(8,128)(2,1)S(1)} %update_last_0.1.refs_0_, bf16[2,64,512]{2,1,0:T(8,128)(2,1)S(1)} %update_last_1.1.refs_1_, ...), custom_call_target="tpu_custom_call" | custom-call | tf_op jit(solution)/shard_map/place_rows/pallas_call | solution.py:370
  117.2 2.6 %collective-permute-start.40 = (bf16[2,128,512]{2,1,0:T(8,128)(2,1)S(1)}, bf16[2,128,512]{2,1,0:T(8,128)(2,1)S(1)}, u32[]{:S(2)}, u32[]{:S(2)}) collective-permute-start(bf16[2,128,512]{2,1,0:T(8,128)(2,1)S(1)} %get-tuple-element.67), channel_id=1, source_target_pairs={{0,4},{1,5},{2,6},{3,7},{4,0},{5,1},{6,2},{7,3},{8,12},{9,13},{10,... | collective-permute-start | bytes 786440 | tf_op jit(solution)/shard_map/ppermute | solution.py:407
  119.9 1.7 %collective-permute-start.41 = (bf16[2,128,512]{2,1,0:T(8,128)(2,1)S(1)}, bf16[2,128,512]{2,1,0:T(8,128)(2,1)S(1)}, u32[]{:S(2)}, u32[]{:S(2)}) collective-permute-start(bf16[2,128,512]{2,1,0:T(8,128)(2,1)S(1)} %get-tuple-element.68), channel_id=1, source_target_pairs={{0,6},{1,7},{2,4},{3,5},{4,2},{5,3},{6,0},{7,1},{8,14},{9,15},{10,... | collective-permute-start | bytes 786440 | tf_op jit(solution)/shard_map/ppermute | solution.py:407
  121.6 5.0 %collective-permute-done.39 = bf16[2,128,512]{2,1,0:T(8,128)(2,1)S(1)} collective-permute-done((bf16[2,128,512]{2,1,0:T(8,128)(2,1)S(1)}, bf16[2,128,512]{2,1,0:T(8,128)(2,1)S(1)}, u32[]{:S(2)}, u32[]{:S(2)}) %collective-permute-start.39) | collective-permute-done | bytes 262176 | tf_op jit(solution)/shard_map/ppermute | solution.py:407
  126.6 7.2 %collective-permute-done.40 = bf16[2,128,512]{2,1,0:T(8,128)(2,1)S(1)} collective-permute-done((bf16[2,128,512]{2,1,0:T(8,128)(2,1)S(1)}, bf16[2,128,512]{2,1,0:T(8,128)(2,1)S(1)}, u32[]{:S(2)}, u32[]{:S(2)}) %collective-permute-start.40) | collective-permute-done | bytes 262176 | tf_op jit(solution)/shard_map/ppermute | solution.py:407
  134.2 1.5 %collective-permute-done.42 = bf16[2,128,512]{2,1,0:T(8,128)(2,1)S(1)} collective-permute-done((bf16[2,128,512]{2,1,0:T(8,128)(2,1)S(1)}, bf16[2,128,512]{2,1,0:T(8,128)(2,1)S(1)}, u32[]{:S(2)}, u32[]{:S(2)}) %collective-permute-start.42) | collective-permute-done | bytes 262176 | tf_op jit(solution)/shard_map/ppermute | solution.py:475
  135.7 1.2 fusion.7
  (98 shorter events, 19.3 us)
Async XLA Ops:
  3.3 11.0 %collective-permute-start = (bf16[2,128,512]{2,1,0:T(8,128)(2,1)S(1)}, bf16[2,128,512]{2,1,0:T(8,128)(2,1)S(1)}, u32[]{:S(2)}, u32[]{:S(2)}) collective-permute-start(bf16[2,128,512]{2,1,0:T(8,128)(2,1)S(1)} %get-tuple-element.38), channel_id=1, source_target_pairs={{0,1},{1,0},{2,3},{3,2},{4,5},{5,4},{6,7},{7,6},{8,9},{9,8},{10,11... | collective-permute-start | bytes 786440 | tf_op jit(solution)/shard_map/ppermute | solution.py:407
  5.9 8.4 %copy-start.1 = (bf16[1,2,512,512]{3,2,1,0:T(8,128)(2,1)S(1)}, bf16[1,2,512,512]{3,2,1,0:T(8,128)(2,1)}, u32[]{:S(2)}) copy-start(bf16[1,2,512,512]{3,2,1,0:T(8,128)(2,1)} %refs_4_.23) | copy-start | bytes 3145732
  5.9 8.4 %copy-start.3 = (bf16[1,2,128,512]{3,2,1,0:T(8,128)(2,1)S(1)}, bf16[1,2,128,512]{3,2,1,0:T(8,128)(2,1)}, u32[]{:S(2)}) copy-start(bf16[1,2,128,512]{3,2,1,0:T(8,128)(2,1)} %refs_1_.18) | copy-start | bytes 786436
  5.9 11.4 %collective-permute-start.3 = (bf16[2,128,512]{2,1,0:T(8,128)(2,1)S(1)}, bf16[2,128,512]{2,1,0:T(8,128)(2,1)S(1)}, u32[]{:S(2)}, u32[]{:S(2)}) collective-permute-start(bf16[2,128,512]{2,1,0:T(8,128)(2,1)S(1)} %get-tuple-element.36.refs_0_.refs_6_), channel_id=1, source_target_pairs={{0,2},{8,10},{16,18},{24,26}} | collective-permute-start | bytes 786440 | tf_op jit(solution)/shard_map/ppermute | solution.py:407
  9.5 12.3 %collective-permute-start.2 = (bf16[2,128,512]{2,1,0:T(8,128)(2,1)S(1)}, bf16[2,128,512]{2,1,0:T(8,128)(2,1)S(1)}, u32[]{:S(2)}, u32[]{:S(2)}) collective-permute-start(bf16[2,128,512]{2,1,0:T(8,128)(2,1)S(1)} %get-tuple-element.36.refs_0_.refs_6_), channel_id=1, source_target_pairs={{0,4},{8,12},{16,20},{24,28}} | collective-permute-start | bytes 786440 | tf_op jit(solution)/shard_map/ppermute | solution.py:407
  11.2 14.8 %collective-permute-start.1 = (bf16[2,128,512]{2,1,0:T(8,128)(2,1)S(1)}, bf16[2,128,512]{2,1,0:T(8,128)(2,1)S(1)}, u32[]{:S(2)}, u32[]{:S(2)}) collective-permute-start(bf16[2,128,512]{2,1,0:T(8,128)(2,1)S(1)} %get-tuple-element.36.refs_0_.refs_6_), channel_id=1, source_target_pairs={{0,6},{8,14},{16,22},{24,30}} | collective-permute-start | bytes 786440 | tf_op jit(solution)/shard_map/ppermute | solution.py:407
  14.3 12.5 %collective-permute-start.4 = (bf16[2,128,512]{2,1,0:T(8,128)(2,1)S(1)}, bf16[2,128,512]{2,1,0:T(8,128)(2,1)S(1)}, u32[]{:S(2)}, u32[]{:S(2)}) collective-permute-start(bf16[2,128,512]{2,1,0:T(8,128)(2,1)S(1)} %get-tuple-element.42), channel_id=1, source_target_pairs={{1,2},{2,3},{3,0},{0,1},{4,5},{5,4},{6,7},{7,6},{9,10},{10,11},{11... | collective-permute-start | bytes 786440 | tf_op jit(solution)/shard_map/ppermute | solution.py:407
  16.6 11.2 %collective-permute-start.8 = (bf16[2,128,512]{2,1,0:T(8,128)(2,1)S(1)}, bf16[2,128,512]{2,1,0:T(8,128)(2,1)S(1)}, u32[]{:S(2)}, u32[]{:S(2)}) collective-permute-start(bf16[2,128,512]{2,1,0:T(8,128)(2,1)S(1)} %get-tuple-element.43.refs_6_.refs_0_), channel_id=1, source_target_pairs={{1,3},{9,11},{17,19},{25,27}} | collective-permute-start | bytes 786440 | tf_op jit(solution)/shard_map/ppermute | solution.py:407
  17.3 9.8 %collective-permute-start.7 = (bf16[2,128,512]{2,1,0:T(8,128)(2,1)S(1)}, bf16[2,128,512]{2,1,0:T(8,128)(2,1)S(1)}, u32[]{:S(2)}, u32[]{:S(2)}) collective-permute-start(bf16[2,128,512]{2,1,0:T(8,128)(2,1)S(1)} %collective-permute-done.3.refs_3_.refs_4_), channel_id=1, source_target_pairs={{2,3},{10,11},{18,19},{26,27}} | collective-permute-start | bytes 786440 | tf_op jit(solution)/shard_map/ppermute | solution.py:407
  21.8 6.6 %collective-permute-start.6 = (bf16[2,128,512]{2,1,0:T(8,128)(2,1)S(1)}, bf16[2,128,512]{2,1,0:T(8,128)(2,1)S(1)}, u32[]{:S(2)}, u32[]{:S(2)}) collective-permute-start(bf16[2,128,512]{2,1,0:T(8,128)(2,1)S(1)} %get-tuple-element.43.refs_6_.refs_0_), channel_id=1, source_target_pairs={{1,5},{9,13},{17,21},{25,29}} | collective-permute-start | bytes 786440 | tf_op jit(solution)/shard_map/ppermute | solution.py:407
  26.0 2.5 %collective-permute-start.5 = (bf16[2,128,512]{2,1,0:T(8,128)(2,1)S(1)}, bf16[2,128,512]{2,1,0:T(8,128)(2,1)S(1)}, u32[]{:S(2)}, u32[]{:S(2)}) collective-permute-start(bf16[2,128,512]{2,1,0:T(8,128)(2,1)S(1)} %get-tuple-element.43.refs_6_.refs_0_), channel_id=1, source_target_pairs={{1,7},{9,15},{17,23},{25,31}} | collective-permute-start | bytes 786440 | tf_op jit(solution)/shard_map/ppermute | solution.py:407
  26.9 6.9 %collective-permute-start.9 = (bf16[2,128,512]{2,1,0:T(8,128)(2,1)S(1)}, bf16[2,128,512]{2,1,0:T(8,128)(2,1)S(1)}, u32[]{:S(2)}, u32[]{:S(2)}) collective-permute-start(bf16[2,128,512]{2,1,0:T(8,128)(2,1)S(1)} %get-tuple-element.46), channel_id=1, source_target_pairs={{0,1},{1,0},{2,3},{3,2},{4,5},{5,4},{6,7},{7,6},{8,9},{9,8},{10,11... | collective-permute-start | bytes 786440 | tf_op jit(solution)/shard_map/ppermute | solution.py:407
  27.1 11.9 %collective-permute-start.10 = (bf16[2,128,512]{2,1,0:T(8,128)(2,1)S(1)}, bf16[2,128,512]{2,1,0:T(8,128)(2,1)S(1)}, u32[]{:S(2)}, u32[]{:S(2)}) collective-permute-start(bf16[2,128,512]{2,1,0:T(8,128)(2,1)S(1)} %get-tuple-element.47.refs_7_), channel_id=1, source_target_pairs={{2,4},{10,12},{18,20},{26,28}} | collective-permute-start | bytes 786440 | tf_op jit(solution)/shard_map/ppermute | solution.py:407
  27.8 10.5 %collective-permute-start.11 = (bf16[2,128,512]{2,1,0:T(8,128)(2,1)S(1)}, bf16[2,128,512]{2,1,0:T(8,128)(2,1)S(1)}, u32[]{:S(2)}, u32[]{:S(2)}) collective-permute-start(bf16[2,128,512]{2,1,0:T(8,128)(2,1)S(1)} %get-tuple-element.45.refs_0_.refs_6_), channel_id=1, source_target_pairs={{2,4},{10,12},{18,20},{26,28}} | collective-permute-start | bytes 786440 | tf_op jit(solution)/shard_map/ppermute | solution.py:407
  33.9 8.9 %collective-permute-start.12 = (bf16[2,128,512]{2,1,0:T(8,128)(2,1)S(1)}, bf16[2,128,512]{2,1,0:T(8,128)(2,1)S(1)}, u32[]{:S(2)}, u32[]{:S(2)}) collective-permute-start(bf16[2,128,512]{2,1,0:T(8,128)(2,1)S(1)} %get-tuple-element.48), channel_id=1, source_target_pairs={{3,4},{4,5},{5,2},{2,3},{0,1},{1,0},{6,7},{7,6},{11,12},{12,13},{1... | collective-permute-start | bytes 786440 | tf_op jit(solution)/shard_map/ppermute | solution.py:407
  37.5 8.5 %collective-permute-start.13 = (bf16[2,128,512]{2,1,0:T(8,128)(2,1)S(1)}, bf16[2,128,512]{2,1,0:T(8,128)(2,1)S(1)}, u32[]{:S(2)}, u32[]{:S(2)}) collective-permute-start(bf16[2,128,512]{2,1,0:T(8,128)(2,1)S(1)} %get-tuple-element.49.refs_6_.refs_0_), channel_id=1, source_target_pairs={{3,5},{2,6},{11,13},{10,14},{19,21},{18,22},{27,29},{26,30}} | collective-permute-start | bytes 786440 | tf_op jit(solution)/shard_map/ppermute | solution.py:407
  38.3 10.2 %collective-permute-start.14 = (bf16[2,128,512]{2,1,0:T(8,128)(2,1)S(1)}, bf16[2,128,512]{2,1,0:T(8,128)(2,1)S(1)}, u32[]{:S(2)}, u32[]{:S(2)}) collective-permute-start(bf16[2,128,512]{2,1,0:T(8,128)(2,1)S(1)} %collective-permute-done.11.refs_2_.refs_3_), channel_id=1, source_target_pairs={{4,5},{12,13},{20,21},{28,29}} | collective-permute-start | bytes 786440 | tf_op jit(solution)/shard_map/ppermute | solution.py:407
  42.8 6.7 %collective-permute-start.15 = (bf16[2,128,512]{2,1,0:T(8,128)(2,1)S(1)}, bf16[2,128,512]{2,1,0:T(8,128)(2,1)S(1)}, u32[]{:S(2)}, u32[]{:S(2)}) collective-permute-start(bf16[2,128,512]{2,1,0:T(8,128)(2,1)S(1)} %get-tuple-element.52), channel_id=1, source_target_pairs={{0,1},{1,0},{2,3},{3,2},{4,5},{5,4},{6,7},{7,6},{8,9},{9,8},{10,11... | collective-permute-start | bytes 786440 | tf_op jit(solution)/shard_map/ppermute | solution.py:407
  44.6 7.6 %collective-permute-start.16 = (bf16[2,128,512]{2,1,0:T(8,128)(2,1)S(1)}, bf16[2,128,512]{2,1,0:T(8,128)(2,1)S(1)}, u32[]{:S(2)}, u32[]{:S(2)}) collective-permute-start(bf16[2,128,512]{2,1,0:T(8,128)(2,1)S(1)} %get-tuple-element.53.refs_7_), channel_id=1, source_target_pairs={{4,6},{12,14},{20,22},{28,30}} | collective-permute-start | bytes 786440 | tf_op jit(solution)/shard_map/ppermute | solution.py:407
  45.3 8.3 %collective-permute-start.17 = (bf16[2,128,512]{2,1,0:T(8,128)(2,1)S(1)}, bf16[2,128,512]{2,1,0:T(8,128)(2,1)S(1)}, u32[]{:S(2)}, u32[]{:S(2)}) collective-permute-start(bf16[2,128,512]{2,1,0:T(8,128)(2,1)S(1)} %get-tuple-element.51.refs_0_.refs_6_), channel_id=1, source_target_pairs={{4,6},{12,14},{20,22},{28,30}} | collective-permute-start | bytes 786440 | tf_op jit(solution)/shard_map/ppermute | solution.py:407
  46.0 8.9 %collective-permute-start.18 = (bf16[2,128,512]{2,1,0:T(8,128)(2,1)S(1)}, bf16[2,128,512]{2,1,0:T(8,128)(2,1)S(1)}, u32[]{:S(2)}, u32[]{:S(2)}) collective-permute-start(bf16[2,128,512]{2,1,0:T(8,128)(2,1)S(1)} %collective-permute-done.13.refs_2_.refs_1_), channel_id=1, source_target_pairs={{5,7},{13,15},{21,23},{29,31}} | collective-permute-start | bytes 786440 | tf_op jit(solution)/shard_map/ppermute | solution.py:407
  49.6 6.4 %collective-permute-start.19 = (bf16[2,128,512]{2,1,0:T(8,128)(2,1)S(1)}, bf16[2,128,512]{2,1,0:T(8,128)(2,1)S(1)}, u32[]{:S(2)}, u32[]{:S(2)}) collective-permute-start(bf16[2,128,512]{2,1,0:T(8,128)(2,1)S(1)} %get-tuple-element.54), channel_id=1, source_target_pairs={{5,6},{6,7},{7,4},{4,5},{0,1},{1,0},{2,3},{3,2},{13,14},{14,15},{1... | collective-permute-start | bytes 786440 | tf_op jit(solution)/shard_map/ppermute | solution.py:407
  51.6 5.1 %collective-permute-start.21 = (bf16[2,128,512]{2,1,0:T(8,128)(2,1)S(1)}, bf16[2,128,512]{2,1,0:T(8,128)(2,1)S(1)}, u32[]{:S(2)}, u32[]{:S(2)}) collective-permute-start(bf16[2,128,512]{2,1,0:T(8,128)(2,1)S(1)} %get-tuple-element.55.refs_6_.refs_0_), channel_id=1, source_target_pairs={{5,3},{4,2},{13,11},{12,10},{21,19},{20,18},{29,27},{28,26}} | collective-permute-start | bytes 786440 | tf_op jit(solution)/shard_map/ppermute | solution.py:407
  52.3 18.8 %collective-permute-start.20 = (bf16[2,128,512]{2,1,0:T(8,128)(2,1)S(1)}, bf16[2,128,512]{2,1,0:T(8,128)(2,1)S(1)}, u32[]{:S(2)}, u32[]{:S(2)}) collective-permute-start(bf16[2,128,512]{2,1,0:T(8,128)(2,1)S(1)} %get-tuple-element.55.refs_6_.refs_0_), channel_id=1, source_target_pairs={{5,1},{4,0},{13,9},{12,8},{21,17},{20,16},{29,25},{28,24}} | collective-permute-start | bytes 786440 | tf_op jit(solution)/shard_map/ppermute | solution.py:407
  53.6 18.0 %collective-permute-start.25 = (bf16[2,128,512]{2,1,0:T(8,128)(2,1)S(1)}, bf16[2,128,512]{2,1,0:T(8,128)(2,1)S(1)}, u32[]{:S(2)}, u32[]{:S(2)}) collective-permute-start(bf16[2,128,512]{2,1,0:T(8,128)(2,1)S(1)} %get-tuple-element.51.refs_0_.refs_6_), channel_id=1, source_target_pairs={{2,0},{3,1},{10,8},{11,9},{18,16},{19,17},{26,24},{27,25}} | collective-permute-start | bytes 786440 | tf_op jit(solution)/shard_map/ppermute | solution.py:407
  54.9 20.3 %collective-permute-start.24 = (bf16[2,128,512]{2,1,0:T(8,128)(2,1)S(1)}, bf16[2,128,512]{2,1,0:T(8,128)(2,1)S(1)}, u32[]{:S(2)}, u32[]{:S(2)}) collective-permute-start(bf16[2,128,512]{2,1,0:T(8,128)(2,1)S(1)} %collective-permute-done.13.refs_2_.refs_1_), channel_id=1, source_target_pairs={{6,7},{14,15},{22,23},{30,31}} | collective-permute-start | bytes 786440 | tf_op jit(solution)/shard_map/ppermute | solution.py:407
  56.0 23.1 %collective-permute-start.22 = (bf16[2,128,512]{2,1,0:T(8,128)(2,1)S(1)}, bf16[2,128,512]{2,1,0:T(8,128)(2,1)S(1)}, u32[]{:S(2)}, u32[]{:S(2)}) collective-permute-start(bf16[2,128,512]{2,1,0:T(8,128)(2,1)S(1)} %get-tuple-element.55.refs_6_.refs_0_), channel_id=1, source_target_pairs={{5,7},{13,15},{21,23},{29,31}} | collective-permute-start | bytes 786440 | tf_op jit(solution)/shard_map/ppermute | solution.py:407
  56.7 21.0 %collective-permute-start.23 = (bf16[2,128,512]{2,1,0:T(8,128)(2,1)S(1)}, bf16[2,128,512]{2,1,0:T(8,128)(2,1)S(1)}, u32[]{:S(2)}, u32[]{:S(2)}) collective-permute-start(bf16[2,128,512]{2,1,0:T(8,128)(2,1)S(1)} %collective-permute-done.17.refs_2_.refs_3_), channel_id=1, source_target_pairs={{6,7},{14,15},{22,23},{30,31}} | collective-permute-start | bytes 786440 | tf_op jit(solution)/shard_map/ppermute | solution.py:407
  71.2 9.4 %collective-permute-start.30 = (bf16[2,128,512]{2,1,0:T(8,128)(2,1)S(1)}, bf16[2,128,512]{2,1,0:T(8,128)(2,1)S(1)}, u32[]{:S(2)}, u32[]{:S(2)}) collective-permute-start(bf16[2,128,512]{2,1,0:T(8,128)(2,1)S(1)} %get-tuple-element.58), channel_id=1, source_target_pairs={{0,1},{1,0},{2,3},{3,2},{4,5},{5,4},{6,7},{7,6},{8,9},{9,8},{10,11... | collective-permute-start | bytes 786440 | tf_op jit(solution)/shard_map/ppermute | solution.py:407
  71.5 11.0 %collective-permute-start.26 = (bf16[2,128,512]{2,1,0:T(8,128)(2,1)S(1)}, bf16[2,128,512]{2,1,0:T(8,128)(2,1)S(1)}, u32[]{:S(2)}, u32[]{:S(2)}) collective-permute-start(bf16[2,128,512]{2,1,0:T(8,128)(2,1)S(1)} %collective-permute-done.25.refs_4_), channel_id=1, source_target_pairs={{0,1},{1,0},{8,9},{9,8},{16,17},{17,16},{24,25},{25,24}} | collective-permute-start | bytes 786440 | tf_op jit(solution)/shard_map/ppermute | solution.py:407
  75.2 5.2 %copy-start.5 = (bf16[2,128,512]{2,1,0:T(8,128)(2,1)}, bf16[2,128,512]{2,1,0:T(8,128)(2,1)S(1)}, u32[]{:S(2)}) copy-start(bf16[2,128,512]{2,1,0:T(8,128)(2,1)S(1)} %collective-permute-done.24.refs_4_.refs_3_) | copy-start | bytes 786436
  75.2 8.7 %collective-permute-start.29 = (bf16[2,128,512]{2,1,0:T(8,128)(2,1)S(1)}, bf16[2,128,512]{2,1,0:T(8,128)(2,1)S(1)}, u32[]{:S(2)}, u32[]{:S(2)}) collective-permute-start(bf16[2,128,512]{2,1,0:T(8,128)(2,1)S(1)} %get-tuple-element.57.refs_0_.refs_6_), channel_id=1, source_target_pairs={{6,4},{14,12},{22,20},{30,28}} | collective-permute-start | bytes 786440 | tf_op jit(solution)/shard_map/ppermute | solution.py:407
  77.7 2.8 %copy-start.7 = (bf16[2,128,512]{2,1,0:T(8,128)(2,1)}, bf16[2,128,512]{2,1,0:T(8,128)(2,1)S(1)}, u32[]{:S(2)}) copy-start(bf16[2,128,512]{2,1,0:T(8,128)(2,1)S(1)} %collective-permute-done.23.refs_3_.refs_2_) | copy-start | bytes 786436
  77.7 12.2 %collective-permute-start.28 = (bf16[2,128,512]{2,1,0:T(8,128)(2,1)S(1)}, bf16[2,128,512]{2,1,0:T(8,128)(2,1)}, u32[]{:S(2)}, u32[]{:S(2)}) collective-permute-start(bf16[2,128,512]{2,1,0:T(8,128)(2,1)S(1)} %get-tuple-element.57.refs_0_.refs_6_), channel_id=1, source_target_pairs={{6,2},{14,10},{22,18},{30,26}} | collective-permute-start | bytes 786440 | tf_op jit(solution)/shard_map/ppermute | solution.py:407
  79.1 12.2 %collective-permute-start.27 = (bf16[2,128,512]{2,1,0:T(8,128)(2,1)S(1)}, bf16[2,128,512]{2,1,0:T(8,128)(2,1)}, u32[]{:S(2)}, u32[]{:S(2)}) collective-permute-start(bf16[2,128,512]{2,1,0:T(8,128)(2,1)S(1)} %get-tuple-element.57.refs_0_.refs_6_), channel_id=1, source_target_pairs={{6,0},{14,8},{22,16},{30,24}} | collective-permute-start | bytes 786440 | tf_op jit(solution)/shard_map/ppermute | solution.py:407
  81.4 13.8 %collective-permute-start.33 = (bf16[2,128,512]{2,1,0:T(8,128)(2,1)S(1)}, bf16[2,128,512]{2,1,0:T(8,128)(2,1)S(1)}, u32[]{:S(2)}, u32[]{:S(2)}) collective-permute-start(bf16[2,128,512]{2,1,0:T(8,128)(2,1)S(1)} %get-tuple-element.60.refs_5_.refs_6_.refs_8_.refs_0_.refs_2_.refs_4_.refs_7_), channel_id=1, source_target_pairs={{7,5},{15,13},{23,21},{31,29}} | collective-permute-start | bytes 786440 | tf_op jit(solution)/shard_map/ppermute | solution.py:407
  83.3 12.0 %collective-permute-start.32 = (bf16[2,128,512]{2,1,0:T(8,128)(2,1)S(1)}, bf16[2,128,512]{2,1,0:T(8,128)(2,1)S(1)}, u32[]{:S(2)}, u32[]{:S(2)}) collective-permute-start(bf16[2,128,512]{2,1,0:T(8,128)(2,1)S(1)} %get-tuple-element.60.refs_5_.refs_6_.refs_8_.refs_0_.refs_2_.refs_4_.refs_7_), channel_id=1, source_target_pairs={{7,3},{15,11},{23,19},{31,27}} | collective-permute-start | bytes 786440 | tf_op jit(solution)/shard_map/ppermute | solution.py:407
  83.9 11.3 %collective-permute-start.31 = (bf16[2,128,512]{2,1,0:T(8,128)(2,1)S(1)}, bf16[2,128,512]{2,1,0:T(8,128)(2,1)S(1)}, u32[]{:S(2)}, u32[]{:S(2)}) collective-permute-start(bf16[2,128,512]{2,1,0:T(8,128)(2,1)S(1)} %get-tuple-element.60.refs_5_.refs_6_.refs_8_.refs_0_.refs_2_.refs_4_.refs_7_), channel_id=1, source_target_pairs={{7,1},{15,9},{23,17},{31,25}} | collective-permute-start | bytes 786440 | tf_op jit(solution)/shard_map/ppermute | solution.py:407
  92.3 10.5 %collective-permute-start.35 = (bf16[2,128,512]{2,1,0:T(8,128)(2,1)S(1)}, bf16[2,128,512]{2,1,0:T(8,128)(2,1)S(1)}, u32[]{:S(2)}, u32[]{:S(2)}) collective-permute-start(bf16[2,128,512]{2,1,0:T(8,128)(2,1)S(1)} %get-tuple-element.63), channel_id=1, source_target_pairs={{0,1},{1,0},{2,3},{3,2},{4,5},{5,4},{6,7},{7,6},{8,9},{9,8},{10,11... | collective-permute-start | bytes 786440 | tf_op jit(solution)/shard_map/ppermute | solution.py:407
  95.5 10.5 %collective-permute-start.34 = (bf16[2,64,512]{2,1,0:T(8,128)(2,1)S(1)}, bf16[2,64,512]{2,1,0:T(8,128)(2,1)S(1)}, u32[]{:S(2)}, u32[]{:S(2)}) collective-permute-start(bf16[2,64,512]{2,1,0:T(8,128)(2,1)S(1)} %get-tuple-element.62), channel_id=1, source_target_pairs={{0,1},{1,0},{2,3},{3,2},{4,5},{5,4},{6,7},{7,6},{8,9},{9,8},{10,11... | collective-permute-start | bytes 393224 | tf_op jit(solution)/shard_map/ppermute | solution.py:407
  101.8 6.9 %collective-permute-start.36 = (bf16[2,64,512]{2,1,0:T(8,128)(2,1)S(1)}, bf16[2,64,512]{2,1,0:T(8,128)(2,1)S(1)}, u32[]{:S(2)}, u32[]{:S(2)}) collective-permute-start(bf16[2,64,512]{2,1,0:T(8,128)(2,1)S(1)} %get-tuple-element.64), channel_id=1, source_target_pairs={{0,1},{1,0},{2,3},{3,2},{4,5},{5,4},{6,7},{7,6},{8,9},{9,8},{10,11... | collective-permute-start | bytes 393224 | tf_op jit(solution)/shard_map/ppermute | solution.py:407
  107.7 5.0 %collective-permute-start.37 = (bf16[2,64,512]{2,1,0:T(8,128)(2,1)S(1)}, bf16[2,64,512]{2,1,0:T(8,128)(2,1)S(1)}, u32[]{:S(2)}, u32[]{:S(2)}) collective-permute-start(bf16[2,64,512]{2,1,0:T(8,128)(2,1)S(1)} %update_last_0.1.refs_0_), channel_id=1, source_target_pairs={{0,1},{1,0},{2,3},{3,2},{4,5},{5,4},{6,7},{7,6},{8,9},{9,8},{10,11... | collective-permute-start | bytes 393224 | tf_op jit(solution)/shard_map/ppermute | solution.py:407
  110.5 5.0 %collective-permute-start.38 = (bf16[2,64,512]{2,1,0:T(8,128)(2,1)S(1)}, bf16[2,64,512]{2,1,0:T(8,128)(2,1)S(1)}, u32[]{:S(2)}, u32[]{:S(2)}) collective-permute-start(bf16[2,64,512]{2,1,0:T(8,128)(2,1)S(1)} %update_last_1.1.refs_1_), channel_id=1, source_target_pairs={{0,1},{1,0},{2,3},{3,2},{4,5},{5,4},{6,7},{7,6},{8,9},{9,8},{10,11... | collective-permute-start | bytes 393224 | tf_op jit(solution)/shard_map/ppermute | solution.py:407
  115.6 20.2 %copy-start.11 = (f32[1,2,128,512]{3,2,1,0:T(8,128)S(1)}, f32[1,2,128,512]{3,2,1,0:T(8,128)}, u32[]{:S(2)}) copy-start(f32[1,2,128,512]{3,2,1,0:T(8,128)} %param.13) | copy-start | bytes 1572868
  117.1 9.5 %collective-permute-start.39 = (bf16[2,128,512]{2,1,0:T(8,128)(2,1)S(1)}, bf16[2,128,512]{2,1,0:T(8,128)(2,1)S(1)}, u32[]{:S(2)}, u32[]{:S(2)}) collective-permute-start(bf16[2,128,512]{2,1,0:T(8,128)(2,1)S(1)} %get-tuple-element.66), channel_id=1, source_target_pairs={{0,2},{1,3},{2,0},{3,1},{4,6},{5,7},{6,4},{7,5},{8,10},{9,11},{10,... | collective-permute-start | bytes 786440 | tf_op jit(solution)/shard_map/ppermute | solution.py:407
  117.2 16.6 %collective-permute-start.40 = (bf16[2,128,512]{2,1,0:T(8,128)(2,1)S(1)}, bf16[2,128,512]{2,1,0:T(8,128)(2,1)S(1)}, u32[]{:S(2)}, u32[]{:S(2)}) collective-permute-start(bf16[2,128,512]{2,1,0:T(8,128)(2,1)S(1)} %get-tuple-element.67), channel_id=1, source_target_pairs={{0,4},{1,5},{2,6},{3,7},{4,0},{5,1},{6,2},{7,3},{8,12},{9,13},{10,... | collective-permute-start | bytes 786440 | tf_op jit(solution)/shard_map/ppermute | solution.py:407
  119.9 13.9 %collective-permute-start.41 = (bf16[2,128,512]{2,1,0:T(8,128)(2,1)S(1)}, bf16[2,128,512]{2,1,0:T(8,128)(2,1)S(1)}, u32[]{:S(2)}, u32[]{:S(2)}) collective-permute-start(bf16[2,128,512]{2,1,0:T(8,128)(2,1)S(1)} %get-tuple-element.68), channel_id=1, source_target_pairs={{0,6},{1,7},{2,4},{3,5},{4,2},{5,3},{6,0},{7,1},{8,14},{9,15},{10,... | collective-permute-start | bytes 786440 | tf_op jit(solution)/shard_map/ppermute | solution.py:407
  134.1 1.6 %collective-permute-start.42 = (bf16[2,128,512]{2,1,0:T(8,128)(2,1)S(1)}, bf16[2,128,512]{2,1,0:T(8,128)(2,1)S(1)}, u32[]{:S(2)}, u32[]{:S(2)}) collective-permute-start(bf16[2,128,512]{2,1,0:T(8,128)(2,1)S(1)} %select_convert_fusion), channel_id=1, source_target_pairs={{0,8},{8,0},{16,24},{24,16},{1,9},{9,1},{17,25},{25,17},{2,10},{10... | collective-permute-start | bytes 786440 | tf_op jit(solution)/shard_map/ppermute | solution.py:475
  (7 other events, 7.1 us)
